TPU v7x, 32 devices: a whole 2x2x4 slice. The times are simulated.
32 devices in a mesh: wide: 8 (over y, x, core), narrow: 4 (over z).
Axes of the slice: x: 2, y: 2, z: 4, core: 2. Of those that a mesh axis runs over, the one named last changes fastest.
Arguments:
- exposures: bfloat16 [4, 128, 3072], P(None, 'narrow', 'wide'), may hold values from -6 to 6
- basis_kernels: bfloat16 [5, 21, 21], replicated, may hold values from -0.25 to 0.25
- poly_coef: float32 [4, 5, 6], replicated, may hold values from -3 to 3
- exposure_weight: float32 [4], replicated, may hold values from 0.5 to 2
- row_start: int32 [4], replicated, may hold values from 0 to 64, as said below
- row_count: int32 [4], replicated, may hold values from 32 to 128, as said below
- filter_taps: float32 [21], replicated, may hold values from -1.5 to 1.5
Outputs:
- coadded: float32 [128, 3072], P('narrow', 'wide')
- detection: float32 [128, 3072], P('narrow', 'wide')
Inputs may be any that keep to these rules, and one draw needn't show every extreme that they name: Each row_start is a multiple of 32; row_start[0] is 0 and row_start + row_count never exceeds 128. Each row_count is a multiple of 8; exposure 0 covers the whole band.
All inputs are finite; a program needn't handle non-finite values.
Results may differ from a plain program's by a relative error of at most 0.0003.
Values may be sent and summed in bfloat16 or wider, within the bound.
No kernel may reach another device: no remote copies, remote signals or barrier semaphores. Data moves between devices by JAX's collectives and lax.ppermute only.
A program may use at most 64 MiB of HBM per device.

v0:
```python
import math

import jax
import jax.numpy as jnp
from jax import lax
from jax.sharding import PartitionSpec as P


def padded(array, sides, width):
    for axis, dim in sides:
        peers, length = (lax.axis_size(axis), array.shape[dim])
        up = [(i, (i + 1) % peers) for i in range(peers - 1)]
        down = [(j, i) for i, j in up]
        last = lax.slice_in_dim(array, length - width, length, axis=dim)
        initial = lax.slice_in_dim(array, 0, width, axis=dim)
        before = lax.ppermute(last, axis, up)
        after = lax.ppermute(initial, axis, down)
        array = jnp.concatenate([before, array, after], axis=dim)
    return array


def respond(window, basis_kernels):
    side = basis_kernels.shape[1]
    kernel_total = basis_kernels.shape[0]
    out_rows = window.shape[0] - (side - 1)
    out_cols = window.shape[1] - (side - 1)
    block = math.gcd(out_cols, 128)
    block_total = out_cols // block
    span = block + side - 1
    shifted = jnp.stack([window[offset : offset + out_rows] for offset in range(side)])
    patches = jnp.stack(
        [shifted[:, :, index * block : index * block + span] for index in range(block_total)]
    )
    lagged = (
        jnp.arange(span, dtype=jnp.int32)[:, None] - jnp.arange(block, dtype=jnp.int32)[None, :]
    )
    onehot = (lagged[None] == jnp.arange(side, dtype=jnp.int32)[:, None, None]).astype(jnp.float32)
    table = jnp.einsum(
        "kab,bco->acko", basis_kernels.astype(jnp.float32), onehot, precision=lax.Precision.HIGHEST
    )
    table = table.astype(jnp.bfloat16).reshape(side, span, kernel_total * block)
    result = jnp.einsum("jarc,acn->jrn", patches, table, preferred_element_type=jnp.float32)
    result = result.reshape(block_total, out_rows, kernel_total, block).transpose(2, 1, 0, 3)
    return result.reshape(kernel_total, out_rows, out_cols)


def on_device(
    exposures, basis_kernels, poly_coef, exposure_weight, row_start, row_count, filter_taps
):
    tile_rows = exposures.shape[1]
    tile_cols = exposures.shape[2]
    band_rows = tile_rows * lax.axis_size("narrow")
    band_cols = tile_cols * lax.axis_size("wide")
    row_base = lax.axis_index("narrow") * tile_rows
    row_index = row_base + jnp.arange(tile_rows, dtype=jnp.int32)
    col_index = lax.axis_index("wide") * tile_cols + jnp.arange(tile_cols, dtype=jnp.int32)
    y_coord = ((2 * row_index + 1).astype(jnp.float32) / band_rows - 1.0)[:, None]
    x_coord = ((2 * col_index + 1).astype(jnp.float32) / band_cols - 1.0)[None, :]
    numerator = jnp.zeros((tile_rows, tile_cols), jnp.float32)
    denominator = jnp.zeros((tile_rows, 1), jnp.float32)
    zero_value = jnp.zeros((), exposures.dtype)
    for member in range(exposures.shape[0]):
        first_row = row_start[member]
        row_total = row_count[member]
        inside = (row_index >= first_row) & (row_index < first_row + row_total)
        lead_row = row_base - 10 - first_row

        def placed_rows(window, portion, anchor, lead_row=lead_row):
            window_len = window.shape[0]
            portion_len = portion.shape[0]
            padding = jnp.zeros((window_len, portion.shape[1]), portion.dtype)
            extended = jnp.concatenate([padding, portion, padding], 0)
            sliced = lax.dynamic_slice_in_dim(extended, lead_row + window_len, window_len, 0)
            local_rows = lead_row + jnp.arange(window_len, dtype=jnp.int32)
            present = (local_rows >= 0) & (local_rows < portion_len)
            return jnp.where(present[:, None], sliced, window)

        empty_window = jnp.zeros((tile_rows + 20, tile_cols), exposures.dtype)
        window = placed_rows(
            empty_window,
            lax.all_gather(exposures[member], "narrow", axis=0, tiled=True),
            jnp.int32(0),
        )
        window_rows = row_base - 10 + jnp.arange(tile_rows + 20, dtype=jnp.int32)
        valid_rows = (window_rows >= first_row) & (window_rows < first_row + row_total)
        window = jnp.where(valid_rows[:, None], window, zero_value)
        window = padded(window, (("wide", 1),), 10)
        touches = (first_row < row_base + tile_rows) & (first_row + row_total > row_base)

        def matched_tile(window, member=member):
            response = respond(window, basis_kernels)
            matched = jnp.zeros((tile_rows, tile_cols), jnp.float32)
            for kernel in range(basis_kernels.shape[0]):
                coeffs = poly_coef[member, kernel]
                spatial = (
                    coeffs[0]
                    + coeffs[1] * x_coord
                    + coeffs[2] * y_coord
                    + coeffs[3] * x_coord * x_coord
                    + coeffs[4] * x_coord * y_coord
                    + coeffs[5] * y_coord * y_coord
                )
                matched = matched + spatial * response[kernel]
            return matched

        def empty_tile(window):
            return jnp.zeros((tile_rows, tile_cols), jnp.float32)

        matched = lax.cond(touches, matched_tile, empty_tile, window)
        weighting = exposure_weight[member] * inside.astype(jnp.float32)[:, None]
        numerator = numerator + weighting * matched
        denominator = denominator + weighting
    coadded = numerator / denominator
    taps_total = filter_taps.shape[0]
    framed = padded(coadded, (("wide", 1),), 10)
    inner = filter_taps[0] * framed[:, 0:tile_cols]
    for offset in range(1, taps_total):
        inner = inner + filter_taps[offset] * framed[:, offset : offset + tile_cols]
    across = padded(inner, (("narrow", 0),), 10)
    detection = filter_taps[0] * across[0:tile_rows]
    for offset in range(1, taps_total):
        detection = detection + filter_taps[offset] * across[offset : offset + tile_rows]
    return (coadded, detection)


def solution(mesh):
    placed = (P(None, "narrow", "wide"), P(), P(), P(), P(), P(), P())
    return jax.shard_map(
        on_device,
        mesh=mesh,
        in_specs=placed,
        out_specs=(P("narrow", "wide"), P("narrow", "wide")),
        check_vma=False,
    )
```

profile of v0, /device:TPU:28, one launch (start us, length us, event | category | flops | bytes accessed | tf_op | source)
XLA Modules:
  0.0 342.5 jit_solution(12545394098957795741)
XLA Ops:
  0.6 1.5 fusion.271
  2.1 1.4 fusion.270
  5.6 0.8 fusion.260
  6.4 13.4 %all-gather.3 = bf16[1,128,384]{2,1,0:T(8,128)(2,1)S(1)} all-gather(bf16[1,32,384]{2,1,0:T(8,128)(2,1)S(1)} %get-tuple-element.333), channel_id=5, replica_groups=mesh['wide'=8,'narrow'=4] {'narrow'}, dimensions={1}, use_global_device_ids=true | all-gather | bytes 122880 | tf_op jit(solution)/shard_map/all_gather | solution.py:81
  19.8 0.7 compare_and_fusion
  20.5 0.1 fusion.241
  20.7 1.9 collective-permute-start.7
  22.7 2.4 collective-permute-start.6
  28.1 13.4 %all-gather = bf16[1,128,384]{2,1,0:T(8,128)(2,1)S(1)} all-gather(bf16[1,32,384]{2,1,0:T(8,128)(2,1)S(1)} %get-tuple-element.331), channel_id=2, replica_groups=mesh['wide'=8,'narrow'=4] {'narrow'}, dimensions={1}, use_global_device_ids=true | all-gather | bytes 122880 | tf_op jit(solution)/shard_map/all_gather | solution.py:81
  42.8 0.7 compare_and_fusion.6
  43.5 13.3 %all-gather.1 = bf16[1,128,384]{2,1,0:T(8,128)(2,1)S(1)} all-gather(bf16[1,32,384]{2,1,0:T(8,128)(2,1)S(1)} %get-tuple-element.332), channel_id=3, replica_groups=mesh['wide'=8,'narrow'=4] {'narrow'}, dimensions={1}, use_global_device_ids=true | all-gather | bytes 122880 | tf_op jit(solution)/shard_map/all_gather | solution.py:81
  58.0 13.4 %all-gather.2 = bf16[1,128,384]{2,1,0:T(8,128)(2,1)S(1)} all-gather(bf16[1,32,384]{2,1,0:T(8,128)(2,1)S(1)} %get-tuple-element.334), channel_id=4, replica_groups=mesh['wide'=8,'narrow'=4] {'narrow'}, dimensions={1}, use_global_device_ids=true | all-gather | bytes 122880 | tf_op jit(solution)/shard_map/all_gather | solution.py:81
  71.5 1.2 compare_and_fusion.3
  72.7 0.3 fusion.247
  73.1 1.9 collective-permute-start.5
  75.0 2.4 collective-permute-start.4
  77.5 4.0 %collective-permute-start.3 = (bf16[52,10]{1,0:T(8,128)(2,1)S(1)}, bf16[52,10]{1,0:T(8,128)(2,1)S(1)}, u32[]{:S(2)}, u32[]{:S(2)}) collective-permute-start(bf16[52,10]{1,0:T(8,128)(2,1)S(1)} %get-tuple-element.345), channel_id=1, source_target_pairs={{4,0},{8,4},{12,8},{16,12},{20,16},{24,20},{28,24},{5,1},{9,5},{13... | collective-permute-start | bytes 3128 | tf_op jit(solution)/shard_map/ppermute | solution.py:17
  81.7 1.5 fusion.269
  83.1 2.1 fusion.267
  85.2 5.0 %add_add_fusion = (f32[32]{0:T(128)S(1)}, f32[32]{0:T(128)S(1)}, f32[32]{0:T(128)S(1)}, f32[32]{0:T(128)S(1)}, f32[32]{0:T(128)S(1)}) fusion(f32[]{:T(128)} %bitcast.314, s32[]{:T(128)S(6)} %add.1350, s32[]{:T(128)} %bitcast.312, s32[]{:T(128)S(6)} %mul.1366, f32[]{:T(128)} %bitcast.310, s32[]{:T(128)S(6)} %add.1334, s32[]{:T(128)} %bitcast.308, ...), kind=kLoop, calls=%fused_computation.574 | loop fusion | flops 640 | bytes 692 | tf_op jit(solution)/shard_map/add | solution.py:112
  92.8 1.9 collective-permute-start.2
  94.8 4.5 %collective-permute-start.1 = (bf16[52,10]{1,0:T(8,128)(2,1)S(1)}, bf16[52,10]{1,0:T(8,128)(2,1)S(1)}, u32[]{:S(2)}, u32[]{:S(2)}) collective-permute-start(bf16[52,10]{1,0:T(8,128)(2,1)S(1)} %get-tuple-element.340), channel_id=1, source_target_pairs={{4,0},{8,4},{12,8},{16,12},{20,16},{24,20},{28,24},{5,1},{9,5},{13... | collective-permute-start | bytes 3128 | tf_op jit(solution)/shard_map/ppermute | solution.py:17
  99.4 1.9 collective-permute-start
  101.5 0.1 pad_maximum_fusion.1
  101.6 3.8 %collective-permute-done = bf16[52,10]{1,0:T(8,128)(2,1)S(1)} collective-permute-done((bf16[52,10]{1,0:T(8,128)(2,1)S(1)}, bf16[52,10]{1,0:T(8,128)(2,1)S(1)}, u32[]{:S(2)}, u32[]{:S(2)}) %collective-permute-start) | collective-permute-done | bytes 1072 | tf_op jit(solution)/shard_map/ppermute | solution.py:16
  105.5 48.8 %conditional.7 = (f32[32,384]{1,0:T(8,128)S(1)}) conditional(s32[]{:T(128)} %convert_element_type.81, () %tuple.38, (f32[4,5,6]{2,0,1:T(4,128)}, f32[1,384]{1,0:T(1,128)S(1)}, f32[32,1]{0,1:T(1,128)S(1)}, bf16[52,404]{1,0:T(8,128)(2,1)S(1)}, bf16[5,21,21]{2,1,0:T(8,128)(2,1)}) %tuple.39), branch_computations={%region_6.7_spmd, %region_7.8_spmd} | conditional | flops 470078048 | bytes 36719428 | solution.py:109
  105.5 2.1 convert_bitcast_fusion.3
  107.6 3.9 %copy.30 = bf16[21,148,5,128]{3,2,1,0:T(8,128)(2,1)} copy(bf16[21,148,5,128]{3,0,2,1:T(8,128)(2,1)S(1)} %convert_bitcast_fusion.3) | data formatting | bytes 7956480 | tf_op jit(solution)/shard_map/cond/branch_1_fun/convert_element_type | solution.py:41
  111.5 8.9 %reshape.485 = bf16[21,148,640]{2,1,0:T(8,128)(2,1)} reshape(bf16[21,148,5,128]{3,2,1,0:T(8,128)(2,1)} %copy.30) | data formatting | bytes 7956480 | tf_op jit(solution)/shard_map/cond/branch_1_fun/reshape | solution.py:41
  120.4 8.8 %dot_general.38 = bf16[5,128,21,148]{1,0,3,2:T(8,128)(2,1)} reshape(bf16[640,21,148]{0,2,1:T(8,128)(2,1)} %bitcast.689) | data formatting | bytes 7956480 | tf_op jit(solution)/shard_map/cond/branch_1_fun/jarc,acn->jrn/dot_general | solution.py:42
  129.6 0.1 slice_bitcast_fusion.11
  129.7 3.8 %fusion.92 = f32[5,32,3,128]{3,1,0,2:T(8,128)S(1)} fusion(bf16[5,128,21,148]{1,0,3,2:T(8,128)(2,1)} %dot_general.38, bf16[1,21,32,148]{3,2,1,0:T(8,128)(2,1)S(1)} %get-tuple-element.284, bf16[1,21,32,148]{3,2,1,0:T(8,128)(2,1)S(1)} %get-tuple-element.285, bf16[1,21,32,148]{3,2,1,0:T(8,128)(2,1)S(1)} %get-tuple-element.283), kind=kOutput, calls=%fused_computation.258 | convolution fusion | flops 383701248 | bytes 4820736 | tf_op jit(solution)/shard_map/cond/branch_1_fun/jarc,acn->jrn/dot_general | solution.py:42
  133.8 0.7 fusion.258
  134.6 0.7 fusion.259
  135.3 6.2 %multiply_bitcast_fusion.19 = (f32[32]{0:T(128)S(1)}, f32[32]{0:T(128)S(1)}, f32[32]{0:T(128)S(1)}, f32[32]{0:T(128)S(1)}, f32[32]{0:T(128)S(1)}, /*index=5*/f32...) fusion(f32[32,1]{0,1:T(1,128)S(1)} %get-tuple-element.69, f32[]{:T(128)} %bitcast.233, ...), kind=kLoop, calls=%fused_computation.334 | loop fusion | flops 480 | bytes 1448 | tf_op jit(solution)/shard_map/cond/branch_1_fun/add | solution.py:96
  141.4 11.3 %add_reduce_fusion.19 = (f32[384]{0:T(512)S(1)}, f32[384]{0:T(512)S(1)}, f32[384]{0:T(512)S(1)}, f32[384]{0:T(512)S(1)}, f32[384]{0:T(512)S(1)}, /*index=5*/f32[...) fusion(f32[1,384]{1,0:T(1,128)S(1)} %get-tuple-element.68, ...), kind=kLoop, calls=%fused_computation.319 | loop fusion | flops 8448 | bytes 21576 | tf_op jit(solution)/shard_map/cond/branch_1_fun/add | solution.py:96
  152.7 1.4 fusion.105
  154.1 0.1 fusion.100
  154.3 0.2 conditional.6
  154.5 0.2 conditional.5
  154.8 49.0 %conditional.4 = (f32[32,384]{1,0:T(8,128)S(1)}) conditional(s32[]{:T(128)} %convert_element_type.76, () %tuple.32, (f32[4,5,6]{2,0,1:T(4,128)}, f32[1,384]{1,0:T(1,128)S(1)}, f32[32,1]{0,1:T(1,128)S(1)}, bf16[52,404]{1,0:T(8,128)(2,1)S(1)}, bf16[5,21,21]{2,1,0:T(8,128)(2,1)}) %tuple.33), branch_computations={%region_0.1_spmd, %region_1.2_spmd} | conditional | flops 470078048 | bytes 36719428 | solution.py:109
  155.1 2.1 convert_bitcast_fusion
  157.1 3.9 %copy.9 = bf16[21,148,5,128]{3,2,1,0:T(8,128)(2,1)} copy(bf16[21,148,5,128]{3,0,2,1:T(8,128)(2,1)S(1)} %convert_bitcast_fusion) | data formatting | bytes 7956480 | tf_op jit(solution)/shard_map/cond/branch_1_fun/convert_element_type | solution.py:41
  161.1 8.9 %reshape.482 = bf16[21,148,640]{2,1,0:T(8,128)(2,1)} reshape(bf16[21,148,5,128]{3,2,1,0:T(8,128)(2,1)} %copy.9) | data formatting | bytes 7956480 | tf_op jit(solution)/shard_map/cond/branch_1_fun/reshape | solution.py:41
  170.0 8.8 %dot_general.18 = bf16[5,128,21,148]{1,0,3,2:T(8,128)(2,1)} reshape(bf16[640,21,148]{0,2,1:T(8,128)(2,1)} %bitcast.692) | data formatting | bytes 7956480 | tf_op jit(solution)/shard_map/cond/branch_1_fun/jarc,acn->jrn/dot_general | solution.py:42
  179.1 0.1 slice_bitcast_fusion.2
  179.3 3.8 %fusion.5 = f32[5,32,3,128]{3,1,0,2:T(8,128)S(1)} fusion(bf16[5,128,21,148]{1,0,3,2:T(8,128)(2,1)} %dot_general.18, bf16[1,21,32,148]{3,2,1,0:T(8,128)(2,1)S(1)} %get-tuple-element.140, bf16[1,21,32,148]{3,2,1,0:T(8,128)(2,1)S(1)} %get-tuple-element.141, bf16[1,21,32,148]{3,2,1,0:T(8,128)(2,1)S(1)} %get-tuple-element.139), kind=kOutput, calls=%fused_computation.6 | convolution fusion | flops 383701248 | bytes 4820736 | tf_op jit(solution)/shard_map/cond/branch_1_fun/jarc,acn->jrn/dot_general | solution.py:42
  183.4 0.7 fusion.249
  184.1 0.7 fusion.250
  184.8 6.2 %multiply_bitcast_fusion.4 = (f32[32]{0:T(128)S(1)}, f32[32]{0:T(128)S(1)}, f32[32]{0:T(128)S(1)}, f32[32]{0:T(128)S(1)}, f32[32]{0:T(128)S(1)}, /*index=5*/f32[...) fusion(f32[32,1]{0,1:T(1,128)S(1)} %get-tuple-element.48, f32[]{:T(128)} %bitcast.2, ...), kind=kLoop, calls=%fused_computation.82 | loop fusion | flops 480 | bytes 1448 | tf_op jit(solution)/shard_map/cond/branch_1_fun/add | solution.py:96
  191.0 11.2 %add_reduce_fusion.4 = (f32[384]{0:T(512)S(1)}, f32[384]{0:T(512)S(1)}, f32[384]{0:T(512)S(1)}, f32[384]{0:T(512)S(1)}, f32[384]{0:T(512)S(1)}, /*index=5*/f32[3...) fusion(f32[1,384]{1,0:T(1,128)S(1)} %get-tuple-element.47, ...), kind=kLoop, calls=%fused_computation.67 | loop fusion | flops 8448 | bytes 21576 | tf_op jit(solution)/shard_map/cond/branch_1_fun/add | solution.py:96
  202.3 1.3 fusion.18
  203.6 0.1 fusion.13
  203.8 0.1 add_divide_fusion
  203.9 1.9 collective-permute-start.9
  205.9 2.4 collective-permute-start.8
  208.3 0.7 fusion.268
  209.0 2.9 collective-permute-done.8
  211.8 13.3 %fusion.119 = f32[32,384]{1,0:T(8,128)S(1)} fusion(f32[32,384]{1,0:T(8,128)S(1)} %add_divide_fusion, f32[32,10]{1,0:T(8,128)S(1)} %collective-permute-done.9, f32[32,10]{1,0:T(8,128)S(1)} %collective-permute-done.8, f32[]{:T(128)} %bitcast.344, f32[]{:T(128)} %bitcast.343, f32[]{:T(128)} %bitcast.342, f32[]{:T(128)} %bitcast.341, f32[]{:T(128)} %bitcast.340, ...), kind=kLoop, calls=%fused_computation.427 | loop fusion | flops 749568 | bytes 100948 | tf_op jit(solution)/shard_map/add | solution.py:118
  225.2 97.9 %collective-permute-start.11 = (f32[10,384]{1,0:T(8,128)S(1)}, f32[10,384]{1,0:T(8,128)S(1)}, u32[]{:S(2)}, u32[]{:S(2)}) collective-permute-start(f32[10,384]{1,0:T(8,128)S(1)} %get-tuple-element.336), channel_id=1, source_target_pairs={{1,0},{2,1},{3,2},{5,4},{6,5},{7,6},{9,8},{10,9},{11,10},{13,12},{... | collective-permute-start | bytes 46088 | tf_op jit(solution)/shard_map/ppermute | solution.py:17
  323.1 1.3 collective-permute-start.10
  324.4 0.2 collective-permute-done.11
  324.6 4.2 %collective-permute-done.10 = f32[10,384]{1,0:T(8,128)S(1)} collective-permute-done((f32[10,384]{1,0:T(8,128)S(1)}, f32[10,384]{1,0:T(8,128)S(1)}, u32[]{:S(2)}, u32[]{:S(2)}) %collective-permute-start.10) | collective-permute-done | bytes 15392 | tf_op jit(solution)/shard_map/ppermute | solution.py:16
  328.8 13.7 %fusion.175 = f32[32,384]{1,0:T(8,128)} fusion(f32[32,384]{1,0:T(8,128)S(1)} %fusion.119, f32[10,384]{1,0:T(8,128)S(1)} %collective-permute-done.11, f32[10,384]{1,0:T(8,128)S(1)} %collective-permute-done.10, f32[]{:T(128)} %bitcast.344, f32[]{:T(128)} %bitcast.343, f32[]{:T(128)} %bitcast.342, f32[]{:T(128)} %bitcast.341, f32[]{:T(128)} %bitcast.340, ...), kind=kLoop, calls=%fused_computation.483 | loop fusion | flops 749568 | bytes 129108 | tf_op jit(solution)/shard_map/add | solution.py:122
  (87 shorter events, 1.7 us)
Async XLA Ops:
  20.7 72.1 %collective-permute-start.7 = (bf16[52,10]{1,0:T(8,128)(2,1)S(1)}, bf16[52,10]{1,0:T(8,128)(2,1)S(1)}, u32[]{:S(2)}, u32[]{:S(2)}) collective-permute-start(bf16[52,10]{1,0:T(8,128)(2,1)S(1)} %get-tuple-element.349), channel_id=1, source_target_pairs={{4,0},{8,4},{12,8},{16,12},{20,16},{24,20},{28,24},{5,1},{9,5},{13... | collective-permute-start | bytes 3128 | tf_op jit(solution)/shard_map/ppermute | solution.py:17
  22.7 72.1 %collective-permute-start.6 = (bf16[52,10]{1,0:T(8,128)(2,1)S(1)}, bf16[52,10]{1,0:T(8,128)(2,1)S(1)}, u32[]{:S(2)}, u32[]{:S(2)}) collective-permute-start(bf16[52,10]{1,0:T(8,128)(2,1)S(1)} %get-tuple-element.348), channel_id=1, source_target_pairs={{0,4},{4,8},{8,12},{12,16},{16,20},{20,24},{24,28},{1,5},{5,9},{9,... | collective-permute-start | bytes 3128 | tf_op jit(solution)/shard_map/ppermute | solution.py:16
  73.1 26.3 %collective-permute-start.5 = (bf16[52,10]{1,0:T(8,128)(2,1)S(1)}, bf16[52,10]{1,0:T(8,128)(2,1)S(1)}, u32[]{:S(2)}, u32[]{:S(2)}) collective-permute-start(bf16[52,10]{1,0:T(8,128)(2,1)S(1)} %get-tuple-element.347), channel_id=1, source_target_pairs={{4,0},{8,4},{12,8},{16,12},{20,16},{24,20},{28,24},{5,1},{9,5},{13... | collective-permute-start | bytes 3128 | tf_op jit(solution)/shard_map/ppermute | solution.py:17
  75.0 26.3 %collective-permute-start.4 = (bf16[52,10]{1,0:T(8,128)(2,1)S(1)}, bf16[52,10]{1,0:T(8,128)(2,1)S(1)}, u32[]{:S(2)}, u32[]{:S(2)}) collective-permute-start(bf16[52,10]{1,0:T(8,128)(2,1)S(1)} %get-tuple-element.346), channel_id=1, source_target_pairs={{0,4},{4,8},{8,12},{12,16},{16,20},{20,24},{24,28},{1,5},{5,9},{9,... | collective-permute-start | bytes 3128 | tf_op jit(solution)/shard_map/ppermute | solution.py:16
  77.5 23.9 %collective-permute-start.3 = (bf16[52,10]{1,0:T(8,128)(2,1)S(1)}, bf16[52,10]{1,0:T(8,128)(2,1)S(1)}, u32[]{:S(2)}, u32[]{:S(2)}) collective-permute-start(bf16[52,10]{1,0:T(8,128)(2,1)S(1)} %get-tuple-element.345), channel_id=1, source_target_pairs={{4,0},{8,4},{12,8},{16,12},{20,16},{24,20},{28,24},{5,1},{9,5},{13... | collective-permute-start | bytes 3128 | tf_op jit(solution)/shard_map/ppermute | solution.py:17
  92.8 8.6 %collective-permute-start.2 = (bf16[52,10]{1,0:T(8,128)(2,1)S(1)}, bf16[52,10]{1,0:T(8,128)(2,1)S(1)}, u32[]{:S(2)}, u32[]{:S(2)}) collective-permute-start(bf16[52,10]{1,0:T(8,128)(2,1)S(1)} %get-tuple-element.344), channel_id=1, source_target_pairs={{0,4},{4,8},{8,12},{12,16},{16,20},{20,24},{24,28},{1,5},{5,9},{9,... | collective-permute-start | bytes 3128 | tf_op jit(solution)/shard_map/ppermute | solution.py:16
  94.8 6.8 %collective-permute-start.1 = (bf16[52,10]{1,0:T(8,128)(2,1)S(1)}, bf16[52,10]{1,0:T(8,128)(2,1)S(1)}, u32[]{:S(2)}, u32[]{:S(2)}) collective-permute-start(bf16[52,10]{1,0:T(8,128)(2,1)S(1)} %get-tuple-element.340), channel_id=1, source_target_pairs={{4,0},{8,4},{12,8},{16,12},{20,16},{24,20},{28,24},{5,1},{9,5},{13... | collective-permute-start | bytes 3128 | tf_op jit(solution)/shard_map/ppermute | solution.py:17
  99.4 5.9 %collective-permute-start = (bf16[52,10]{1,0:T(8,128)(2,1)S(1)}, bf16[52,10]{1,0:T(8,128)(2,1)S(1)}, u32[]{:S(2)}, u32[]{:S(2)}) collective-permute-start(bf16[52,10]{1,0:T(8,128)(2,1)S(1)} %get-tuple-element.339), channel_id=1, source_target_pairs={{0,4},{4,8},{8,12},{12,16},{16,20},{20,24},{24,28},{1,5},{5,9},{9,... | collective-permute-start | bytes 3128 | tf_op jit(solution)/shard_map/ppermute | solution.py:16
  129.7 4.1 %copy-start = (f32[4,5,6]{2,0,1:T(4,128)S(1)}, f32[4,5,6]{2,0,1:T(4,128)}, u32[]{:S(2)}) copy-start(f32[4,5,6]{2,0,1:T(4,128)} %get-tuple-element.67) | copy-start | bytes 1444 | tf_op jit(solution)/shard_map/cond
  154.7 53.5 %copy-start.5 = (f32[21]{0:T(128)S(1)}, f32[21]{0:T(128)}, u32[]{:S(2)}) copy-start(f32[21]{0:T(128)} %param.21) | copy-start | bytes 256
  179.3 4.1 %copy-start.3 = (f32[4,5,6]{2,0,1:T(4,128)S(1)}, f32[4,5,6]{2,0,1:T(4,128)}, u32[]{:S(2)}) copy-start(f32[4,5,6]{2,0,1:T(4,128)} %get-tuple-element.46) | copy-start | bytes 1444 | tf_op jit(solution)/shard_map/cond
  203.9 138.6 %copy-start.4 = (f32[32,384]{1,0:T(8,128)}, f32[32,384]{1,0:T(8,128)S(1)}, u32[]{:S(2)}) copy-start(f32[32,384]{1,0:T(8,128)S(1)} %add_divide_fusion) | copy-start | bytes 147460
  203.9 5.0 %collective-permute-start.9 = (f32[32,10]{1,0:T(8,128)S(1)}, f32[32,10]{1,0:T(8,128)S(1)}, u32[]{:S(2)}, u32[]{:S(2)}) collective-permute-start(f32[32,10]{1,0:T(8,128)S(1)} %get-tuple-element.338), channel_id=1, source_target_pairs={{4,0},{8,4},{12,8},{16,12},{20,16},{24,20},{28,24},{5,1},{9,5},{13... | collective-permute-start | bytes 3848 | tf_op jit(solution)/shard_map/ppermute | solution.py:17
  205.9 6.0 %collective-permute-start.8 = (f32[32,10]{1,0:T(8,128)S(1)}, f32[32,10]{1,0:T(8,128)S(1)}, u32[]{:S(2)}, u32[]{:S(2)}) collective-permute-start(f32[32,10]{1,0:T(8,128)S(1)} %get-tuple-element.337), channel_id=1, source_target_pairs={{0,4},{4,8},{8,12},{12,16},{16,20},{20,24},{24,28},{1,5},{5,9},{9,... | collective-permute-start | bytes 3848 | tf_op jit(solution)/shard_map/ppermute | solution.py:16
  225.2 99.4 %collective-permute-start.11 = (f32[10,384]{1,0:T(8,128)S(1)}, f32[10,384]{1,0:T(8,128)S(1)}, u32[]{:S(2)}, u32[]{:S(2)}) collective-permute-start(f32[10,384]{1,0:T(8,128)S(1)} %get-tuple-element.336), channel_id=1, source_target_pairs={{1,0},{2,1},{3,2},{5,4},{6,5},{7,6},{9,8},{10,9},{11,10},{13,12},{... | collective-permute-start | bytes 46088 | tf_op jit(solution)/shard_map/ppermute | solution.py:17
  323.1 5.7 %collective-permute-start.10 = (f32[10,384]{1,0:T(8,128)S(1)}, f32[10,384]{1,0:T(8,128)S(1)}, u32[]{:S(2)}, u32[]{:S(2)}) collective-permute-start(f32[10,384]{1,0:T(8,128)S(1)} %get-tuple-element.335), channel_id=1, source_target_pairs={{0,1},{1,2},{2,3},{4,5},{5,6},{6,7},{8,9},{9,10},{10,11},{12,13},{... | collective-permute-start | bytes 46088 | tf_op jit(solution)/shard_map/ppermute | solution.py:16
where the time goes:
time: 346 us; the launch traced here: 342 us
  starting transfers between devices  125 us (36%)
  other arithmetic  73.5 us (21%)
  local copies, waits for them, and re-layouts  55.5 us (16%)
  blocking collectives  53.5 us (15%)
  matrix products  11.9 us (3%)
  between operations  11.2 us (3%)
  waiting for transfers between devices  11.1 us (3%)
    ppermute x6, starting transfers between devices, padded(): after = lax.ppermute(initial, axis, down)  112 us
    all_gather x4, blocking collectives, on_device(): lax.all_gather(exposures[member], 'narrow', axis=0, tiled=True)  53.5 us
    add x4, other arithmetic, matched_tile(): coeffs[0] + coeffs[1] * x_coord + coeffs[2] * y_coord  34.9 us
    reshape x2, local copies, waits for them, and re-layouts, respond(): table = table.astype(jnp.bfloat16).reshape(side, span, kernel_total * block)  17.8 us
    dot_general x2, local copies, waits for them, and re-layouts, respond(): jnp.einsum('jarc,acn->jrn', patches, table, preferred_element_type=jnp.fl...  17.6 us
    add x1, other arithmetic, on_device(): detection + filter_taps[offset] * across[offset:offset + tile_rows]  13.7 us
    add x1, other arithmetic, on_device(): inner = inner + filter_taps[offset] * framed[:, offset:offset + tile_cols]  13.3 us
    ppermute x6, starting transfers between devices, padded(): before = lax.ppermute(last, axis, up)  12.4 us
  transfers between devices with their start and end apart: 12, of which 4 were waited for; matrix products, arithmetic and copies ran while one was open for 3% of the time, Pallas kernels for 0%

commit v1 on v0

v1 whole, which is shorter than its diff:
```python
import functools

import jax
import jax.numpy as jnp
from jax import lax
from jax.experimental import pallas as pl
from jax.experimental.pallas import tpu as pltpu
from jax.sharding import PartitionSpec as P

LANES = 128
VMEM_BYTES = 48 << 20


def rounded(value, unit):
    return -(-value // unit) * unit


def sizes(tile_rows, side):
    half = side // 2
    out_rows = rounded(tile_rows + 2 * half, 8)
    in_rows = rounded(tile_rows + 4 * half, 16)
    return half, out_rows, in_rows


def band_matrix_kernel(side, tile_rows, base_ref, band_ref):
    half, out_rows, in_rows = sizes(tile_rows, side)
    kernel_total, wide = base_ref.shape
    depth = band_ref.shape[1]
    lane = lax.broadcasted_iota(jnp.int32, (8, wide), 1)
    place = lax.rem(lane, in_rows)
    row = lax.broadcasted_iota(jnp.int32, (8, wide), 0)
    split = tile_rows + half
    for kernel in range(kernel_total):
        spread = jnp.broadcast_to(base_ref[kernel : kernel + 1, :], (8, wide))

        def shifted(shift, spread=spread):
            plain = pltpu.roll(spread, shift % wide, 1)
            plain = pltpu.roll(plain, 0, 1, stride=1, stride_axis=0)
            wrapped = pltpu.roll(spread, (shift + in_rows) % wide, 1)
            wrapped = pltpu.roll(wrapped, 0, 1, stride=1, stride_axis=0)
            return jnp.where(place >= tile_rows + 2 * half + 4, wrapped, plain)

        parts = []
        for first in range(0, out_rows, 8):
            if first + 8 <= split:
                block = shifted(first - half)
            elif first >= split:
                block = shifted(first - out_rows - half)
            else:
                block = jnp.where(
                    row + first < split, shifted(first - half), shifted(first - out_rows - half)
                )
            parts.append(block)
        block = jnp.concatenate(parts, axis=0)[:, :depth]
        band_ref[kernel * out_rows : (kernel + 1) * out_rows, :] = block.astype(jnp.bfloat16)


def band_matrix(basis_kernels, tile_rows):
    kernel_total, side = basis_kernels.shape[:2]
    _, out_rows, in_rows = sizes(tile_rows, side)
    depth = side * in_rows
    wide = rounded(depth, LANES)
    base = basis_kernels.astype(jnp.float32).transpose(0, 2, 1)
    base = jnp.pad(base, ((0, 0), (0, 0), (0, in_rows - side))).reshape(kernel_total, depth)
    base = jnp.pad(base, ((0, 0), (0, wide - depth)))
    return pl.pallas_call(
        functools.partial(band_matrix_kernel, side, tile_rows),
        out_shape=jax.ShapeDtypeStruct((kernel_total * out_rows, depth), jnp.bfloat16),
        compiler_params=pltpu.CompilerParams(vmem_limit_bytes=VMEM_BYTES),
        name="band_matrix",
    )(base)


def edges_kernel(rim, tile_ref, core_ref, cross_ref):
    odd = lax.rem(lax.axis_index("wide"), 2) == 1
    members, rows, columns = tile_ref.shape
    lane = lax.broadcasted_iota(jnp.int32, (rows, LANES), 1)
    leftward = jnp.zeros((rows, LANES), jnp.bfloat16)
    rightward = jnp.zeros((rows, LANES), jnp.bfloat16)
    for member in range(members):
        own = lane // 32 == member
        first = pltpu.roll(tile_ref[member, :, :LANES], 32 * member, 1)
        last = pltpu.roll(tile_ref[member, :, columns - LANES :], (32 * member + 32) % LANES, 1)
        leftward = jnp.where(own, first, leftward)
        rightward = jnp.where(own, last, rightward)

    @pl.when(odd)
    def _():
        core_ref[...] = leftward
        cross_ref[...] = rightward

    @pl.when(jnp.logical_not(odd))
    def _():
        core_ref[...] = rightward
        cross_ref[...] = leftward


def coadd_kernel(
    peers,
    wide_peers,
    side,
    coef_ref,
    weight_ref,
    start_ref,
    count_ref,
    taps_ref,
    band_ref,
    *refs,
):
    tiles, edges = refs[:peers], refs[peers : 2 * peers]
    coadd_ref, detection_ref, frame, patches, tall = refs[2 * peers :]
    members, tile_rows, tile_cols = tiles[0].shape
    half, out_rows, in_rows = sizes(tile_rows, side)
    rim = 2 * half
    total_cols = tile_cols + LANES
    kernel_total = band_ref.shape[0] // out_rows
    narrow, wide = lax.axis_index("narrow"), lax.axis_index("wide")
    odd = lax.rem(wide, 2)
    row_base = narrow * tile_rows
    band_rows, band_cols = peers * tile_rows, wide_peers * tile_cols

    edge_lane = lax.broadcasted_iota(jnp.int32, (tile_rows, LANES), 1)
    keep_after = (edge_lane < rim) & (wide < wide_peers - 1)
    keep_before = (edge_lane >= LANES - rim) & (wide > 0)
    none = jnp.zeros((tile_rows, LANES), jnp.bfloat16)
    for index in range(peers):
        slot = jnp.bitwise_xor(narrow, index)
        after = edges[index][odd]
        before = edges[index][1 - odd]
        for member in range(members):
            frame[slot, member, :, :tile_cols] = tiles[index][member]
            right = pltpu.roll(after, (LANES - 32 * member) % LANES, 1)
            left = pltpu.roll(before, (LANES + 96 - 32 * member) % LANES, 1)
            frame[slot, member, :, tile_cols:] = jnp.where(
                keep_after, right, jnp.where(keep_before, left, none)
            )

    place = lax.broadcasted_iota(jnp.int32, (out_rows, LANES), 0)
    row = row_base + jnp.where(place < tile_rows + half, place, place - out_rows)
    y_coord = (2 * row + 1).astype(jnp.float32) / band_rows - 1.0
    lane = lax.broadcasted_iota(jnp.int32, (8, total_cols), 1)
    column = wide * tile_cols + jnp.where(lane < tile_cols + LANES // 2, lane, lane - total_cols)
    x_coord = ((2 * column + 1).astype(jnp.float32) / band_cols - 1.0)[:1]
    in_band = (column >= 0) & (column < band_cols)
    weighting = []
    for member in range(members):
        inside = (row >= start_ref[member]) & (row < start_ref[member] + count_ref[member])
        weighting.append(jnp.where(inside, weight_ref[member], 0.0))
    denominator = functools.reduce(jnp.add, weighting)
    valid = (row >= 0) & (row < band_rows)
    inverse = jnp.where(valid, 1.0 / jnp.where(valid, denominator, 1.0), 0.0)

    in_place = lax.broadcasted_iota(jnp.int32, (in_rows, total_cols), 0)
    in_offset = jnp.where(in_place < tile_rows + rim + 4, in_place, in_place - in_rows)
    sums = [jnp.zeros((out_rows, total_cols), jnp.float32) for _ in range(3)]

    def over_columns(array):
        return jnp.concatenate([array] * (total_cols // LANES), axis=1)

    for member in range(members):
        slot = narrow - start_ref[member] // tile_rows
        here = jnp.clip(slot, 0, peers - 1)
        above = jnp.clip(slot - 1, 0, peers - 1)
        below = jnp.clip(slot + 1, 0, peers - 1)
        mixed = lax.broadcasted_iota(jnp.int32, (16, total_cols), 0) < 8
        window = jnp.concatenate(
            [
                frame[here, member],
                frame[below, member, :16],
                jnp.where(mixed, frame[below, member, 16:], frame[above, member, :16]),
                frame[above, member, 16:],
            ],
            axis=0,
        )
        frame_row = in_offset + (row_base - start_ref[member])
        present = (frame_row >= 0) & (frame_row < count_ref[member])
        window = jnp.where(present, window, jnp.zeros((), window.dtype))
        for tap in range(side):
            patches[member, tap * in_rows : (tap + 1) * in_rows, :] = pltpu.roll(
                window, (half - tap) % total_cols, 1
            )
        response = jnp.dot(band_ref[...], patches[member], preferred_element_type=jnp.float32)
        scale = weighting[member] * inverse
        for kernel in range(kernel_total):
            coeffs = [coef_ref[member, kernel, order] for order in range(6)]
            own = response[kernel * out_rows : (kernel + 1) * out_rows]
            factors = (
                coeffs[0] + coeffs[2] * y_coord + coeffs[5] * (y_coord * y_coord),
                coeffs[1] + coeffs[4] * y_coord,
                coeffs[3],
            )
            sums = [
                value + over_columns(factor * scale) * own
                for value, factor in zip(sums, factors, strict=True)
            ]
    coadded = sums[0] + x_coord * (sums[1] + x_coord * sums[2])
    coadd_ref[...] = coadded[:tile_rows, :tile_cols]

    coadded = jnp.where(in_band[:1], coadded, 0.0)
    lead = out_rows - tile_rows - 8
    tall[lead : lead + tile_rows + 16, :] = coadded[: tile_rows + 16]
    tall[:lead, :] = coadded[out_rows - lead :]
    filtered = taps_ref[0] * tall[lead - half : lead - half + tile_rows, :]
    for tap in range(1, side):
        begin = lead - half + tap
        filtered = filtered + taps_ref[tap] * tall[begin : begin + tile_rows, :]
    detection = taps_ref[0] * pltpu.roll(filtered, half, 1)
    for tap in range(1, side):
        detection = detection + taps_ref[tap] * pltpu.roll(filtered, (half - tap) % total_cols, 1)
    detection_ref[...] = detection[:, :tile_cols]


def on_device(
    exposures, basis_kernels, poly_coef, exposure_weight, row_start, row_count, filter_taps
):
    members, tile_rows, tile_cols = exposures.shape
    side = basis_kernels.shape[1]
    half, out_rows, in_rows = sizes(tile_rows, side)
    peers, wide_peers = lax.axis_size("narrow"), lax.axis_size("wide")

    def swapped(array, index):
        return lax.ppermute(array, "narrow", [(i, i ^ index) for i in range(peers)])

    core_pairs = [(i, i ^ 1) for i in range(wide_peers)]
    cross_pairs = [(i, ((i - 1) ^ 1) + 1) for i in range(1, wide_peers - 1)]
    cross_pairs += [(0, wide_peers - 1), (wide_peers - 1, 0)]

    edge_shape = jax.ShapeDtypeStruct((tile_rows, LANES), exposures.dtype)
    to_core, to_cross = pl.pallas_call(
        functools.partial(edges_kernel, 2 * half), out_shape=(edge_shape, edge_shape), name="edges"
    )(exposures)
    from_core = lax.ppermute(to_core, "wide", core_pairs)
    from_cross = lax.ppermute(to_cross, "wide", cross_pairs)
    tiles = [exposures] + [swapped(exposures, index) for index in range(1, peers)]
    both = jnp.stack([from_core, from_cross])
    edges = [both] + [swapped(both, index) for index in range(1, peers)]

    band = band_matrix(basis_kernels, tile_rows)
    depth = band.shape[1]
    total_cols = tile_cols + LANES
    smem = pl.BlockSpec(memory_space=pltpu.SMEM)
    vmem = pl.BlockSpec(memory_space=pltpu.VMEM)
    out = jax.ShapeDtypeStruct((tile_rows, tile_cols), jnp.float32)
    return pl.pallas_call(
        functools.partial(coadd_kernel, peers, wide_peers, side),
        out_shape=(out, out),
        in_specs=[smem] * 5 + [vmem] * (1 + 2 * peers),
        out_specs=(vmem, vmem),
        scratch_shapes=[
            pltpu.VMEM((peers, members, tile_rows, total_cols), jnp.bfloat16),
            pltpu.VMEM((members, depth, total_cols), jnp.bfloat16),
            pltpu.VMEM((out_rows + 8, total_cols), jnp.float32),
        ],
        compiler_params=pltpu.CompilerParams(vmem_limit_bytes=VMEM_BYTES),
        name="coadd",
    )(
        poly_coef,
        exposure_weight,
        row_start,
        row_count,
        filter_taps,
        band,
        *tiles,
        *edges,
    )


def solution(mesh):
    placed = (P(None, "narrow", "wide"), P(), P(), P(), P(), P(), P())
    return jax.shard_map(
        on_device,
        mesh=mesh,
        in_specs=placed,
        out_specs=(P("narrow", "wide"), P("narrow", "wide")),
        check_vma=False,
    )
```

time: 346 us -> 27.8 us (0.08)
  the two profiles are of different devices: /device:TPU:28 before, /device:TPU:0 now
where the time goes in v1:
time: 27.8 us; the launch traced here: 27.7 us
  starting transfers between devices  12.8 us (46%)
  Pallas kernels  12.1 us (44%)
  waiting for transfers between devices  1.59 us (6%)
  between operations  0.8 us (3%)
  local copies, waits for them, and re-layouts  0.29 us (1%)
    ppermute x6, starting transfers between devices, swapped(): return lax.ppermute(array, 'narrow', [(i, i ^ index) for i in range(peers)])  8.83 us
    pallas_call x1, Pallas kernels, band_matrix(): pl.pallas_call(functools.partial(band_matrix_kernel, side, tile_rows), ou...  5.36 us
    pallas_call x1, Pallas kernels, on_device(): pl.pallas_call(functools.partial(coadd_kernel, peers, wide_peers, side),...  5.14 us
    ppermute x1, starting transfers between devices, on_device(): from_cross = lax.ppermute(to_cross, 'wide', cross_pairs)  3.56 us
    pallas_call x1, Pallas kernels, on_device(): pl.pallas_call(functools.partial(edges_kernel, 2 * half), out_shape=(edge...  1.64 us
    ppermute x1, waiting for transfers between devices, on_device(): from_cross = lax.ppermute(to_cross, 'wide', cross_pairs)  1.57 us
  transfers between devices with their start and end apart: 8, of which 1 were waited for; matrix products, arithmetic and copies ran while one was open for 1% of the time, Pallas kernels for 19%

profile of v1, /device:TPU:0, one launch (start us, length us, event | category | flops | bytes accessed | tf_op | source)
XLA Modules:
  0.0 27.7 jit_solution(7531040935546198338)
XLA Ops:
  0.6 0.0 copy-start
  0.6 1.6 %edges.1 = (bf16[32,128]{1,0:T(8,128)(2,1)}, bf16[32,128]{1,0:T(8,128)(2,1)}) custom-call(bf16[4,32,384]{2,1,0:T(8,128)(2,1)} %refs_0_.1), custom_call_target="tpu_custom_call" | custom-call | tf_op jit(solution)/shard_map/edges/pallas_call | solution.py:229
  2.3 0.0 copy-start.5
  2.3 0.5 %collective-permute-start.3 = (bf16[32,128]{1,0:T(8,128)(2,1)}, bf16[32,128]{1,0:T(8,128)(2,1)S(1)}, u32[]{:S(2)}, u32[]{:S(2)}) collective-permute-start(bf16[32,128]{1,0:T(8,128)(2,1)} %get-tuple-element.4), channel_id=1, source_target_pairs={{0,4},{4,0},{8,12},{12,8},{16,20},{20,16},{24,28},{28,24},{1,5},{5... | collective-permute-start | bytes 24584 | tf_op jit(solution)/shard_map/ppermute | solution.py:232
  2.7 3.6 %collective-permute-start.4 = (bf16[32,128]{1,0:T(8,128)(2,1)}, bf16[32,128]{1,0:T(8,128)(2,1)S(1)}, u32[]{:S(2)}, u32[]{:S(2)}) collective-permute-start(bf16[32,128]{1,0:T(8,128)(2,1)} %get-tuple-element.5), channel_id=1, source_target_pairs={{4,8},{8,4},{12,16},{16,12},{20,24},{24,20},{0,28},{28,0},{5,9},{9... | collective-permute-start | bytes 24584 | tf_op jit(solution)/shard_map/ppermute | solution.py:233
  6.3 0.0 collective-permute-done.3
  6.3 1.6 %collective-permute-done.4 = bf16[32,128]{1,0:T(8,128)(2,1)S(1)} collective-permute-done((bf16[32,128]{1,0:T(8,128)(2,1)}, bf16[32,128]{1,0:T(8,128)(2,1)S(1)}, u32[]{:S(2)}, u32[]{:S(2)}) %collective-permute-start.4) | collective-permute-done | bytes 8224 | tf_op jit(solution)/shard_map/ppermute | solution.py:233
  7.9 3.7 %collective-permute-start.7 = (bf16[2,32,128]{2,1,0:T(8,128)(2,1)S(1)}, bf16[2,32,128]{2,1,0:T(8,128)(2,1)S(1)}, u32[]{:S(2)}, u32[]{:S(2)}) collective-permute-start(bf16[2,32,128]{2,1,0:T(8,128)(2,1)S(1)} %pad_maximum_fusion.refs_4_), channel_id=1, source_target_pairs={{0,3},{1,2},{2,1},{3,0},{4,7},{5,6},{6,5},{7,4},{8,11},{9,10},{10,... | collective-permute-start | bytes 49160 | tf_op jit(solution)/shard_map/ppermute | solution.py:222
  11.5 0.0 copy-done
  11.5 0.2 collective-permute-start.2
  11.7 0.8 %collective-permute-start.1 = (bf16[4,32,384]{2,1,0:T(8,128)(2,1)S(1)}, bf16[4,32,384]{2,1,0:T(8,128)(2,1)S(1)}, u32[]{:S(2)}, u32[]{:S(2)}) collective-permute-start(bf16[4,32,384]{2,1,0:T(8,128)(2,1)S(1)} %copy-done), channel_id=1, source_target_pairs={{0,2},{1,3},{2,0},{3,1},{4,6},{5,7},{6,4},{7,5},{8,10},{9,11},{10,... | collective-permute-start | bytes 294920 | tf_op jit(solution)/shard_map/ppermute | solution.py:222
  12.5 3.4 %collective-permute-start = (bf16[4,32,384]{2,1,0:T(8,128)(2,1)S(1)}, bf16[4,32,384]{2,1,0:T(8,128)(2,1)S(1)}, u32[]{:S(2)}, u32[]{:S(2)}) collective-permute-start(bf16[4,32,384]{2,1,0:T(8,128)(2,1)S(1)} %copy-done), channel_id=1, source_target_pairs={{0,1},{1,0},{2,3},{3,2},{4,5},{5,4},{6,7},{7,6},{8,9},{9,8},{10,11... | collective-permute-start | bytes 294920 | tf_op jit(solution)/shard_map/ppermute | solution.py:222
  15.9 0.0 copy-done.5
  15.9 0.1 copy.11
  16.1 0.1 reshape.8
  16.2 0.0 copy-start.6
  16.2 0.1 collective-permute-start.6
  16.3 0.0 collective-permute-done.7.refs_7_
  16.3 0.7 %collective-permute-start.5 = (bf16[2,32,128]{2,1,0:T(8,128)(2,1)S(1)}, bf16[2,32,128]{2,1,0:T(8,128)(2,1)S(1)}, u32[]{:S(2)}, u32[]{:S(2)}) collective-permute-start(bf16[2,32,128]{2,1,0:T(8,128)(2,1)S(1)} %pad_maximum_fusion.refs_4_), channel_id=1, source_target_pairs={{0,1},{1,0},{2,3},{3,2},{4,5},{5,4},{6,7},{7,6},{8,9},{9,8},{10,11... | collective-permute-start | bytes 49160 | tf_op jit(solution)/shard_map/ppermute | solution.py:222
  17.0 0.0 copy-done.6
  17.0 0.0 copy-start.1
  17.0 0.0 copy-start.2
  17.0 0.0 copy-start.3
  17.1 0.0 copy-start.4
  17.1 5.4 %band_matrix.1.band_ref = bf16[280,1680]{1,0:T(8,128)(2,1)S(1)} custom-call(f32[5,1792]{1,0:T(8,128)S(1)} %pad_convert_fusion.base_ref), custom_call_target="tpu_custom_call" | custom-call | tf_op jit(solution)/shard_map/band_matrix/pallas_call | solution.py:66
  22.4 0.0 collective-permute-done.6.refs_6_
  22.4 0.0 collective-permute-done.5.refs_5_
  22.5 0.0 collective-permute-done.2.refs_3_
  22.5 0.0 collective-permute-done.1.refs_2_
  22.5 0.0 collective-permute-done.refs_1_
  22.5 0.0 copy-done.1
  22.5 0.0 copy-done.2
  22.5 0.0 copy-done.3
  22.5 0.0 copy-done.4
  22.5 5.1 %coadd.1 = (f32[32,384]{1,0:T(8,128)}, f32[32,384]{1,0:T(8,128)}) custom-call(f32[4,5,6]{2,1,0:T(8,128)S(1)} %copy.10.coef_ref, f32[4]{0:T(128)S(1)} %copy-done.1, s32[4]{0:T(128)S(1)} %copy-done.2, s32[4]{0:T(128)S(1)} %copy-done.3, f32[21]{0:T(128)S(1)} %copy-done.4, bf16[280,1680]{1,0:T(8,128)(2,1)S(1)} %band_matrix.1.band_ref, ...), custom_call_target="tpu_custom_call" | custom-call | tf_op jit(solution)/shard_map/coadd/pallas_call | solution.py:244
  (4 shorter events, 0.0 us)
Async XLA Ops:
  0.6 10.9 %copy-start = (bf16[4,32,384]{2,1,0:T(8,128)(2,1)S(1)}, bf16[4,32,384]{2,1,0:T(8,128)(2,1)}, u32[]{:S(2)}) copy-start(bf16[4,32,384]{2,1,0:T(8,128)(2,1)} %refs_0_.1) | copy-start | bytes 294916
  2.3 13.6 %copy-start.5 = (bf16[5,21,21]{2,1,0:T(8,128)(2,1)S(1)}, bf16[5,21,21]{2,1,0:T(8,128)(2,1)}, u32[]{:S(2)}) copy-start(bf16[5,21,21]{2,1,0:T(8,128)(2,1)} %param.8) | copy-start | bytes 13234
  2.3 4.0 %collective-permute-start.3 = (bf16[32,128]{1,0:T(8,128)(2,1)}, bf16[32,128]{1,0:T(8,128)(2,1)S(1)}, u32[]{:S(2)}, u32[]{:S(2)}) collective-permute-start(bf16[32,128]{1,0:T(8,128)(2,1)} %get-tuple-element.4), channel_id=1, source_target_pairs={{0,4},{4,0},{8,12},{12,8},{16,20},{20,16},{24,28},{28,24},{1,5},{5... | collective-permute-start | bytes 24584 | tf_op jit(solution)/shard_map/ppermute | solution.py:232
  2.7 5.1 %collective-permute-start.4 = (bf16[32,128]{1,0:T(8,128)(2,1)}, bf16[32,128]{1,0:T(8,128)(2,1)S(1)}, u32[]{:S(2)}, u32[]{:S(2)}) collective-permute-start(bf16[32,128]{1,0:T(8,128)(2,1)} %get-tuple-element.5), channel_id=1, source_target_pairs={{4,8},{8,4},{12,16},{16,12},{20,24},{24,20},{0,28},{28,0},{5,9},{9... | collective-permute-start | bytes 24584 | tf_op jit(solution)/shard_map/ppermute | solution.py:233
  7.9 8.4 %collective-permute-start.7 = (bf16[2,32,128]{2,1,0:T(8,128)(2,1)S(1)}, bf16[2,32,128]{2,1,0:T(8,128)(2,1)S(1)}, u32[]{:S(2)}, u32[]{:S(2)}) collective-permute-start(bf16[2,32,128]{2,1,0:T(8,128)(2,1)S(1)} %pad_maximum_fusion.refs_4_), channel_id=1, source_target_pairs={{0,3},{1,2},{2,1},{3,0},{4,7},{5,6},{6,5},{7,4},{8,11},{9,10},{10,... | collective-permute-start | bytes 49160 | tf_op jit(solution)/shard_map/ppermute | solution.py:222
  11.5 10.9 %collective-permute-start.2 = (bf16[4,32,384]{2,1,0:T(8,128)(2,1)S(1)}, bf16[4,32,384]{2,1,0:T(8,128)(2,1)S(1)}, u32[]{:S(2)}, u32[]{:S(2)}) collective-permute-start(bf16[4,32,384]{2,1,0:T(8,128)(2,1)S(1)} %copy-done), channel_id=1, source_target_pairs={{0,3},{1,2},{2,1},{3,0},{4,7},{5,6},{6,5},{7,4},{8,11},{9,10},{10,... | collective-permute-start | bytes 294920 | tf_op jit(solution)/shard_map/ppermute | solution.py:222
  11.7 10.8 %collective-permute-start.1 = (bf16[4,32,384]{2,1,0:T(8,128)(2,1)S(1)}, bf16[4,32,384]{2,1,0:T(8,128)(2,1)S(1)}, u32[]{:S(2)}, u32[]{:S(2)}) collective-permute-start(bf16[4,32,384]{2,1,0:T(8,128)(2,1)S(1)} %copy-done), channel_id=1, source_target_pairs={{0,2},{1,3},{2,0},{3,1},{4,6},{5,7},{6,4},{7,5},{8,10},{9,11},{10,... | collective-permute-start | bytes 294920 | tf_op jit(solution)/shard_map/ppermute | solution.py:222
  12.5 9.9 %collective-permute-start = (bf16[4,32,384]{2,1,0:T(8,128)(2,1)S(1)}, bf16[4,32,384]{2,1,0:T(8,128)(2,1)S(1)}, u32[]{:S(2)}, u32[]{:S(2)}) collective-permute-start(bf16[4,32,384]{2,1,0:T(8,128)(2,1)S(1)} %copy-done), channel_id=1, source_target_pairs={{0,1},{1,0},{2,3},{3,2},{4,5},{5,4},{6,7},{7,6},{8,9},{9,8},{10,11... | collective-permute-start | bytes 294920 | tf_op jit(solution)/shard_map/ppermute | solution.py:222
  16.2 0.8 %copy-start.6 = (f32[4,5,6]{2,0,1:T(4,128)S(1)}, f32[4,5,6]{2,0,1:T(4,128)}, u32[]{:S(2)}) copy-start(f32[4,5,6]{2,0,1:T(4,128)} %param.9) | copy-start | bytes 1444
  16.2 6.3 %collective-permute-start.6 = (bf16[2,32,128]{2,1,0:T(8,128)(2,1)S(1)}, bf16[2,32,128]{2,1,0:T(8,128)(2,1)S(1)}, u32[]{:S(2)}, u32[]{:S(2)}) collective-permute-start(bf16[2,32,128]{2,1,0:T(8,128)(2,1)S(1)} %pad_maximum_fusion.refs_4_), channel_id=1, source_target_pairs={{0,2},{1,3},{2,0},{3,1},{4,6},{5,7},{6,4},{7,5},{8,10},{9,11},{10,... | collective-permute-start | bytes 49160 | tf_op jit(solution)/shard_map/ppermute | solution.py:222
  16.3 6.2 %collective-permute-start.5 = (bf16[2,32,128]{2,1,0:T(8,128)(2,1)S(1)}, bf16[2,32,128]{2,1,0:T(8,128)(2,1)S(1)}, u32[]{:S(2)}, u32[]{:S(2)}) collective-permute-start(bf16[2,32,128]{2,1,0:T(8,128)(2,1)S(1)} %pad_maximum_fusion.refs_4_), channel_id=1, source_target_pairs={{0,1},{1,0},{2,3},{3,2},{4,5},{5,4},{6,7},{7,6},{8,9},{9,8},{10,11... | collective-permute-start | bytes 49160 | tf_op jit(solution)/shard_map/ppermute | solution.py:222
  17.0 5.5 %copy-start.1 = (f32[4]{0:T(128)S(1)}, f32[4]{0:T(128)}, u32[]{:S(2)}) copy-start(f32[4]{0:T(128)} %weight_ref.1) | copy-start | bytes 52
  17.0 5.5 %copy-start.2 = (s32[4]{0:T(128)S(1)}, s32[4]{0:T(128)}, u32[]{:S(2)}) copy-start(s32[4]{0:T(128)} %start_ref.1) | copy-start | bytes 52
  17.0 5.5 %copy-start.3 = (s32[4]{0:T(128)S(1)}, s32[4]{0:T(128)}, u32[]{:S(2)}) copy-start(s32[4]{0:T(128)} %count_ref.1) | copy-start | bytes 52
  17.1 5.5 %copy-start.4 = (f32[21]{0:T(128)S(1)}, f32[21]{0:T(128)}, u32[]{:S(2)}) copy-start(f32[21]{0:T(128)} %taps_ref.1) | copy-start | bytes 256

commit v2 on v1

v2 whole, which is shorter than its diff:
```python
import functools

import jax
import jax.numpy as jnp
from jax import lax
from jax.experimental import pallas as pl
from jax.experimental.pallas import tpu as pltpu
from jax.sharding import PartitionSpec as P

LANES = 128
VMEM_BYTES = 48 << 20


def rounded(value, unit):
    return -(-value // unit) * unit


def sizes(tile_rows, side):
    half = side // 2
    out_rows = rounded(tile_rows + 2 * half, 8)
    in_rows = rounded(tile_rows + 4 * half, 16)
    return half, out_rows, in_rows


def band_matrix_kernel(out_rows, base_ref, band_ref):
    kernel_total, wide = base_ref.shape
    depth = band_ref.shape[1]
    parts = []
    for kernel in range(kernel_total):
        spread = jnp.broadcast_to(base_ref[kernel : kernel + 1, :], (8, wide))
        block = pltpu.roll(spread, 0, 1, stride=1, stride_axis=0)
        parts += [block] + [pltpu.roll(block, first, 1) for first in range(8, out_rows, 8)]
    band_ref[...] = jnp.concatenate(parts, axis=0).astype(jnp.bfloat16)[:, :depth]


def band_matrix(basis_kernels, tile_rows):
    kernel_total, side = basis_kernels.shape[:2]
    half, out_rows, in_rows = sizes(tile_rows, side)
    depth = side * in_rows + 16
    wide = rounded(depth, LANES)
    lead = 32 - 2 * half
    base = basis_kernels.astype(jnp.float32).transpose(0, 2, 1)
    base = jnp.pad(base, ((0, 0), (0, 0), (0, in_rows - side))).reshape(kernel_total, -1)
    base = jnp.pad(base, ((0, 0), (lead, wide - lead - base.shape[1])))
    return pl.pallas_call(
        functools.partial(band_matrix_kernel, out_rows),
        out_shape=jax.ShapeDtypeStruct((kernel_total * out_rows, depth), jnp.bfloat16),
        compiler_params=pltpu.CompilerParams(vmem_limit_bytes=VMEM_BYTES),
        name="band_matrix",
    )(base)


def place_kernel(peers, start_ref, count_ref, *refs):
    tiles = refs[:peers]
    window_ref, core_ref, cross_ref, frame = refs[peers:]
    members, tile_rows, tile_cols = tiles[0].shape
    narrow = lax.axis_index("narrow")
    odd = lax.rem(lax.axis_index("wide"), 2) == 1
    for index in range(peers):
        frame[jnp.bitwise_xor(narrow, index)] = tiles[index][...]
    rows = window_ref.shape[1]
    lane = lax.broadcasted_iota(jnp.int32, (rows, LANES), 1)
    leftward = jnp.zeros((rows, LANES), jnp.bfloat16)
    rightward = jnp.zeros((rows, LANES), jnp.bfloat16)
    for member in range(members):
        slot = narrow - start_ref[member] // tile_rows
        here = jnp.clip(slot, 0, peers - 1)
        above = jnp.clip(slot - 1, 0, peers - 1)
        below = jnp.clip(slot + 1, 0, peers - 1)
        window = jnp.concatenate([frame[above, member], frame[here, member], frame[below, member]])
        frame_row = lax.broadcasted_iota(jnp.int32, window.shape, 0) + (slot - 1) * tile_rows
        present = (frame_row >= 0) & (frame_row < count_ref[member])
        window = jnp.where(present, window, jnp.zeros((), window.dtype))
        window_ref[member] = window
        own = lane // 32 == member
        first = pltpu.roll(window[:, :LANES], 32 * member, 1)
        last = pltpu.roll(window[:, tile_cols - LANES :], (32 * member + 32) % LANES, 1)
        leftward = jnp.where(own, first, leftward)
        rightward = jnp.where(own, last, rightward)

    @pl.when(odd)
    def _():
        core_ref[...] = leftward
        cross_ref[...] = rightward

    @pl.when(jnp.logical_not(odd))
    def _():
        core_ref[...] = rightward
        cross_ref[...] = leftward


def coadd_kernel(
    peers,
    wide_peers,
    side,
    coef_ref,
    weight_ref,
    start_ref,
    count_ref,
    taps_ref,
    band_ref,
    window_ref,
    core_ref,
    cross_ref,
    coadd_ref,
    detection_ref,
    patches,
    tall,
):
    tile_rows, tile_cols = coadd_ref.shape
    members, window_rows = window_ref.shape[:2]
    half, out_rows, in_rows = sizes(tile_rows, side)
    rim = 2 * half
    total_cols = tile_cols + LANES
    kernel_total = band_ref.shape[0] // out_rows
    narrow, wide = lax.axis_index("narrow"), lax.axis_index("wide")
    odd = lax.rem(wide, 2) == 1
    row_base = narrow * tile_rows
    band_rows, band_cols = peers * tile_rows, wide_peers * tile_cols

    edge_lane = lax.broadcasted_iota(jnp.int32, (window_rows, LANES), 1)
    keep_after = (edge_lane < rim) & (wide < wide_peers - 1)
    keep_before = (edge_lane >= LANES - rim) & (wide > 0)
    none = jnp.zeros((window_rows, LANES), jnp.bfloat16)
    after = jnp.where(odd, cross_ref[...], core_ref[...])
    before = jnp.where(odd, core_ref[...], cross_ref[...])

    place = lax.broadcasted_iota(jnp.int32, (out_rows, LANES), 0)
    row = row_base - half + place
    y_coord = (2 * row + 1).astype(jnp.float32) / band_rows - 1.0
    lane = lax.broadcasted_iota(jnp.int32, (8, total_cols), 1)
    column = wide * tile_cols + jnp.where(lane < tile_cols + LANES // 2, lane, lane - total_cols)
    x_coord = ((2 * column + 1).astype(jnp.float32) / band_cols - 1.0)[:1]
    in_band = (column >= 0) & (column < band_cols)
    weighting = []
    for member in range(members):
        inside = (row >= start_ref[member]) & (row < start_ref[member] + count_ref[member])
        weighting.append(jnp.where(inside, weight_ref[member], 0.0))
    denominator = functools.reduce(jnp.add, weighting)
    valid = (row >= 0) & (row < band_rows)
    inverse = jnp.where(valid, 1.0 / jnp.where(valid, denominator, 1.0), 0.0)
    sums = [jnp.zeros((out_rows, total_cols), jnp.float32) for _ in range(3)]

    def over_columns(array):
        return jnp.concatenate([array] * (total_cols // LANES), axis=1)

    for member in range(members):
        right = pltpu.roll(after, (LANES - 32 * member) % LANES, 1)
        left = pltpu.roll(before, (LANES + 96 - 32 * member) % LANES, 1)
        edge = jnp.where(keep_after, right, jnp.where(keep_before, left, none))
        window = jnp.concatenate([window_ref[member], edge], axis=1)
        upper = lax.broadcasted_iota(jnp.int32, (16, total_cols), 0) < 8
        last = jnp.zeros((16, total_cols), jnp.bfloat16)
        for tap in range(side):
            turned = pltpu.roll(window, (half - tap) % total_cols, 1)
            begin = tap * in_rows
            patches[member, begin : begin + 16, :] = jnp.where(upper, last, turned[:16])
            patches[member, begin + 16 : begin + in_rows, :] = turned[16:in_rows]
            last = turned[in_rows:]
        patches[member, side * in_rows :, :] = last
        response = jnp.dot(band_ref[...], patches[member], preferred_element_type=jnp.float32)
        scale = weighting[member] * inverse
        for kernel in range(kernel_total):
            coeffs = [coef_ref[member, kernel, order] for order in range(6)]
            own = response[kernel * out_rows : (kernel + 1) * out_rows]
            factors = (
                coeffs[0] + coeffs[2] * y_coord + coeffs[5] * (y_coord * y_coord),
                coeffs[1] + coeffs[4] * y_coord,
                coeffs[3],
            )
            sums = [
                value + over_columns(factor * scale) * own
                for value, factor in zip(sums, factors, strict=True)
            ]
    coadded = sums[0] + x_coord * (sums[1] + x_coord * sums[2])
    coadded = jnp.where(in_band[:1], coadded, 0.0)
    tall[...] = coadded
    coadd_ref[...] = tall[half : half + tile_rows, :tile_cols]
    filtered = taps_ref[0] * tall[:tile_rows, :]
    for tap in range(1, side):
        filtered = filtered + taps_ref[tap] * tall[tap : tap + tile_rows, :]
    detection = taps_ref[0] * pltpu.roll(filtered, half, 1)
    for tap in range(1, side):
        detection = detection + taps_ref[tap] * pltpu.roll(filtered, (half - tap) % total_cols, 1)
    detection_ref[...] = detection[:, :tile_cols]


def on_device(
    exposures, basis_kernels, poly_coef, exposure_weight, row_start, row_count, filter_taps
):
    members, tile_rows, tile_cols = exposures.shape
    side = basis_kernels.shape[1]
    half, out_rows, in_rows = sizes(tile_rows, side)
    peers, wide_peers = lax.axis_size("narrow"), lax.axis_size("wide")
    smem = pl.BlockSpec(memory_space=pltpu.SMEM)
    vmem = pl.BlockSpec(memory_space=pltpu.VMEM)

    def swapped(array, index):
        return lax.ppermute(array, "narrow", [(i, i ^ index) for i in range(peers)])

    tiles = [exposures] + [swapped(exposures, index) for index in range(1, peers)]
    band = band_matrix(basis_kernels, tile_rows)
    depth = band.shape[1]
    window_rows = 3 * tile_rows
    edge_shape = jax.ShapeDtypeStruct((window_rows, LANES), exposures.dtype)
    window_shape = jax.ShapeDtypeStruct((members, window_rows, tile_cols), exposures.dtype)
    window, to_core, to_cross = pl.pallas_call(
        functools.partial(place_kernel, peers),
        out_shape=(window_shape, edge_shape, edge_shape),
        in_specs=[smem] * 2 + [vmem] * peers,
        out_specs=[vmem] * 3,
        scratch_shapes=[pltpu.VMEM((peers, members, tile_rows, tile_cols), jnp.bfloat16)],
        compiler_params=pltpu.CompilerParams(vmem_limit_bytes=VMEM_BYTES),
        name="place",
    )(row_start, row_count, *tiles)
    core_pairs = [(i, i ^ 1) for i in range(wide_peers)]
    cross_pairs = [(i, ((i - 1) ^ 1) + 1) for i in range(1, wide_peers - 1)]
    cross_pairs += [(0, wide_peers - 1), (wide_peers - 1, 0)]
    from_core = lax.ppermute(to_core, "wide", core_pairs)
    from_cross = lax.ppermute(to_cross, "wide", cross_pairs)

    total_cols = tile_cols + LANES
    out = jax.ShapeDtypeStruct((tile_rows, tile_cols), jnp.float32)
    return pl.pallas_call(
        functools.partial(coadd_kernel, peers, wide_peers, side),
        out_shape=(out, out),
        in_specs=[smem] * 5 + [vmem] * 4,
        out_specs=(vmem, vmem),
        scratch_shapes=[
            pltpu.VMEM((members, depth, total_cols), jnp.bfloat16),
            pltpu.VMEM((out_rows, total_cols), jnp.float32),
        ],
        compiler_params=pltpu.CompilerParams(vmem_limit_bytes=VMEM_BYTES),
        name="coadd",
    )(
        poly_coef,
        exposure_weight,
        row_start,
        row_count,
        filter_taps,
        band,
        window,
        from_core,
        from_cross,
    )


def solution(mesh):
    placed = (P(None, "narrow", "wide"), P(), P(), P(), P(), P(), P())
    return jax.shard_map(
        on_device,
        mesh=mesh,
        in_specs=placed,
        out_specs=(P("narrow", "wide"), P("narrow", "wide")),
        check_vma=False,
    )
```

time: 27.8 us -> 23.6 us (0.85)
  Pallas kernels: 12.1 us -> 6.43 us
  waiting for transfers between devices: 1.59 us -> 6.77 us
  starting transfers between devices: 12.8 us -> 8.25 us
  local copies, waits for them, and re-layouts: 0.29 us -> 1.03 us
    ppermute x6 -> x3, waiting for transfers between devices: 0.02 us -> 5.78 us  [swapped(): return lax.ppermute(array, 'narrow', [(i, i ^ index) for i in range(peers)])]
    pallas_call x2, Pallas kernels: 7 us -> 1.32 us  [the longest x1 0.73 us: on_device(): pl.pallas_call(functools.partial(place_kernel, peers), out_shape=(window_...]
    ppermute x6 -> x3, starting transfers between devices: 8.83 us -> 5.68 us  [swapped(): return lax.ppermute(array, 'narrow', [(i, i ^ index) for i in range(peers)])]
    ppermute x1, starting transfers between devices: 3.56 us -> 2.5 us  [on_device(): from_cross = lax.ppermute(to_cross, 'wide', cross_pairs)]
    unnamed x16 -> x14, local copies, waits for them, and re-layouts: 0.17 us -> 0.91 us
    ppermute x1, waiting for transfers between devices: 1.57 us -> 0.99 us  [on_device(): from_cross = lax.ppermute(to_cross, 'wide', cross_pairs)]
    ppermute x1, starting transfers between devices: 0.45 us -> 0.07 us  [on_device(): from_core = lax.ppermute(to_core, 'wide', core_pairs)]
  transfers between devices with their start and end apart: 8 -> 5, of which waited for: 1 -> 3; matrix products, arithmetic and copies ran while one was open for 1% -> 5% of each run, Pallas kernels for 19% -> 3%
where the time goes in v2:
time: 23.6 us; the launch traced here: 23.3 us
  starting transfers between devices  8.25 us (35%)
  waiting for transfers between devices  6.77 us (29%)
  Pallas kernels  6.43 us (27%)
  local copies, waits for them, and re-layouts  1.03 us (4%)
  between operations  0.73 us (3%)
    ppermute x3, waiting for transfers between devices, swapped(): return lax.ppermute(array, 'narrow', [(i, i ^ index) for i in range(peers)])  5.78 us
    ppermute x3, starting transfers between devices, swapped(): return lax.ppermute(array, 'narrow', [(i, i ^ index) for i in range(peers)])  5.68 us
    pallas_call x1, Pallas kernels, on_device(): pl.pallas_call(functools.partial(coadd_kernel, peers, wide_peers, side),...  5.11 us
    ppermute x1, starting transfers between devices, on_device(): from_cross = lax.ppermute(to_cross, 'wide', cross_pairs)  2.5 us
    ppermute x1, waiting for transfers between devices, on_device(): from_cross = lax.ppermute(to_cross, 'wide', cross_pairs)  0.99 us
    unnamed x14, local copies, waits for them, and re-layouts  0.91 us
    pallas_call x1, Pallas kernels, on_device(): pl.pallas_call(functools.partial(place_kernel, peers), out_shape=(window_...  0.73 us
    pallas_call x1, Pallas kernels, band_matrix(): pl.pallas_call(functools.partial(band_matrix_kernel, out_rows), out_shape...  0.59 us
  transfers between devices with their start and end apart: 5, of which 3 were waited for; matrix products, arithmetic and copies ran while one was open for 5% of the time, Pallas kernels for 3%

profile of v2, /device:TPU:0, one launch (start us, length us, event | category | flops | bytes accessed | tf_op | source)
XLA Modules:
  0.0 23.3 jit_solution(8736251019869844536)
XLA Ops:
  0.6 0.0 copy-start
  0.6 4.1 %collective-permute-start.1 = (bf16[4,32,384]{2,1,0:T(8,128)(2,1)}, bf16[4,32,384]{2,1,0:T(8,128)(2,1)S(1)}, u32[]{:S(2)}, u32[]{:S(2)}) collective-permute-start(bf16[4,32,384]{2,1,0:T(8,128)(2,1)} %refs_0_.1), channel_id=1, source_target_pairs={{0,2},{1,3},{2,0},{3,1},{4,6},{5,7},{6,4},{7,5},{8,10},{9,11},{10,... | collective-permute-start | bytes 294920 | tf_op jit(solution)/shard_map/ppermute | solution.py:199
  4.7 1.6 %collective-permute-start = (bf16[4,32,384]{2,1,0:T(8,128)(2,1)}, bf16[4,32,384]{2,1,0:T(8,128)(2,1)S(1)}, u32[]{:S(2)}, u32[]{:S(2)}) collective-permute-start(bf16[4,32,384]{2,1,0:T(8,128)(2,1)} %refs_0_.1), channel_id=1, source_target_pairs={{0,1},{1,0},{2,3},{3,2},{4,5},{5,4},{6,7},{7,6},{8,9},{9,8},{10,11... | collective-permute-start | bytes 294920 | tf_op jit(solution)/shard_map/ppermute | solution.py:199
  6.3 0.0 collective-permute-start.2
  6.3 0.9 %copy.11 = bf16[5,21,21]{2,1,0:T(8,128)(2,1)S(1)} copy(bf16[5,21,21]{1,2,0:T(8,128)(2,1)} %bitcast.1) | data formatting | bytes 8820
  7.2 0.0 copy-start.1
  7.2 0.0 copy-start.2
  7.2 0.1 reshape.8
  7.3 3.6 %collective-permute-done.1.refs_2_ = bf16[4,32,384]{2,1,0:T(8,128)(2,1)S(1)} collective-permute-done((bf16[4,32,384]{2,1,0:T(8,128)(2,1)}, bf16[4,32,384]{2,1,0:T(8,128)(2,1)S(1)}, u32[]{:S(2)}, u32[]{:S(2)}) %collective-permute-start.1) | collective-permute-done | bytes 98336 | tf_op jit(solution)/shard_map/ppermute | solution.py:199
  10.9 0.0 collective-permute-done.refs_1_
  10.9 2.2 %collective-permute-done.2.refs_3_ = bf16[4,32,384]{2,1,0:T(8,128)(2,1)S(1)} collective-permute-done((bf16[4,32,384]{2,1,0:T(8,128)(2,1)}, bf16[4,32,384]{2,1,0:T(8,128)(2,1)S(1)}, u32[]{:S(2)}, u32[]{:S(2)}) %collective-permute-start.2) | collective-permute-done | bytes 98336 | tf_op jit(solution)/shard_map/ppermute | solution.py:199
  13.1 0.0 copy-done
  13.1 0.0 copy-done.1
  13.1 0.0 copy-done.2
  13.1 0.7 %place.1 = (bf16[4,96,384]{2,1,0:T(8,128)(2,1)S(1)}, bf16[96,128]{1,0:T(8,128)(2,1)S(1)}, bf16[96,128]{1,0:T(8,128)(2,1)S(1)}) custom-call(s32[4]{0:T(128)S(1)} %copy-done.1, s32[4]{0:T(128)S(1)} %copy-done.2, bf16[4,32,384]{2,1,0:T(8,128)(2,1)S(1)} %copy-done, bf16[4,32,384]{2,1,0:T(8,128)(2,1)S(1)} %collective-permute-done.refs_1_, ...), custom_call_target="tpu_custom_call" | custom-call | tf_op jit(solution)/shard_map/place/pallas_call | solution.py:207
  13.9 0.1 collective-permute-start.3
  13.9 0.0 copy-start.5
  14.0 2.5 %collective-permute-start.4 = (bf16[96,128]{1,0:T(8,128)(2,1)S(1)}, bf16[96,128]{1,0:T(8,128)(2,1)S(1)}, u32[]{:S(2)}, u32[]{:S(2)}) collective-permute-start(bf16[96,128]{1,0:T(8,128)(2,1)S(1)} %get-tuple-element.7), channel_id=1, source_target_pairs={{4,8},{8,4},{12,16},{16,12},{20,24},{24,20},{0,28},{28,0},{5,9},{9... | collective-permute-start | bytes 73736 | tf_op jit(solution)/shard_map/ppermute | solution.py:220
  16.5 0.1 pad_convert_fusion.base_ref
  16.5 0.0 copy-done.5
  16.6 0.6 %band_matrix.1.band_ref = bf16[280,1696]{1,0:T(8,128)(2,1)S(1)} custom-call(f32[5,1792]{1,0:T(8,128)S(1)} %pad_convert_fusion.base_ref), custom_call_target="tpu_custom_call" | custom-call | tf_op jit(solution)/shard_map/band_matrix/pallas_call | solution.py:45
  17.2 0.0 copy-start.3
  17.2 0.0 copy-start.4
  17.2 0.0 collective-permute-done.3.core_ref
  17.2 1.0 %collective-permute-done.4.cross_ref = bf16[96,128]{1,0:T(8,128)(2,1)S(1)} collective-permute-done((bf16[96,128]{1,0:T(8,128)(2,1)S(1)}, bf16[96,128]{1,0:T(8,128)(2,1)S(1)}, u32[]{:S(2)}, u32[]{:S(2)}) %collective-permute-start.4) | collective-permute-done | bytes 24608 | tf_op jit(solution)/shard_map/ppermute | solution.py:220
  18.2 0.0 copy-done.3
  18.2 0.0 copy-done.4
  18.2 5.1 %coadd.1 = (f32[32,384]{1,0:T(8,128)}, f32[32,384]{1,0:T(8,128)}) custom-call(f32[4,5,6]{2,1,0:T(8,128)S(1)} %copy.10.coef_ref, f32[4]{0:T(128)S(1)} %copy-done.3, s32[4]{0:T(128)S(1)} %copy-done.1, s32[4]{0:T(128)S(1)} %copy-done.2, f32[21]{0:T(128)S(1)} %copy-done.4, bf16[280,1696]{1,0:T(8,128)(2,1)S(1)} %band_matrix.1.band_ref, ...), custom_call_target="tpu_custom_call" | custom-call | tf_op jit(solution)/shard_map/coadd/pallas_call | solution.py:224
  (2 shorter events, 0.0 us)
Async XLA Ops:
  0.6 12.5 %copy-start = (bf16[4,32,384]{2,1,0:T(8,128)(2,1)S(1)}, bf16[4,32,384]{2,1,0:T(8,128)(2,1)}, u32[]{:S(2)}) copy-start(bf16[4,32,384]{2,1,0:T(8,128)(2,1)} %refs_0_.1) | copy-start | bytes 294916
  0.6 10.3 %collective-permute-start.1 = (bf16[4,32,384]{2,1,0:T(8,128)(2,1)}, bf16[4,32,384]{2,1,0:T(8,128)(2,1)S(1)}, u32[]{:S(2)}, u32[]{:S(2)}) collective-permute-start(bf16[4,32,384]{2,1,0:T(8,128)(2,1)} %refs_0_.1), channel_id=1, source_target_pairs={{0,2},{1,3},{2,0},{3,1},{4,6},{5,7},{6,4},{7,5},{8,10},{9,11},{10,... | collective-permute-start | bytes 294920 | tf_op jit(solution)/shard_map/ppermute | solution.py:199
  4.7 6.2 %collective-permute-start = (bf16[4,32,384]{2,1,0:T(8,128)(2,1)}, bf16[4,32,384]{2,1,0:T(8,128)(2,1)S(1)}, u32[]{:S(2)}, u32[]{:S(2)}) collective-permute-start(bf16[4,32,384]{2,1,0:T(8,128)(2,1)} %refs_0_.1), channel_id=1, source_target_pairs={{0,1},{1,0},{2,3},{3,2},{4,5},{5,4},{6,7},{7,6},{8,9},{9,8},{10,11... | collective-permute-start | bytes 294920 | tf_op jit(solution)/shard_map/ppermute | solution.py:199
  6.3 6.8 %collective-permute-start.2 = (bf16[4,32,384]{2,1,0:T(8,128)(2,1)}, bf16[4,32,384]{2,1,0:T(8,128)(2,1)S(1)}, u32[]{:S(2)}, u32[]{:S(2)}) collective-permute-start(bf16[4,32,384]{2,1,0:T(8,128)(2,1)} %refs_0_.1), channel_id=1, source_target_pairs={{0,3},{1,2},{2,1},{3,0},{4,7},{5,6},{6,5},{7,4},{8,11},{9,10},{10,... | collective-permute-start | bytes 294920 | tf_op jit(solution)/shard_map/ppermute | solution.py:199
  7.2 5.9 %copy-start.1 = (s32[4]{0:T(128)S(1)}, s32[4]{0:T(128)}, u32[]{:S(2)}) copy-start(s32[4]{0:T(128)} %start_ref.3) | copy-start | bytes 52
  7.2 5.9 %copy-start.2 = (s32[4]{0:T(128)S(1)}, s32[4]{0:T(128)}, u32[]{:S(2)}) copy-start(s32[4]{0:T(128)} %count_ref.3) | copy-start | bytes 52
  13.9 3.3 %collective-permute-start.3 = (bf16[96,128]{1,0:T(8,128)(2,1)S(1)}, bf16[96,128]{1,0:T(8,128)(2,1)S(1)}, u32[]{:S(2)}, u32[]{:S(2)}) collective-permute-start(bf16[96,128]{1,0:T(8,128)(2,1)S(1)} %get-tuple-element.6), channel_id=1, source_target_pairs={{0,4},{4,0},{8,12},{12,8},{16,20},{20,16},{24,28},{28,24},{1,5},{5... | collective-permute-start | bytes 73736 | tf_op jit(solution)/shard_map/ppermute | solution.py:219
  13.9 2.6 %copy-start.5 = (f32[4,5,6]{2,0,1:T(4,128)S(1)}, f32[4,5,6]{2,0,1:T(4,128)}, u32[]{:S(2)}) copy-start(f32[4,5,6]{2,0,1:T(4,128)} %param.9) | copy-start | bytes 1444
  14.0 4.2 %collective-permute-start.4 = (bf16[96,128]{1,0:T(8,128)(2,1)S(1)}, bf16[96,128]{1,0:T(8,128)(2,1)S(1)}, u32[]{:S(2)}, u32[]{:S(2)}) collective-permute-start(bf16[96,128]{1,0:T(8,128)(2,1)S(1)} %get-tuple-element.7), channel_id=1, source_target_pairs={{4,8},{8,4},{12,16},{16,12},{20,24},{24,20},{0,28},{28,0},{5,9},{9... | collective-permute-start | bytes 73736 | tf_op jit(solution)/shard_map/ppermute | solution.py:220
  17.2 1.0 %copy-start.3 = (f32[4]{0:T(128)S(1)}, f32[4]{0:T(128)}, u32[]{:S(2)}) copy-start(f32[4]{0:T(128)} %weight_ref.1) | copy-start | bytes 52
  17.2 1.0 %copy-start.4 = (f32[21]{0:T(128)S(1)}, f32[21]{0:T(128)}, u32[]{:S(2)}) copy-start(f32[21]{0:T(128)} %taps_ref.1) | copy-start | bytes 256

commit v3 on v2

v3 whole, which is shorter than its diff:
```python
import functools

import jax
import jax.numpy as jnp
from jax import lax
from jax.experimental import pallas as pl
from jax.experimental.pallas import tpu as pltpu
from jax.sharding import PartitionSpec as P

LANES = 128
VMEM_BYTES = 48 << 20


def rounded(value, unit):
    return -(-value // unit) * unit


def sizes(tile_rows, side):
    half = side // 2
    out_rows = rounded(tile_rows + 2 * half, 8)
    in_rows = rounded(tile_rows + 4 * half, 16)
    return half, out_rows, in_rows


def band_matrix_kernel(half, out_rows, in_rows, base_ref, band_ref):
    kernel_total, wide = base_ref.shape
    depth = band_ref.shape[1]
    place = lax.rem(lax.broadcasted_iota(jnp.int32, (8, wide), 1), in_rows)
    below = place < in_rows - 24
    parts = []
    for kernel in range(kernel_total):
        spread = jnp.broadcast_to(base_ref[kernel : kernel + 1, :], (8, wide))
        block = pltpu.roll(spread, 0, 1, stride=1, stride_axis=0)
        for first in range(0, out_rows, 8):
            shift = first - 2 * half
            plain = pltpu.roll(block, shift % wide, 1)
            wrapped = pltpu.roll(block, (shift + in_rows) % wide, 1)
            parts.append(jnp.where(below, plain, wrapped))
    band_ref[...] = jnp.concatenate(parts, axis=0).astype(jnp.bfloat16)[:, :depth]


def band_matrix(basis_kernels, tile_rows):
    kernel_total, side = basis_kernels.shape[:2]
    half, out_rows, in_rows = sizes(tile_rows, side)
    depth = side * in_rows
    wide = rounded(depth, LANES)
    base = basis_kernels.astype(jnp.float32).transpose(0, 2, 1)
    base = jnp.pad(base, ((0, 0), (0, 0), (0, in_rows - side))).reshape(kernel_total, depth)
    base = jnp.pad(base, ((0, 0), (0, wide - depth)))
    return pl.pallas_call(
        functools.partial(band_matrix_kernel, half, out_rows, in_rows),
        out_shape=jax.ShapeDtypeStruct((kernel_total * out_rows, depth), jnp.bfloat16),
        compiler_params=pltpu.CompilerParams(vmem_limit_bytes=VMEM_BYTES),
        cost_estimate=pl.CostEstimate(flops=10**9, bytes_accessed=10**6, transcendentals=0),
        name="band_matrix",
    )(base)


def place_kernel(sent, start_ref, count_ref, band_ref, *refs):
    peers = len(sent)
    tiles = refs[:peers][::-1]
    window_ref, core_ref, cross_ref, frame = refs[peers:]
    members, window_rows, tile_cols = window_ref.shape
    tile_rows = tiles[0].shape[1]
    narrow = lax.axis_index("narrow")
    odd = lax.rem(lax.axis_index("wide"), 2) == 1
    for index in range(peers):
        frame[jnp.bitwise_xor(narrow, index), sent[index] :] = tiles[index][...]
    lane = lax.broadcasted_iota(jnp.int32, (window_rows, LANES), 1)
    upper = lax.broadcasted_iota(jnp.int32, (16, tile_cols), 0) < 8
    leftward = jnp.zeros((window_rows, LANES), jnp.bfloat16)
    rightward = jnp.zeros((window_rows, LANES), jnp.bfloat16)
    for member in range(members):
        slot = narrow - start_ref[member] // tile_rows
        here = jnp.clip(slot, 0, peers - 1)
        above = jnp.clip(slot - 1, 0, peers - 1)
        below = jnp.clip(slot + 1, 0, peers - 1)
        window = jnp.concatenate(
            [
                frame[here, member],
                frame[below, member, :16],
                jnp.where(upper, frame[below, member, 16:], frame[above, member, :16]),
                frame[above, member, 16:],
            ]
        )
        place = lax.broadcasted_iota(jnp.int32, window.shape, 0)
        offset = jnp.where(place < window_rows - 24, place, place - window_rows)
        frame_row = offset + slot * tile_rows
        present = (frame_row >= 0) & (frame_row < count_ref[member])
        window = jnp.where(present, window, jnp.zeros((), window.dtype))
        window_ref[member] = window
        own = lane // 32 == member
        first = pltpu.roll(window[:, :LANES], 32 * member, 1)
        last = pltpu.roll(window[:, tile_cols - LANES :], (32 * member + 32) % LANES, 1)
        leftward = jnp.where(own, first, leftward)
        rightward = jnp.where(own, last, rightward)

    @pl.when(odd)
    def _():
        core_ref[...] = leftward
        cross_ref[...] = rightward

    @pl.when(jnp.logical_not(odd))
    def _():
        core_ref[...] = rightward
        cross_ref[...] = leftward


def row_factors(tile_rows, band_rows, half, out_rows, kernel_total, scalars):
    coef_ref, weight_ref, start_ref, count_ref = scalars
    members = weight_ref.shape[0]
    place = lax.broadcasted_iota(jnp.int32, (out_rows, LANES), 0)
    row = lax.axis_index("narrow") * tile_rows - half + place
    y_coord = (2 * row + 1).astype(jnp.float32) / band_rows - 1.0
    weighting = []
    for member in range(members):
        inside = (row >= start_ref[member]) & (row < start_ref[member] + count_ref[member])
        weighting.append(jnp.where(inside, weight_ref[member], 0.0))
    denominator = functools.reduce(jnp.add, weighting)
    valid = (row >= 0) & (row < band_rows)
    inverse = jnp.where(valid, 1.0 / jnp.where(valid, denominator, 1.0), 0.0)

    def factors(member, kernel):
        coeffs = [coef_ref[member, kernel, order] for order in range(6)]
        scale = weighting[member] * inverse
        return (
            (coeffs[0] + coeffs[2] * y_coord + coeffs[5] * (y_coord * y_coord)) * scale,
            (coeffs[1] + coeffs[4] * y_coord) * scale,
            coeffs[3] * scale,
        )

    return factors


def column_position(column, band_cols):
    return (2 * column + 1).astype(jnp.float32) / band_cols - 1.0


def main_kernel(
    peers, wide_peers, side, tile_rows, coef_ref, weight_ref, start_ref, count_ref, band_ref, window_ref, out_ref, patches
):
    members, in_rows, tile_cols = window_ref.shape
    half, out_rows, _ = sizes(tile_rows, side)
    kernel_total = band_ref.shape[0] // out_rows
    scalars = (coef_ref, weight_ref, start_ref, count_ref)
    factors = row_factors(tile_rows, peers * tile_rows, half, out_rows, kernel_total, scalars)
    sums = [jnp.zeros((out_rows, tile_cols), jnp.float32) for _ in range(3)]
    group = patches.shape[2] // tile_cols
    for begin in range(0, members, group):
        for member in range(begin, begin + group):
            window = window_ref[member]
            lanes = slice((member - begin) * tile_cols, (member - begin + 1) * tile_cols)
            for tap in range(side):
                patches[begin // group, tap * in_rows : (tap + 1) * in_rows, lanes] = pltpu.roll(
                    window, (half - tap) % tile_cols, 1
                )
        responses = jnp.dot(
            band_ref[...], patches[begin // group], preferred_element_type=jnp.float32
        )
        for member in range(begin, begin + group):
            response = responses[:, (member - begin) * tile_cols : (member - begin + 1) * tile_cols]
            for kernel in range(kernel_total):
                own = response[kernel * out_rows : (kernel + 1) * out_rows]
                sums = [
                    value + jnp.concatenate([factor] * (tile_cols // LANES), axis=1) * own
                    for value, factor in zip(sums, factors(member, kernel), strict=True)
                ]
    column = lax.axis_index("wide") * tile_cols + lax.broadcasted_iota(
        jnp.int32, (8, tile_cols), 1
    )
    x_coord = column_position(column, wide_peers * tile_cols)[:1]
    out_ref[...] = sums[0] + x_coord * (sums[1] + x_coord * sums[2])


def rim_kernel(
    peers,
    wide_peers,
    side,
    coef_ref,
    weight_ref,
    start_ref,
    count_ref,
    taps_ref,
    band_ref,
    inner_ref,
    to_core_ref,
    to_cross_ref,
    from_core_ref,
    from_cross_ref,
    coadd_ref,
    detection_ref,
    patches,
    tall,
):
    tile_rows, tile_cols = coadd_ref.shape
    in_rows = to_core_ref.shape[0]
    members = weight_ref.shape[0]
    half, out_rows, _ = sizes(tile_rows, side)
    rim = 2 * half
    kernel_total = band_ref.shape[0] // out_rows
    band_cols = wide_peers * tile_cols
    wide = lax.axis_index("wide")
    odd = lax.rem(wide, 2) == 1
    scalars = (coef_ref, weight_ref, start_ref, count_ref)
    factors = row_factors(tile_rows, peers * tile_rows, half, out_rows, kernel_total, scalars)

    none = jnp.zeros((in_rows, LANES), jnp.bfloat16)
    core, cross = from_core_ref[...], from_cross_ref[...]
    before = jnp.where(wide > 0, jnp.where(odd, core, cross), none)
    after = jnp.where(wide < wide_peers - 1, jnp.where(odd, cross, core), none)
    first = jnp.where(odd, to_core_ref[...], to_cross_ref[...])
    last = jnp.where(odd, to_cross_ref[...], to_core_ref[...])
    lane = lax.broadcasted_iota(jnp.int32, (in_rows, LANES), 1)
    zones = []
    for member in range(members):
        pieces = [
            pltpu.roll(piece, (target - 32 * member) % LANES, 1)
            for piece, target in ((before, -12), (first, rim), (last, 2 * rim - 12), (after, 3 * rim))
        ]
        zone = none
        for index in reversed(range(4)):
            zone = jnp.where(lane < (index + 1) * rim, pieces[index], zone)
        zones.append(zone)
    zones = jnp.concatenate(zones, axis=1)
    for tap in range(side):
        patches[tap * in_rows : (tap + 1) * in_rows, :] = pltpu.roll(
            zones, (half - tap) % zones.shape[1], 1
        )
    response = jnp.dot(band_ref[...], patches[...], preferred_element_type=jnp.float32)
    sums = [jnp.zeros((out_rows, LANES), jnp.float32) for _ in range(3)]
    for member in range(members):
        for kernel in range(kernel_total):
            own = response[
                kernel * out_rows : (kernel + 1) * out_rows, member * LANES : (member + 1) * LANES
            ]
            sums = [
                value + factor * own
                for value, factor in zip(sums, factors(member, kernel), strict=True)
            ]
    lane = lax.broadcasted_iota(jnp.int32, (out_rows, LANES), 1)
    column = wide * tile_cols + jnp.where(lane < 2 * rim, lane - rim, tile_cols - 3 * rim + lane)
    x_coord = column_position(column, band_cols)
    border = sums[0] + x_coord * (sums[1] + x_coord * sums[2])
    border = jnp.where((column >= 0) & (column < band_cols), border, 0.0)

    width = tile_cols + LANES
    head = pltpu.roll(border, LANES - rim, 1)
    tail = pltpu.roll(border, LANES - 3 * rim, 1)
    left = pltpu.roll(border, LANES - rim, 1)
    right = pltpu.roll(border, LANES - 3 * rim, 1)
    tall[:, :LANES] = jnp.where(lane < half, head, inner_ref[:, :LANES])
    tall[:, LANES : tile_cols - LANES] = inner_ref[:, LANES : tile_cols - LANES]
    tall[:, tile_cols - LANES : tile_cols] = jnp.where(
        lane >= LANES - half, tail, inner_ref[:, tile_cols - LANES :]
    )
    tall[:, tile_cols:] = jnp.where(lane < LANES // 2, right, left)
    coadd_ref[...] = tall[half : half + tile_rows, :tile_cols]
    filtered = taps_ref[0] * tall[:tile_rows, :]
    for tap in range(1, side):
        filtered = filtered + taps_ref[tap] * tall[tap : tap + tile_rows, :]
    detection = taps_ref[0] * pltpu.roll(filtered, half, 1)
    for tap in range(1, side):
        detection = detection + taps_ref[tap] * pltpu.roll(filtered, (half - tap) % width, 1)
    detection_ref[...] = detection[:, :tile_cols]


def on_device(
    exposures, basis_kernels, poly_coef, exposure_weight, row_start, row_count, filter_taps
):
    members, tile_rows, tile_cols = exposures.shape
    side = basis_kernels.shape[1]
    half, out_rows, in_rows = sizes(tile_rows, side)
    peers, wide_peers = lax.axis_size("narrow"), lax.axis_size("wide")
    smem = pl.BlockSpec(memory_space=pltpu.SMEM)
    vmem = pl.BlockSpec(memory_space=pltpu.VMEM)
    params = pltpu.CompilerParams(vmem_limit_bytes=VMEM_BYTES)

    def skipped(index):
        return 0 if any(abs(i - (i ^ index)) <= 1 for i in range(peers)) else 1

    sent = [skipped(index) for index in range(peers)]
    tiles = [exposures] * peers
    for index in reversed(range(1, peers)):
        pairs = [(i, i ^ index) for i in range(peers)]
        tiles[index] = lax.ppermute(exposures[sent[index] :], "narrow", pairs)
    band = band_matrix(basis_kernels, tile_rows)
    depth = band.shape[1]
    edge_shape = jax.ShapeDtypeStruct((in_rows, LANES), exposures.dtype)
    window_shape = jax.ShapeDtypeStruct((members, in_rows, tile_cols), exposures.dtype)
    window, to_core, to_cross = pl.pallas_call(
        functools.partial(place_kernel, sent),
        out_shape=(window_shape, edge_shape, edge_shape),
        in_specs=[smem] * 2 + [pl.BlockSpec(memory_space=pl.ANY)] + [vmem] * peers,
        out_specs=[vmem] * 3,
        scratch_shapes=[pltpu.VMEM((peers, members, tile_rows, tile_cols), jnp.bfloat16)],
        compiler_params=params,
        name="place",
    )(row_start, row_count, band, *reversed(tiles))
    core_pairs = [(i, i ^ 1) for i in range(wide_peers)]
    cross_pairs = [(i, ((i - 1) ^ 1) + 1) for i in range(1, wide_peers - 1)]
    cross_pairs += [(0, wide_peers - 1), (wide_peers - 1, 0)]
    from_core = lax.ppermute(to_core, "wide", core_pairs)
    from_cross = lax.ppermute(to_cross, "wide", cross_pairs)

    scalars = (poly_coef, exposure_weight, row_start, row_count)
    inner = pl.pallas_call(
        functools.partial(main_kernel, peers, wide_peers, side, tile_rows),
        out_shape=jax.ShapeDtypeStruct((out_rows, tile_cols), jnp.float32),
        in_specs=[smem] * 4 + [vmem] * 2,
        out_specs=vmem,
        scratch_shapes=[pltpu.VMEM((members // 2, depth, 2 * tile_cols), jnp.bfloat16)],
        compiler_params=params,
        cost_estimate=pl.CostEstimate(flops=2 * 10**9, bytes_accessed=10**6, transcendentals=0),
        name="main",
    )(*scalars, band, window)
    out = jax.ShapeDtypeStruct((tile_rows, tile_cols), jnp.float32)
    return pl.pallas_call(
        functools.partial(rim_kernel, peers, wide_peers, side),
        out_shape=(out, out),
        in_specs=[smem] * 5 + [vmem] * 6,
        out_specs=(vmem, vmem),
        scratch_shapes=[
            pltpu.VMEM((depth, members * LANES), jnp.bfloat16),
            pltpu.VMEM((out_rows, tile_cols + LANES), jnp.float32),
        ],
        compiler_params=params,
        name="rim",
    )(*scalars, filter_taps, band, inner, to_core, to_cross, from_core, from_cross)


def solution(mesh):
    placed = (P(None, "narrow", "wide"), P(), P(), P(), P(), P(), P())
    return jax.shard_map(
        on_device,
        mesh=mesh,
        in_specs=placed,
        out_specs=(P("narrow", "wide"), P("narrow", "wide")),
        check_vma=False,
    )
```

time: 23.6 us -> 22.8 us (0.966)
  waiting for transfers between devices: 6.77 us -> 3.33 us
  Pallas kernels: 6.43 us -> 8.13 us
  local copies, waits for them, and re-layouts: 1.03 us -> 1.91 us
    ppermute x3, waiting for transfers between devices: 5.78 us -> 3.32 us  [on_device(): tiles[index] = lax.ppermute(exposures[sent[index]:], 'narrow', pairs)]
    pallas_call x3 -> x4, Pallas kernels: 6.43 us -> 8.13 us  [the longest x1 3.32 us: on_device(): pl.pallas_call(functools.partial(main_kernel, peers, wide_peers, side, ti...]
    ppermute x1, waiting for transfers between devices: 0.99 us -> 0.01 us  [on_device(): from_cross = lax.ppermute(to_cross, 'wide', cross_pairs)]
    slice x0 -> x1, local copies, waits for them, and re-layouts: none -> 0.96 us  [on_device(): tiles[index] = lax.ppermute(exposures[sent[index]:], 'narrow', pairs)]
    unnamed x14 -> x16, local copies, waits for them, and re-layouts: 0.91 us -> 0.84 us
  transfers between devices with their start and end apart: 5 -> 5, of which waited for: 3 -> 1; matrix products, arithmetic and copies ran while one was open for 5% -> 5% of each run, Pallas kernels for 3% -> 19%
where the time goes in v3:
time: 22.8 us; the launch traced here: 22.6 us
  starting transfers between devices  8.42 us (37%)
  Pallas kernels  8.13 us (36%)
  waiting for transfers between devices  3.33 us (15%)
  local copies, waits for them, and re-layouts  1.91 us (8%)
  between operations  0.75 us (3%)
    ppermute x3, starting transfers between devices, on_device(): tiles[index] = lax.ppermute(exposures[sent[index]:], 'narrow', pairs)  5.73 us
    ppermute x3, waiting for transfers between devices, on_device(): tiles[index] = lax.ppermute(exposures[sent[index]:], 'narrow', pairs)  3.32 us
    pallas_call x1, Pallas kernels, on_device(): pl.pallas_call(functools.partial(main_kernel, peers, wide_peers, side, ti...  3.32 us
    pallas_call x1, Pallas kernels, on_device(): pl.pallas_call(functools.partial(rim_kernel, peers, wide_peers, side), ou...  3.17 us
    ppermute x1, starting transfers between devices, on_device(): from_cross = lax.ppermute(to_cross, 'wide', cross_pairs)  2.63 us
    slice x1, local copies, waits for them, and re-layouts, on_device(): tiles[index] = lax.ppermute(exposures[sent[index]:], 'narrow', pairs)  0.96 us
    pallas_call x1, Pallas kernels, band_matrix(): pl.pallas_call(functools.partial(band_matrix_kernel, half, out_rows, in_r...  0.93 us
    unnamed x16, local copies, waits for them, and re-layouts  0.84 us
  transfers between devices with their start and end apart: 5, of which 1 were waited for; matrix products, arithmetic and copies ran while one was open for 5% of the time, Pallas kernels for 19%

profile of v3, /device:TPU:0, one launch (start us, length us, event | category | flops | bytes accessed | tf_op | source)
XLA Modules:
  0.0 22.6 jit_solution(7188103375373081257)
XLA Ops:
  0.6 0.0 copy-start.5
  0.6 5.1 %collective-permute-start = (bf16[4,32,384]{2,1,0:T(8,128)(2,1)}, bf16[4,32,384]{2,1,0:T(8,128)(2,1)S(1)}, u32[]{:S(2)}, u32[]{:S(2)}) collective-permute-start(bf16[4,32,384]{2,1,0:T(8,128)(2,1)} %refs_3_.1), channel_id=1, source_target_pairs={{0,3},{1,2},{2,1},{3,0},{4,7},{5,6},{6,5},{7,4},{8,11},{9,10},{10,... | collective-permute-start | bytes 294920 | tf_op jit(solution)/shard_map/ppermute | solution.py:285
  5.8 0.0 collective-permute-start.2
  5.8 1.0 %slice.3 = bf16[3,32,384]{2,1,0:T(8,128)(2,1)S(1)} slice(bf16[4,32,384]{2,1,0:T(8,128)(2,1)} %refs_3_.1), slice={[1:4], [0:32], [0:384]} | slice | bytes 147456 | tf_op jit(solution)/shard_map/slice | solution.py:285
  6.7 0.6 %collective-permute-start.1 = (bf16[3,32,384]{2,1,0:T(8,128)(2,1)S(1)}, bf16[3,32,384]{2,1,0:T(8,128)(2,1)S(1)}, u32[]{:S(2)}, u32[]{:S(2)}) collective-permute-start(bf16[3,32,384]{2,1,0:T(8,128)(2,1)S(1)} %slice.3), channel_id=1, source_target_pairs={{0,2},{1,3},{2,0},{3,1},{4,6},{5,7},{6,4},{7,5},{8,10},{9,11},{10,... | collective-permute-start | bytes 221192 | tf_op jit(solution)/shard_map/ppermute | solution.py:285
  7.3 0.0 copy-done.5
  7.3 0.1 copy.12
  7.5 0.1 reshape.8
  7.6 0.0 copy-start.6
  7.6 0.7 %copy-done.6 = f32[4,5,6]{2,0,1:T(4,128)S(1)} copy-done((f32[4,5,6]{2,0,1:T(4,128)S(1)}, f32[4,5,6]{2,0,1:T(4,128)}, u32[]{:S(2)}) %copy-start.6) | copy-done | bytes 504
  8.3 0.0 copy-start
  8.3 0.0 copy-start.1
  8.3 0.0 copy-start.2
  8.3 0.9 %band_matrix.1.band_ref = bf16[280,1680]{1,0:T(8,128)(2,1)S(1)} custom-call(f32[5,1792]{1,0:T(8,128)S(1)} %pad_convert_fusion.base_ref), custom_call_target="tpu_custom_call" | custom-call | flops 1000000000 | bytes 1000000 | tf_op jit(solution)/shard_map/band_matrix/pallas_call | solution.py:50
  9.2 3.3 %collective-permute-done.1.refs_1_ = bf16[3,32,384]{2,1,0:T(8,128)(2,1)S(1)} collective-permute-done((bf16[3,32,384]{2,1,0:T(8,128)(2,1)S(1)}, bf16[3,32,384]{2,1,0:T(8,128)(2,1)S(1)}, u32[]{:S(2)}, u32[]{:S(2)}) %collective-permute-start.1) | collective-permute-done | bytes 73760 | tf_op jit(solution)/shard_map/ppermute | solution.py:285
  12.6 0.0 collective-permute-done.refs_0_
  12.6 0.0 collective-permute-done.2.refs_2_
  12.6 0.0 copy-done
  12.6 0.0 copy-done.1
  12.6 0.0 copy-done.2
  12.6 0.7 %place.1 = (bf16[4,80,384]{2,1,0:T(8,128)(2,1)S(1)}, bf16[80,128]{1,0:T(8,128)(2,1)S(1)}, bf16[80,128]{1,0:T(8,128)(2,1)S(1)}) custom-call(s32[4]{0:T(128)S(1)} %copy-done.1, s32[4]{0:T(128)S(1)} %copy-done.2, bf16[280,1680]{1,0:T(8,128)(2,1)S(1)} %band_matrix.1.band_ref, bf16[4,32,384]{2,1,0:T(8,128)(2,1)S(1)} %collective-permute-done.refs_0_, ...), custom_call_target="tpu_custom_call" | custom-call | tf_op jit(solution)/shard_map/place/pallas_call | solution.py:290
  13.3 0.1 collective-permute-start.3
  13.4 0.0 copy-start.3
  13.4 2.6 %collective-permute-start.4 = (bf16[80,128]{1,0:T(8,128)(2,1)S(1)}, bf16[80,128]{1,0:T(8,128)(2,1)S(1)}, u32[]{:S(2)}, u32[]{:S(2)}) collective-permute-start(bf16[80,128]{1,0:T(8,128)(2,1)S(1)} %get-tuple-element.7.to_cross_ref), channel_id=1, source_target_pairs={{4,8},{8,4},{12,16},{16,12},{20,24},{24,20},{0,28},{28,0},{5,9},{9... | collective-permute-start | bytes 61448 | tf_op jit(solution)/shard_map/ppermute | solution.py:303
  16.0 0.0 copy-done.3
  16.0 0.0 copy-start.4
  16.0 3.3 %main.1.inner_ref = f32[56,384]{1,0:T(8,128)S(1)} custom-call(f32[4,5,6]{2,1,0:T(8,128)S(1)} %copy.11.coef_ref, f32[4]{0:T(128)S(1)} %copy-done.3, s32[4]{0:T(128)S(1)} %copy-done.1, s32[4]{0:T(128)S(1)} %copy-done.2, bf16[280,1680]{1,0:T(8,128)(2,1)S(1)} %band_matrix.1.band_ref, bf16[4,80,384]{2,1,0:T(8,128)(2,1)S(1)} %get-tuple-element.5.window_ref), custom_call_target="tpu_custom_call" | custom-call | flops 2000000000 | bytes 1000000 | tf_op jit(solution)/shard_map/main/pallas_call | solution.py:306
  19.4 0.0 collective-permute-done.3.from_core_ref
  19.4 0.0 collective-permute-done.4.from_cross_ref
  19.4 0.0 copy-done.4
  19.4 3.2 %rim.1 = (f32[32,384]{1,0:T(8,128)}, f32[32,384]{1,0:T(8,128)}) custom-call(f32[4,5,6]{2,1,0:T(8,128)S(1)} %copy.11.coef_ref, f32[4]{0:T(128)S(1)} %copy-done.3, s32[4]{0:T(128)S(1)} %copy-done.1, s32[4]{0:T(128)S(1)} %copy-done.2, f32[21]{0:T(128)S(1)} %copy-done.4, bf16[280,1680]{1,0:T(8,128)(2,1)S(1)} %band_matrix.1.band_ref, ...), custom_call_target="tpu_custom_call" | custom-call | tf_op jit(solution)/shard_map/rim/pallas_call | solution.py:317
  (3 shorter events, 0.0 us)
Async XLA Ops:
  0.6 6.7 %copy-start.5 = (bf16[5,21,21]{2,1,0:T(8,128)(2,1)S(1)}, bf16[5,21,21]{2,1,0:T(8,128)(2,1)}, u32[]{:S(2)}) copy-start(bf16[5,21,21]{2,1,0:T(8,128)(2,1)} %param.8) | copy-start | bytes 13234
  0.6 11.9 %collective-permute-start = (bf16[4,32,384]{2,1,0:T(8,128)(2,1)}, bf16[4,32,384]{2,1,0:T(8,128)(2,1)S(1)}, u32[]{:S(2)}, u32[]{:S(2)}) collective-permute-start(bf16[4,32,384]{2,1,0:T(8,128)(2,1)} %refs_3_.1), channel_id=1, source_target_pairs={{0,3},{1,2},{2,1},{3,0},{4,7},{5,6},{6,5},{7,4},{8,11},{9,10},{10,... | collective-permute-start | bytes 294920 | tf_op jit(solution)/shard_map/ppermute | solution.py:285
  5.8 6.8 %collective-permute-start.2 = (bf16[4,32,384]{2,1,0:T(8,128)(2,1)}, bf16[4,32,384]{2,1,0:T(8,128)(2,1)S(1)}, u32[]{:S(2)}, u32[]{:S(2)}) collective-permute-start(bf16[4,32,384]{2,1,0:T(8,128)(2,1)} %refs_3_.1), channel_id=1, source_target_pairs={{0,1},{1,0},{2,3},{3,2},{4,5},{5,4},{6,7},{7,6},{8,9},{9,8},{10,11... | collective-permute-start | bytes 294920 | tf_op jit(solution)/shard_map/ppermute | solution.py:285
  6.7 5.8 %collective-permute-start.1 = (bf16[3,32,384]{2,1,0:T(8,128)(2,1)S(1)}, bf16[3,32,384]{2,1,0:T(8,128)(2,1)S(1)}, u32[]{:S(2)}, u32[]{:S(2)}) collective-permute-start(bf16[3,32,384]{2,1,0:T(8,128)(2,1)S(1)} %slice.3), channel_id=1, source_target_pairs={{0,2},{1,3},{2,0},{3,1},{4,6},{5,7},{6,4},{7,5},{8,10},{9,11},{10,... | collective-permute-start | bytes 221192 | tf_op jit(solution)/shard_map/ppermute | solution.py:285
  7.6 0.7 %copy-start.6 = (f32[4,5,6]{2,0,1:T(4,128)S(1)}, f32[4,5,6]{2,0,1:T(4,128)}, u32[]{:S(2)}) copy-start(f32[4,5,6]{2,0,1:T(4,128)} %param.9) | copy-start | bytes 1444
  8.3 4.3 %copy-start = (bf16[4,32,384]{2,1,0:T(8,128)(2,1)S(1)}, bf16[4,32,384]{2,1,0:T(8,128)(2,1)}, u32[]{:S(2)}) copy-start(bf16[4,32,384]{2,1,0:T(8,128)(2,1)} %refs_3_.1) | copy-start | bytes 294916
  8.3 4.3 %copy-start.1 = (s32[4]{0:T(128)S(1)}, s32[4]{0:T(128)}, u32[]{:S(2)}) copy-start(s32[4]{0:T(128)} %start_ref.5) | copy-start | bytes 52
  8.3 4.3 %copy-start.2 = (s32[4]{0:T(128)S(1)}, s32[4]{0:T(128)}, u32[]{:S(2)}) copy-start(s32[4]{0:T(128)} %count_ref.5) | copy-start | bytes 52
  13.3 6.1 %collective-permute-start.3 = (bf16[80,128]{1,0:T(8,128)(2,1)S(1)}, bf16[80,128]{1,0:T(8,128)(2,1)S(1)}, u32[]{:S(2)}, u32[]{:S(2)}) collective-permute-start(bf16[80,128]{1,0:T(8,128)(2,1)S(1)} %get-tuple-element.6.to_core_ref), channel_id=1, source_target_pairs={{0,4},{4,0},{8,12},{12,8},{16,20},{20,16},{24,28},{28,24},{1,5},{5... | collective-permute-start | bytes 61448 | tf_op jit(solution)/shard_map/ppermute | solution.py:302
  13.4 2.6 %copy-start.3 = (f32[4]{0:T(128)S(1)}, f32[4]{0:T(128)}, u32[]{:S(2)}) copy-start(f32[4]{0:T(128)} %weight_ref.3) | copy-start | bytes 52
  13.4 6.0 %collective-permute-start.4 = (bf16[80,128]{1,0:T(8,128)(2,1)S(1)}, bf16[80,128]{1,0:T(8,128)(2,1)S(1)}, u32[]{:S(2)}, u32[]{:S(2)}) collective-permute-start(bf16[80,128]{1,0:T(8,128)(2,1)S(1)} %get-tuple-element.7.to_cross_ref), channel_id=1, source_target_pairs={{4,8},{8,4},{12,16},{16,12},{20,24},{24,20},{0,28},{28,0},{5,9},{9... | collective-permute-start | bytes 61448 | tf_op jit(solution)/shard_map/ppermute | solution.py:303
  16.0 3.4 %copy-start.4 = (f32[21]{0:T(128)S(1)}, f32[21]{0:T(128)}, u32[]{:S(2)}) copy-start(f32[21]{0:T(128)} %taps_ref.1) | copy-start | bytes 256

commit v4 on v3

v4 whole, which is shorter than its diff:
```python
import functools

import jax
import jax.numpy as jnp
from jax import lax
from jax.experimental import pallas as pl
from jax.experimental.pallas import tpu as pltpu
from jax.sharding import PartitionSpec as P

LANES = 128
VMEM_BYTES = 48 << 20


def rounded(value, unit):
    return -(-value // unit) * unit


def sizes(tile_rows, side):
    half = side // 2
    out_rows = rounded(tile_rows + 2 * half, 8)
    in_rows = rounded(tile_rows + 4 * half, 16)
    return half, out_rows, in_rows


UPPER = 24
PART = 48


def band_matrix(half, begin, base, band_ref):
    kernel_total, wide = len(base), base[0].shape[1]
    rows, depth = band_ref.shape
    place = lax.rem(lax.broadcasted_iota(jnp.int32, (8, wide), 1), PART)
    lead = begin - 2 * half
    parts = []
    for kernel in range(kernel_total):
        spread = jnp.broadcast_to(base[kernel], (8, wide))
        block = pltpu.roll(spread, 0, 1, stride=1, stride_axis=0)
        for first in range(0, rows // kernel_total, 8):
            shift = first + lead
            plain = pltpu.roll(block, shift % wide, 1)
            wrapped = pltpu.roll(block, (shift + (PART if lead < 0 else -PART)) % wide, 1)
            if lead < 0:
                parts.append(jnp.where(place < PART + lead - 4, plain, wrapped))
            else:
                parts.append(jnp.where(place < lead, wrapped, plain))
    band_ref[...] = jnp.concatenate(parts, axis=0).astype(jnp.bfloat16)[:, :depth]


def factors_kernel(
    tile_rows, band_rows, half, coef_ref, weight_ref, start_ref, count_ref, after_ref, factor_ref
):
    kernel_total, members = coef_ref.shape[:2]
    out_rows = factor_ref.shape[1]
    place = lax.broadcasted_iota(jnp.int32, (out_rows, LANES), 0)
    row = lax.axis_index("narrow") * tile_rows - half + place
    y_coord = (2 * row + 1).astype(jnp.float32) / band_rows - 1.0
    weighting = []
    for member in range(members):
        inside = (row >= start_ref[member]) & (row < start_ref[member] + count_ref[member])
        weighting.append(jnp.where(inside, weight_ref[member], 0.0))
    denominator = functools.reduce(jnp.add, weighting)
    valid = (row >= 0) & (row < band_rows)
    inverse = jnp.where(valid, 1.0 / jnp.where(valid, denominator, 1.0), 0.0)
    for member in range(members):
        scale = weighting[member] * inverse
        for kernel in range(kernel_total):
            coeffs = [coef_ref[kernel, member, order] for order in range(6)]
            constant = coeffs[0] + coeffs[2] * y_coord + coeffs[5] * (y_coord * y_coord)
            index = 3 * (member * kernel_total + kernel)
            factor_ref[index] = constant * scale
            factor_ref[index + 1] = (coeffs[1] + coeffs[4] * y_coord) * scale
            factor_ref[index + 2] = coeffs[3] * scale


def spread_taps(basis_ref, square):
    kernel_total, side = basis_ref.shape[:2]
    rows = square.shape[0] // kernel_total
    wide = rounded(side * PART, LANES)
    square[...] = jnp.zeros_like(square)
    for kernel in range(kernel_total):
        square[kernel * rows : kernel * rows + side, :side] = basis_ref[kernel].astype(jnp.float32)
    across = lax.broadcasted_iota(jnp.int32, (LANES, wide), 0)
    begin = across * PART
    lane = lax.broadcasted_iota(jnp.int32, (LANES, wide), 1)
    onehot = jnp.where((lane >= begin) & (lane < begin + PART), 1.0, 0.0).astype(jnp.bfloat16)
    repeated = jnp.dot(
        square[...].astype(jnp.bfloat16), onehot, preferred_element_type=jnp.float32
    )
    down = lax.broadcasted_iota(jnp.int32, (rows, wide), 0)
    chosen = lax.rem(lax.broadcasted_iota(jnp.int32, (rows, wide), 1), PART) == down
    return [
        jnp.sum(
            jnp.where(chosen, repeated[kernel * rows : (kernel + 1) * rows], 0.0),
            axis=0,
            keepdims=True,
        )
        for kernel in range(kernel_total)
    ]


def bands_kernel(half, basis_ref, upper_ref, lower_ref, square):
    base = spread_taps(basis_ref, square)
    band_matrix(half, 0, base, upper_ref)
    band_matrix(half, UPPER, base, lower_ref)


def prepared(basis_kernels, poly_coef, weight, start, count, tile_rows):
    kernel_total, side = basis_kernels.shape[:2]
    members = poly_coef.shape[0]
    half, out_rows, _ = sizes(tile_rows, side)
    depth = side * PART
    smem = pl.BlockSpec(memory_space=pltpu.SMEM)
    vmem = pl.BlockSpec(memory_space=pltpu.VMEM)
    params = pltpu.CompilerParams(vmem_limit_bytes=VMEM_BYTES)
    band_rows = lax.axis_size("narrow") * tile_rows
    upper, lower = pl.pallas_call(
        functools.partial(bands_kernel, half),
        out_shape=(
            jax.ShapeDtypeStruct((kernel_total * UPPER, depth), jnp.bfloat16),
            jax.ShapeDtypeStruct((kernel_total * (out_rows - UPPER), depth), jnp.bfloat16),
        ),
        in_specs=[vmem],
        out_specs=(vmem, vmem),
        scratch_shapes=[pltpu.VMEM((kernel_total * rounded(side, 8), LANES), jnp.float32)],
        compiler_params=params,
        cost_estimate=pl.CostEstimate(flops=10**9, bytes_accessed=10**6, transcendentals=0),
        name="bands",
    )(basis_kernels)
    factors = pl.pallas_call(
        functools.partial(factors_kernel, tile_rows, band_rows, half),
        out_shape=jax.ShapeDtypeStruct((3 * members * kernel_total, out_rows, LANES), jnp.float32),
        in_specs=[smem] * 4 + [pl.BlockSpec(memory_space=pl.ANY)],
        out_specs=vmem,
        compiler_params=params,
        cost_estimate=pl.CostEstimate(flops=10**8, bytes_accessed=10**6, transcendentals=0),
        name="factors",
    )(poly_coef.transpose(1, 0, 2), weight, start, count, upper)
    return factors, upper, lower


def part_rows_of(moved):
    first, second, below, mixed, above = [moved[row : row + 16] for row in range(0, 80, 16)]
    place = lax.broadcasted_iota(jnp.int32, first.shape, 0)
    return (
        (first, jnp.where(place < 8, second, mixed), above),
        (jnp.where(place < 4, mixed, first), second, below),
    )


def fill_patches(window, half, side, patch_refs, lanes):
    width = window.shape[1]
    for tap in range(side):
        moved = pltpu.roll(window, (half - tap) % width, 1)
        for patch_ref, rows in zip(patch_refs, part_rows_of(moved), strict=True):
            for index, piece in enumerate(rows):
                begin = tap * PART + 16 * index
                patch_ref[begin : begin + 16, lanes] = piece


def products(band_refs, patch_refs):
    return [
        jnp.dot(band_ref[...], patch_ref[...], preferred_element_type=jnp.float32)
        for band_ref, patch_ref in zip(band_refs, patch_refs, strict=True)
    ]


def response_of(parts, kernel, kernel_total, lanes):
    pieces = []
    for part in parts:
        rows = part.shape[0] // kernel_total
        pieces.append(part[kernel * rows : (kernel + 1) * rows, lanes])
    return jnp.concatenate(pieces, axis=0)


def place_kernel(sent, start_ref, count_ref, *refs):
    peers = len(sent)
    tiles = refs[:peers][::-1]
    window_ref, core_ref, cross_ref, frame = refs[peers:]
    members, window_rows, tile_cols = window_ref.shape
    tile_rows = tiles[0].shape[1]
    narrow = lax.axis_index("narrow")
    odd = lax.rem(lax.axis_index("wide"), 2) == 1
    for index in range(peers):
        frame[jnp.bitwise_xor(narrow, index), sent[index] :] = tiles[index][...]
    lane = lax.broadcasted_iota(jnp.int32, (window_rows, LANES), 1)
    upper = lax.broadcasted_iota(jnp.int32, (16, tile_cols), 0) < 8
    leftward = jnp.zeros((window_rows, LANES), jnp.bfloat16)
    rightward = jnp.zeros((window_rows, LANES), jnp.bfloat16)
    for member in range(members):
        slot = narrow - start_ref[member] // tile_rows
        here = jnp.clip(slot, 0, peers - 1)
        above = jnp.clip(slot - 1, 0, peers - 1)
        below = jnp.clip(slot + 1, 0, peers - 1)
        window = jnp.concatenate(
            [
                frame[here, member],
                frame[below, member, :16],
                jnp.where(upper, frame[below, member, 16:], frame[above, member, :16]),
                frame[above, member, 16:],
            ]
        )
        place = lax.broadcasted_iota(jnp.int32, window.shape, 0)
        offset = jnp.where(place < window_rows - 24, place, place - window_rows)
        frame_row = offset + slot * tile_rows
        present = (frame_row >= 0) & (frame_row < count_ref[member])
        window = jnp.where(present, window, jnp.zeros((), window.dtype))
        window_ref[member] = window
        own = lane // 32 == member
        first = pltpu.roll(window[:, :LANES], 32 * member, 1)
        last = pltpu.roll(window[:, tile_cols - LANES :], (32 * member + 32) % LANES, 1)
        leftward = jnp.where(own, first, leftward)
        rightward = jnp.where(own, last, rightward)

    @pl.when(odd)
    def _():
        core_ref[...] = leftward
        cross_ref[...] = rightward

    @pl.when(jnp.logical_not(odd))
    def _():
        core_ref[...] = rightward
        cross_ref[...] = leftward


def column_position(column, band_cols):
    return (2 * column + 1).astype(jnp.float32) / band_cols - 1.0


def main_kernel(
    wide_peers,
    side,
    tile_rows,
    factor_ref,
    upper_ref,
    lower_ref,
    window_ref,
    out_ref,
    upper_patches,
    lower_patches,
):
    members, in_rows, tile_cols = window_ref.shape
    half, out_rows, _ = sizes(tile_rows, side)
    kernel_total = upper_ref.shape[0] // UPPER
    sums = [jnp.zeros((out_rows, tile_cols), jnp.float32) for _ in range(3)]
    group = upper_patches.shape[2] // tile_cols
    for begin in range(0, members, group):
        patch_refs = upper_patches.at[begin // group], lower_patches.at[begin // group]
        strips = [slice(index * tile_cols, (index + 1) * tile_cols) for index in range(group)]
        for index, lanes in enumerate(strips):
            fill_patches(window_ref[begin + index], half, side, patch_refs, lanes)
        parts = products((upper_ref, lower_ref), patch_refs)
        for index, lanes in enumerate(strips):
            for kernel in range(kernel_total):
                own = response_of(parts, kernel, kernel_total, lanes)
                place = 3 * ((begin + index) * kernel_total + kernel)
                for order in range(3):
                    factor = [factor_ref[place + order]] * (tile_cols // LANES)
                    sums[order] = sums[order] + jnp.concatenate(factor, axis=1) * own
    column = lax.axis_index("wide") * tile_cols + lax.broadcasted_iota(
        jnp.int32, (8, tile_cols), 1
    )
    x_coord = column_position(column, wide_peers * tile_cols)[:1]
    out_ref[...] = sums[0] + x_coord * (sums[1] + x_coord * sums[2])


def rim_kernel(
    wide_peers,
    side,
    members,
    taps_ref,
    factor_ref,
    upper_ref,
    lower_ref,
    inner_ref,
    to_core_ref,
    to_cross_ref,
    from_core_ref,
    from_cross_ref,
    coadd_ref,
    detection_ref,
    upper_patches,
    lower_patches,
    tall,
):
    tile_rows, tile_cols = coadd_ref.shape
    in_rows = to_core_ref.shape[0]
    half, out_rows, _ = sizes(tile_rows, side)
    rim = 2 * half
    kernel_total = upper_ref.shape[0] // UPPER
    band_cols = wide_peers * tile_cols
    wide = lax.axis_index("wide")
    odd = lax.rem(wide, 2) == 1

    none = jnp.zeros((in_rows, LANES), jnp.bfloat16)
    core, cross = from_core_ref[...], from_cross_ref[...]
    before = jnp.where(wide > 0, jnp.where(odd, core, cross), none)
    after = jnp.where(wide < wide_peers - 1, jnp.where(odd, cross, core), none)
    first = jnp.where(odd, to_core_ref[...], to_cross_ref[...])
    last = jnp.where(odd, to_cross_ref[...], to_core_ref[...])
    lane = lax.broadcasted_iota(jnp.int32, (in_rows, LANES), 1)
    zones = []
    for member in range(members):
        pieces = [
            pltpu.roll(piece, (target - 32 * member) % LANES, 1)
            for piece, target in ((before, -12), (first, rim), (last, 2 * rim - 12), (after, 3 * rim))
        ]
        zone = none
        for index in reversed(range(4)):
            zone = jnp.where(lane < (index + 1) * rim, pieces[index], zone)
        zones.append(zone)
    zones = jnp.concatenate(zones, axis=1)
    patch_refs = upper_patches, lower_patches
    fill_patches(zones, half, side, patch_refs, slice(0, members * LANES))
    parts = products((upper_ref, lower_ref), patch_refs)
    sums = [jnp.zeros((out_rows, LANES), jnp.float32) for _ in range(3)]
    for member in range(members):
        for kernel in range(kernel_total):
            lanes = slice(member * LANES, (member + 1) * LANES)
            own = response_of(parts, kernel, kernel_total, lanes)
            place = 3 * (member * kernel_total + kernel)
            for order in range(3):
                sums[order] = sums[order] + factor_ref[place + order] * own
    lane = lax.broadcasted_iota(jnp.int32, (out_rows, LANES), 1)
    column = wide * tile_cols + jnp.where(lane < 2 * rim, lane - rim, tile_cols - 3 * rim + lane)
    x_coord = column_position(column, band_cols)
    border = sums[0] + x_coord * (sums[1] + x_coord * sums[2])
    border = jnp.where((column >= 0) & (column < band_cols), border, 0.0)

    width = tile_cols + LANES
    head = pltpu.roll(border, LANES - rim, 1)
    tail = pltpu.roll(border, LANES - 3 * rim, 1)
    left = pltpu.roll(border, LANES - rim, 1)
    right = pltpu.roll(border, LANES - 3 * rim, 1)
    tall[:, :LANES] = jnp.where(lane < half, head, inner_ref[:, :LANES])
    tall[:, LANES : tile_cols - LANES] = inner_ref[:, LANES : tile_cols - LANES]
    tall[:, tile_cols - LANES : tile_cols] = jnp.where(
        lane >= LANES - half, tail, inner_ref[:, tile_cols - LANES :]
    )
    tall[:, tile_cols:] = jnp.where(lane < LANES // 2, right, left)
    coadd_ref[...] = tall[half : half + tile_rows, :tile_cols]
    filtered = taps_ref[0] * tall[:tile_rows, :]
    for tap in range(1, side):
        filtered = filtered + taps_ref[tap] * tall[tap : tap + tile_rows, :]
    detection = taps_ref[0] * pltpu.roll(filtered, half, 1)
    for tap in range(1, side):
        detection = detection + taps_ref[tap] * pltpu.roll(filtered, (half - tap) % width, 1)
    detection_ref[...] = detection[:, :tile_cols]


def on_device(
    exposures, basis_kernels, poly_coef, exposure_weight, row_start, row_count, filter_taps
):
    members, tile_rows, tile_cols = exposures.shape
    side = basis_kernels.shape[1]
    half, out_rows, in_rows = sizes(tile_rows, side)
    peers, wide_peers = lax.axis_size("narrow"), lax.axis_size("wide")
    smem = pl.BlockSpec(memory_space=pltpu.SMEM)
    vmem = pl.BlockSpec(memory_space=pltpu.VMEM)
    params = pltpu.CompilerParams(vmem_limit_bytes=VMEM_BYTES)

    def skipped(index):
        return 0 if any(abs(i - (i ^ index)) <= 1 for i in range(peers)) else 1

    sent = [skipped(index) for index in range(peers)]
    tiles = [exposures] * peers
    moving, latter = lax.optimization_barrier((exposures, exposures[1:]))
    for index in reversed(range(1, peers)):
        pairs = [(i, i ^ index) for i in range(peers)]
        whole = moving if index == 1 else exposures
        tiles[index] = lax.ppermute(latter if sent[index] else whole, "narrow", pairs)
    tables = prepared(
        basis_kernels, poly_coef, exposure_weight, row_start, row_count, tile_rows
    )
    depth = side * PART
    edge_shape = jax.ShapeDtypeStruct((in_rows, LANES), exposures.dtype)
    window_shape = jax.ShapeDtypeStruct((members, in_rows, tile_cols), exposures.dtype)
    window, to_core, to_cross = pl.pallas_call(
        functools.partial(place_kernel, sent),
        out_shape=(window_shape, edge_shape, edge_shape),
        in_specs=[smem] * 2 + [vmem] * peers,
        out_specs=[vmem] * 3,
        scratch_shapes=[pltpu.VMEM((peers, members, tile_rows, tile_cols), jnp.bfloat16)],
        compiler_params=params,
        name="place",
    )(row_start, row_count, *reversed(tiles))
    core_pairs = [(i, i ^ 1) for i in range(wide_peers)]
    cross_pairs = [(i, ((i - 1) ^ 1) + 1) for i in range(1, wide_peers - 1)]
    cross_pairs += [(0, wide_peers - 1), (wide_peers - 1, 0)]
    from_core = lax.ppermute(to_core, "wide", core_pairs)
    from_cross = lax.ppermute(to_cross, "wide", cross_pairs)

    inner = pl.pallas_call(
        functools.partial(main_kernel, wide_peers, side, tile_rows),
        out_shape=jax.ShapeDtypeStruct((out_rows, tile_cols), jnp.float32),
        in_specs=[vmem] * 4,
        out_specs=vmem,
        scratch_shapes=[pltpu.VMEM((members // 2, depth, 2 * tile_cols), jnp.bfloat16)] * 2,
        compiler_params=params,
        cost_estimate=pl.CostEstimate(flops=2 * 10**9, bytes_accessed=10**6, transcendentals=0),
        name="main",
    )(*tables, window)
    out = jax.ShapeDtypeStruct((tile_rows, tile_cols), jnp.float32)
    return pl.pallas_call(
        functools.partial(rim_kernel, wide_peers, side, members),
        out_shape=(out, out),
        in_specs=[smem] + [vmem] * 8,
        out_specs=(vmem, vmem),
        scratch_shapes=[
            pltpu.VMEM((depth, members * LANES), jnp.bfloat16),
            pltpu.VMEM((depth, members * LANES), jnp.bfloat16),
            pltpu.VMEM((out_rows, tile_cols + LANES), jnp.float32),
        ],
        compiler_params=params,
        name="rim",
    )(filter_taps, *tables, inner, to_core, to_cross, from_core, from_cross)


def solution(mesh):
    placed = (P(None, "narrow", "wide"), P(), P(), P(), P(), P(), P())
    return jax.shard_map(
        on_device,
        mesh=mesh,
        in_specs=placed,
        out_specs=(P("narrow", "wide"), P("narrow", "wide")),
        check_vma=False,
    )
```

time: 22.8 us -> 21.7 us (0.952)
  Pallas kernels: 8.13 us -> 7.31 us
    pallas_call x3 -> x4, Pallas kernels: 7.42 us -> 6.59 us  [the longest x1 2.82 us: on_device(): pl.pallas_call(functools.partial(rim_kernel, wide_peers, side, members),...]
    unnamed x16 -> x14, local copies, waits for them, and re-layouts: 0.84 us -> 0.78 us
  transfers between devices with their start and end apart: 5 -> 5, of which waited for: 1 -> 1; matrix products, arithmetic and copies ran while one was open for 5% -> 4% of each run, Pallas kernels for 19% -> 18%
where the time goes in v4:
time: 21.7 us; the launch traced here: 21.5 us
  starting transfers between devices  8.36 us (39%)
  Pallas kernels  7.31 us (34%)
  waiting for transfers between devices  3.35 us (15%)
  local copies, waits for them, and re-layouts  1.71 us (8%)
  between operations  0.77 us (4%)
    ppermute x3, starting transfers between devices, on_device(): lax.ppermute(latter if sent[index] else whole, 'narrow', pairs)  5.74 us
    ppermute x3, waiting for transfers between devices, on_device(): lax.ppermute(latter if sent[index] else whole, 'narrow', pairs)  3.35 us
    pallas_call x1, Pallas kernels, on_device(): pl.pallas_call(functools.partial(rim_kernel, wide_peers, side, members),...  2.82 us
    ppermute x1, starting transfers between devices, on_device(): from_cross = lax.ppermute(to_cross, 'wide', cross_pairs)  2.55 us
    pallas_call x1, Pallas kernels, on_device(): pl.pallas_call(functools.partial(main_kernel, wide_peers, side, tile_rows...  2.12 us
    pallas_call x1, Pallas kernels, prepared(): pl.pallas_call(functools.partial(factors_kernel, tile_rows, band_rows, ha...  0.98 us
    slice x1, local copies, waits for them, and re-layouts, on_device(): moving, latter = lax.optimization_barrier((exposures, exposures[1:]))  0.93 us
    unnamed x14, local copies, waits for them, and re-layouts  0.78 us
  transfers between devices with their start and end apart: 5, of which 1 were waited for; matrix products, arithmetic and copies ran while one was open for 4% of the time, Pallas kernels for 18%

profile of v4, /device:TPU:0, one launch (start us, length us, event | category | flops | bytes accessed | tf_op | source)
XLA Modules:
  0.0 21.5 jit_solution(5955553635488971505)
XLA Ops:
  0.6 5.1 %collective-permute-start = (bf16[4,32,384]{2,1,0:T(8,128)(2,1)}, bf16[4,32,384]{2,1,0:T(8,128)(2,1)S(1)}, u32[]{:S(2)}, u32[]{:S(2)}) collective-permute-start(bf16[4,32,384]{2,1,0:T(8,128)(2,1)} %refs_3_.1), channel_id=1, source_target_pairs={{0,3},{1,2},{2,1},{3,0},{4,7},{5,6},{6,5},{7,4},{8,11},{9,10},{10,... | collective-permute-start | bytes 294920 | tf_op jit(solution)/shard_map/ppermute | solution.py:370
  5.7 0.9 %slice.3 = bf16[3,32,384]{2,1,0:T(8,128)(2,1)S(1)} slice(bf16[4,32,384]{2,1,0:T(8,128)(2,1)} %refs_3_.1), slice={[1:4], [0:32], [0:384]} | slice | bytes 147456 | tf_op jit(solution)/shard_map/slice | solution.py:366
  6.7 0.0 copy-start.1
  6.7 0.0 copy-start.2
  6.7 0.0 copy-start.3
  6.7 0.0 copy-start.4
  6.7 0.1 collective-permute-start.1
  6.8 0.6 %collective-permute-start.2 = (bf16[4,32,384]{2,1,0:T(8,128)(2,1)}, bf16[4,32,384]{2,1,0:T(8,128)(2,1)S(1)}, u32[]{:S(2)}, u32[]{:S(2)}) collective-permute-start(bf16[4,32,384]{2,1,0:T(8,128)(2,1)} %refs_3_.1), channel_id=1, source_target_pairs={{0,1},{1,0},{2,3},{3,2},{4,5},{5,4},{6,7},{7,6},{8,9},{9,8},{10,11... | collective-permute-start | bytes 294920 | tf_op jit(solution)/shard_map/ppermute | solution.py:370
  7.4 0.0 copy-start.6
  7.4 0.8 %copy-done.6 = bf16[5,21,21]{2,1,0:T(8,128)(2,1)S(1)} copy-done((bf16[5,21,21]{2,1,0:T(8,128)(2,1)S(1)}, bf16[5,21,21]{2,1,0:T(8,128)(2,1)}, u32[]{:S(2)}) %copy-start.6) | copy-done | bytes 4434
  8.1 0.7 %bands.1 = (bf16[120,1008]{1,0:T(8,128)(2,1)S(1)}, bf16[160,1008]{1,0:T(8,128)(2,1)S(1)}) custom-call(bf16[5,21,21]{2,1,0:T(8,128)(2,1)S(1)} %copy-done.6), custom_call_target="tpu_custom_call" | custom-call | flops 1000000000 | bytes 1000000 | tf_op jit(solution)/shard_map/bands/pallas_call | solution.py:116
  8.8 0.0 copy-start
  8.8 0.0 copy-done.1
  8.8 0.0 copy-done.2
  8.8 0.0 copy-done.3
  8.8 0.0 copy-done.4
  8.8 1.0 %factors.1.factor_ref = f32[60,56,128]{2,1,0:T(8,128)S(1)} custom-call(f32[5,4,6]{2,1,0:T(4,128)S(1)} %bitcast.1, f32[4]{0:T(128)S(1)} %copy-done.4, s32[4]{0:T(128)S(1)} %copy-done.2, s32[4]{0:T(128)S(1)} %copy-done.3, bf16[120,1008]{1,0:T(8,128)(2,1)S(1)} %get-tuple-element.9.after_ref.upper_ref), custom_call_target="tpu_custom_call" | custom-call | flops 100000000 | bytes 1000000 | tf_op jit(solution)/shard_map/factors/pallas_call | solution.py:129
  9.8 3.3 %collective-permute-done.1.refs_1_ = bf16[3,32,384]{2,1,0:T(8,128)(2,1)S(1)} collective-permute-done((bf16[3,32,384]{2,1,0:T(8,128)(2,1)S(1)}, bf16[3,32,384]{2,1,0:T(8,128)(2,1)S(1)}, u32[]{:S(2)}, u32[]{:S(2)}) %collective-permute-start.1) | collective-permute-done | bytes 73760 | tf_op jit(solution)/shard_map/ppermute | solution.py:370
  13.2 0.0 collective-permute-done.2.refs_2_
  13.2 0.0 collective-permute-done.refs_0_
  13.2 0.0 copy-done
  13.2 0.7 %place.1 = (bf16[4,80,384]{2,1,0:T(8,128)(2,1)S(1)}, bf16[80,128]{1,0:T(8,128)(2,1)S(1)}, bf16[80,128]{1,0:T(8,128)(2,1)S(1)}) custom-call(s32[4]{0:T(128)S(1)} %copy-done.2, s32[4]{0:T(128)S(1)} %copy-done.3, bf16[4,32,384]{2,1,0:T(8,128)(2,1)S(1)} %collective-permute-done.refs_0_, bf16[3,32,384]{2,1,0:T(8,128)(2,1)S(1)} %collective-permute-done.1.refs_1_, ...), custom_call_target="tpu_custom_call" | custom-call | tf_op jit(solution)/shard_map/place/pallas_call | solution.py:377
  13.9 0.1 collective-permute-start.3
  14.0 2.5 %collective-permute-start.4 = (bf16[80,128]{1,0:T(8,128)(2,1)S(1)}, bf16[80,128]{1,0:T(8,128)(2,1)S(1)}, u32[]{:S(2)}, u32[]{:S(2)}) collective-permute-start(bf16[80,128]{1,0:T(8,128)(2,1)S(1)} %get-tuple-element.15.to_cross_ref), channel_id=1, source_target_pairs={{4,8},{8,4},{12,16},{16,12},{20,24},{24,20},{0,28},{28,0},{5,9},{9... | collective-permute-start | bytes 61448 | tf_op jit(solution)/shard_map/ppermute | solution.py:390
  16.5 0.0 copy-start.5
  16.5 2.1 %main.1.inner_ref = f32[56,384]{1,0:T(8,128)S(1)} custom-call(f32[60,56,128]{2,1,0:T(8,128)S(1)} %factors.1.factor_ref, bf16[120,1008]{1,0:T(8,128)(2,1)S(1)} %get-tuple-element.9.after_ref.upper_ref, bf16[160,1008]{1,0:T(8,128)(2,1)S(1)} %get-tuple-element.10.lower_ref, bf16[4,80,384]{2,1,0:T(8,128)(2,1)S(1)} %get-tuple-element.13.window_ref), custom_call_target="tpu_custom_call" | custom-call | flops 2000000000 | bytes 1000000 | tf_op jit(solution)/shard_map/main/pallas_call | solution.py:392
  18.7 0.0 collective-permute-done.3.from_core_ref
  18.7 0.0 collective-permute-done.4.from_cross_ref
  18.7 0.0 copy-done.5
  18.7 2.8 %rim.1 = (f32[32,384]{1,0:T(8,128)}, f32[32,384]{1,0:T(8,128)}) custom-call(f32[21]{0:T(128)S(1)} %copy-done.5, f32[60,56,128]{2,1,0:T(8,128)S(1)} %factors.1.factor_ref, bf16[120,1008]{1,0:T(8,128)(2,1)S(1)} %get-tuple-element.9.after_ref.upper_ref, bf16[160,1008]{1,0:T(8,128)(2,1)S(1)} %get-tuple-element.10.lower_ref, f32[56,384]{1,0:T(8,128)S(1)} %main.1.inner_ref, ...), custom_call_target="tpu_custom_call" | custom-call | tf_op jit(solution)/shard_map/rim/pallas_call | solution.py:403
Async XLA Ops:
  0.6 12.5 %collective-permute-start = (bf16[4,32,384]{2,1,0:T(8,128)(2,1)}, bf16[4,32,384]{2,1,0:T(8,128)(2,1)S(1)}, u32[]{:S(2)}, u32[]{:S(2)}) collective-permute-start(bf16[4,32,384]{2,1,0:T(8,128)(2,1)} %refs_3_.1), channel_id=1, source_target_pairs={{0,3},{1,2},{2,1},{3,0},{4,7},{5,6},{6,5},{7,4},{8,11},{9,10},{10,... | collective-permute-start | bytes 294920 | tf_op jit(solution)/shard_map/ppermute | solution.py:370
  6.7 2.1 %copy-start.1 = (f32[4,5,6]{2,0,1:T(4,128)S(1)}, f32[4,5,6]{2,0,1:T(4,128)}, u32[]{:S(2)}) copy-start(f32[4,5,6]{2,0,1:T(4,128)} %param.9) | copy-start | bytes 1444
  6.7 2.1 %copy-start.2 = (s32[4]{0:T(128)S(1)}, s32[4]{0:T(128)}, u32[]{:S(2)}) copy-start(s32[4]{0:T(128)} %start_ref.3) | copy-start | bytes 52
  6.7 2.1 %copy-start.3 = (s32[4]{0:T(128)S(1)}, s32[4]{0:T(128)}, u32[]{:S(2)}) copy-start(s32[4]{0:T(128)} %count_ref.3) | copy-start | bytes 52
  6.7 2.1 %copy-start.4 = (f32[4]{0:T(128)S(1)}, f32[4]{0:T(128)}, u32[]{:S(2)}) copy-start(f32[4]{0:T(128)} %weight_ref.1) | copy-start | bytes 52
  6.7 6.5 %collective-permute-start.1 = (bf16[3,32,384]{2,1,0:T(8,128)(2,1)S(1)}, bf16[3,32,384]{2,1,0:T(8,128)(2,1)S(1)}, u32[]{:S(2)}, u32[]{:S(2)}) collective-permute-start(bf16[3,32,384]{2,1,0:T(8,128)(2,1)S(1)} %slice.3), channel_id=1, source_target_pairs={{0,2},{1,3},{2,0},{3,1},{4,6},{5,7},{6,4},{7,5},{8,10},{9,11},{10,... | collective-permute-start | bytes 221192 | tf_op jit(solution)/shard_map/ppermute | solution.py:370
  6.8 6.4 %collective-permute-start.2 = (bf16[4,32,384]{2,1,0:T(8,128)(2,1)}, bf16[4,32,384]{2,1,0:T(8,128)(2,1)S(1)}, u32[]{:S(2)}, u32[]{:S(2)}) collective-permute-start(bf16[4,32,384]{2,1,0:T(8,128)(2,1)} %refs_3_.1), channel_id=1, source_target_pairs={{0,1},{1,0},{2,3},{3,2},{4,5},{5,4},{6,7},{7,6},{8,9},{9,8},{10,11... | collective-permute-start | bytes 294920 | tf_op jit(solution)/shard_map/ppermute | solution.py:370
  7.4 0.8 %copy-start.6 = (bf16[5,21,21]{2,1,0:T(8,128)(2,1)S(1)}, bf16[5,21,21]{2,1,0:T(8,128)(2,1)}, u32[]{:S(2)}) copy-start(bf16[5,21,21]{2,1,0:T(8,128)(2,1)} %basis_ref.1) | copy-start | bytes 13234
  8.8 4.4 %copy-start = (bf16[4,32,384]{2,1,0:T(8,128)(2,1)S(1)}, bf16[4,32,384]{2,1,0:T(8,128)(2,1)}, u32[]{:S(2)}) copy-start(bf16[4,32,384]{2,1,0:T(8,128)(2,1)} %refs_3_.1) | copy-start | bytes 294916
  13.9 4.8 %collective-permute-start.3 = (bf16[80,128]{1,0:T(8,128)(2,1)S(1)}, bf16[80,128]{1,0:T(8,128)(2,1)S(1)}, u32[]{:S(2)}, u32[]{:S(2)}) collective-permute-start(bf16[80,128]{1,0:T(8,128)(2,1)S(1)} %get-tuple-element.14.to_core_ref), channel_id=1, source_target_pairs={{0,4},{4,0},{8,12},{12,8},{16,20},{20,16},{24,28},{28,24},{1,5},{5... | collective-permute-start | bytes 61448 | tf_op jit(solution)/shard_map/ppermute | solution.py:389
  14.0 4.7 %collective-permute-start.4 = (bf16[80,128]{1,0:T(8,128)(2,1)S(1)}, bf16[80,128]{1,0:T(8,128)(2,1)S(1)}, u32[]{:S(2)}, u32[]{:S(2)}) collective-permute-start(bf16[80,128]{1,0:T(8,128)(2,1)S(1)} %get-tuple-element.15.to_cross_ref), channel_id=1, source_target_pairs={{4,8},{8,4},{12,16},{16,12},{20,24},{24,20},{0,28},{28,0},{5,9},{9... | collective-permute-start | bytes 61448 | tf_op jit(solution)/shard_map/ppermute | solution.py:390
  16.5 2.1 %copy-start.5 = (f32[21]{0:T(128)S(1)}, f32[21]{0:T(128)}, u32[]{:S(2)}) copy-start(f32[21]{0:T(128)} %taps_ref.1) | copy-start | bytes 256

commit v5 on v4

--- a/solution.py
+++ b/solution.py
@@ -384,10 +384,17 @@
         name="place",
     )(row_start, row_count, *reversed(tiles))
     core_pairs = [(i, i ^ 1) for i in range(wide_peers)]
-    cross_pairs = [(i, ((i - 1) ^ 1) + 1) for i in range(1, wide_peers - 1)]
-    cross_pairs += [(0, wide_peers - 1), (wide_peers - 1, 0)]
+    cross_pairs = []
+    for row in range(peers):
+        for column in range(wide_peers):
+            other = ((column - 1) ^ 1) + 1
+            if other in (-1, wide_peers):
+                pair = (row ^ 1, column)
+            else:
+                pair = (row, other)
+            cross_pairs.append((column * peers + row, pair[1] * peers + pair[0]))
     from_core = lax.ppermute(to_core, "wide", core_pairs)
-    from_cross = lax.ppermute(to_cross, "wide", cross_pairs)
+    from_cross = lax.ppermute(to_cross, ("wide", "narrow"), cross_pairs)
 
     inner = pl.pallas_call(
         functools.partial(main_kernel, wide_peers, side, tile_rows),

time: 21.7 us -> 20.9 us (0.963)
  starting transfers between devices: 8.36 us -> 6.93 us
  waiting for transfers between devices: 3.35 us -> 3.95 us
    ppermute x1, starting transfers between devices: 2.55 us -> 1.11 us  [on_device(): from_cross = lax.ppermute(to_cross, ('wide', 'narrow'), cross_pairs)]
    ppermute x1, waiting for transfers between devices: 0.01 us -> 0.6 us  [on_device(): from_cross = lax.ppermute(to_cross, ('wide', 'narrow'), cross_pairs)]
  transfers between devices with their start and end apart: 5 -> 5, of which waited for: 1 -> 2; matrix products, arithmetic and copies ran while one was open for 4% -> 4% of each run, Pallas kernels for 18% -> 18%
where the time goes in v5:
time: 20.9 us; the launch traced here: 20.6 us
  Pallas kernels  7.3 us (35%)
  starting transfers between devices  6.93 us (33%)
  waiting for transfers between devices  3.95 us (19%)
  local copies, waits for them, and re-layouts  1.71 us (8%)
  between operations  0.76 us (4%)
    ppermute x3, starting transfers between devices, on_device(): lax.ppermute(latter if sent[index] else whole, 'narrow', pairs)  5.74 us
    ppermute x3, waiting for transfers between devices, on_device(): lax.ppermute(latter if sent[index] else whole, 'narrow', pairs)  3.35 us
    pallas_call x1, Pallas kernels, on_device(): pl.pallas_call(functools.partial(rim_kernel, wide_peers, side, members),...  2.81 us
    pallas_call x1, Pallas kernels, on_device(): pl.pallas_call(functools.partial(main_kernel, wide_peers, side, tile_rows...  2.12 us
    ppermute x1, starting transfers between devices, on_device(): from_cross = lax.ppermute(to_cross, ('wide', 'narrow'), cross_pairs)  1.11 us
    pallas_call x1, Pallas kernels, prepared(): pl.pallas_call(functools.partial(factors_kernel, tile_rows, band_rows, ha...  0.98 us
    slice x1, local copies, waits for them, and re-layouts, on_device(): moving, latter = lax.optimization_barrier((exposures, exposures[1:]))  0.93 us
    unnamed x14, local copies, waits for them, and re-layouts  0.78 us
  transfers between devices with their start and end apart: 5, of which 2 were waited for; matrix products, arithmetic and copies ran while one was open for 4% of the time, Pallas kernels for 18%

profile of v5, /device:TPU:0, one launch (start us, length us, event | category | flops | bytes accessed | tf_op | source)
XLA Modules:
  0.0 20.6 jit_solution(12111084520928015729)
XLA Ops:
  0.6 5.1 %collective-permute-start = (bf16[4,32,384]{2,1,0:T(8,128)(2,1)}, bf16[4,32,384]{2,1,0:T(8,128)(2,1)S(1)}, u32[]{:S(2)}, u32[]{:S(2)}) collective-permute-start(bf16[4,32,384]{2,1,0:T(8,128)(2,1)} %refs_3_.1), channel_id=1, source_target_pairs={{0,3},{1,2},{2,1},{3,0},{4,7},{5,6},{6,5},{7,4},{8,11},{9,10},{10,... | collective-permute-start | bytes 294920 | tf_op jit(solution)/shard_map/ppermute | solution.py:370
  5.7 0.9 %slice.3 = bf16[3,32,384]{2,1,0:T(8,128)(2,1)S(1)} slice(bf16[4,32,384]{2,1,0:T(8,128)(2,1)} %refs_3_.1), slice={[1:4], [0:32], [0:384]} | slice | bytes 147456 | tf_op jit(solution)/shard_map/slice | solution.py:366
  6.7 0.0 copy-start.1
  6.7 0.0 copy-start.2
  6.7 0.0 copy-start.3
  6.7 0.0 copy-start.4
  6.7 0.1 collective-permute-start.1
  6.8 0.6 %collective-permute-start.2 = (bf16[4,32,384]{2,1,0:T(8,128)(2,1)}, bf16[4,32,384]{2,1,0:T(8,128)(2,1)S(1)}, u32[]{:S(2)}, u32[]{:S(2)}) collective-permute-start(bf16[4,32,384]{2,1,0:T(8,128)(2,1)} %refs_3_.1), channel_id=1, source_target_pairs={{0,1},{1,0},{2,3},{3,2},{4,5},{5,4},{6,7},{7,6},{8,9},{9,8},{10,11... | collective-permute-start | bytes 294920 | tf_op jit(solution)/shard_map/ppermute | solution.py:370
  7.4 0.0 copy-start.6
  7.4 0.8 %copy-done.6 = bf16[5,21,21]{2,1,0:T(8,128)(2,1)S(1)} copy-done((bf16[5,21,21]{2,1,0:T(8,128)(2,1)S(1)}, bf16[5,21,21]{2,1,0:T(8,128)(2,1)}, u32[]{:S(2)}) %copy-start.6) | copy-done | bytes 4434
  8.1 0.7 %bands.1 = (bf16[120,1008]{1,0:T(8,128)(2,1)S(1)}, bf16[160,1008]{1,0:T(8,128)(2,1)S(1)}) custom-call(bf16[5,21,21]{2,1,0:T(8,128)(2,1)S(1)} %copy-done.6), custom_call_target="tpu_custom_call" | custom-call | flops 1000000000 | bytes 1000000 | tf_op jit(solution)/shard_map/bands/pallas_call | solution.py:116
  8.8 0.0 copy-start
  8.8 0.0 copy-done.1
  8.8 0.0 copy-done.2
  8.8 0.0 copy-done.3
  8.8 0.0 copy-done.4
  8.8 1.0 %factors.1.factor_ref = f32[60,56,128]{2,1,0:T(8,128)S(1)} custom-call(f32[5,4,6]{2,1,0:T(4,128)S(1)} %bitcast.1, f32[4]{0:T(128)S(1)} %copy-done.4, s32[4]{0:T(128)S(1)} %copy-done.2, s32[4]{0:T(128)S(1)} %copy-done.3, bf16[120,1008]{1,0:T(8,128)(2,1)S(1)} %get-tuple-element.9.after_ref.upper_ref), custom_call_target="tpu_custom_call" | custom-call | flops 100000000 | bytes 1000000 | tf_op jit(solution)/shard_map/factors/pallas_call | solution.py:129
  9.8 3.3 %collective-permute-done.1.refs_1_ = bf16[3,32,384]{2,1,0:T(8,128)(2,1)S(1)} collective-permute-done((bf16[3,32,384]{2,1,0:T(8,128)(2,1)S(1)}, bf16[3,32,384]{2,1,0:T(8,128)(2,1)S(1)}, u32[]{:S(2)}, u32[]{:S(2)}) %collective-permute-start.1) | collective-permute-done | bytes 73760 | tf_op jit(solution)/shard_map/ppermute | solution.py:370
  13.2 0.0 collective-permute-done.2.refs_2_
  13.2 0.0 collective-permute-done.refs_0_
  13.2 0.0 copy-done
  13.2 0.7 %place.1 = (bf16[4,80,384]{2,1,0:T(8,128)(2,1)S(1)}, bf16[80,128]{1,0:T(8,128)(2,1)S(1)}, bf16[80,128]{1,0:T(8,128)(2,1)S(1)}) custom-call(s32[4]{0:T(128)S(1)} %copy-done.2, s32[4]{0:T(128)S(1)} %copy-done.3, bf16[4,32,384]{2,1,0:T(8,128)(2,1)S(1)} %collective-permute-done.refs_0_, bf16[3,32,384]{2,1,0:T(8,128)(2,1)S(1)} %collective-permute-done.1.refs_1_, ...), custom_call_target="tpu_custom_call" | custom-call | tf_op jit(solution)/shard_map/place/pallas_call | solution.py:377
  13.9 0.1 collective-permute-start.3
  14.0 1.1 %collective-permute-start.4 = (bf16[80,128]{1,0:T(8,128)(2,1)S(1)}, bf16[80,128]{1,0:T(8,128)(2,1)S(1)}, u32[]{:S(2)}, u32[]{:S(2)}) collective-permute-start(bf16[80,128]{1,0:T(8,128)(2,1)S(1)} %get-tuple-element.15.to_cross_ref), channel_id=1, source_target_pairs={{0,1},{4,8},{8,4},{12,16},{16,12},{20,24},{24,20},{28,29},{1,0},{5... | collective-permute-start | bytes 61448 | tf_op jit(solution)/shard_map/ppermute | solution.py:397
  15.1 0.0 copy-start.5
  15.1 2.1 %main.1.inner_ref = f32[56,384]{1,0:T(8,128)S(1)} custom-call(f32[60,56,128]{2,1,0:T(8,128)S(1)} %factors.1.factor_ref, bf16[120,1008]{1,0:T(8,128)(2,1)S(1)} %get-tuple-element.9.after_ref.upper_ref, bf16[160,1008]{1,0:T(8,128)(2,1)S(1)} %get-tuple-element.10.lower_ref, bf16[4,80,384]{2,1,0:T(8,128)(2,1)S(1)} %get-tuple-element.13.window_ref), custom_call_target="tpu_custom_call" | custom-call | flops 2000000000 | bytes 1000000 | tf_op jit(solution)/shard_map/main/pallas_call | solution.py:399
  17.2 0.0 collective-permute-done.3.from_core_ref
  17.2 0.6 %collective-permute-done.4.from_cross_ref = bf16[80,128]{1,0:T(8,128)(2,1)S(1)} collective-permute-done((bf16[80,128]{1,0:T(8,128)(2,1)S(1)}, bf16[80,128]{1,0:T(8,128)(2,1)S(1)}, u32[]{:S(2)}, u32[]{:S(2)}) %collective-permute-start.4) | collective-permute-done | bytes 20512 | tf_op jit(solution)/shard_map/ppermute | solution.py:397
  17.8 0.0 copy-done.5
  17.8 2.8 %rim.1 = (f32[32,384]{1,0:T(8,128)}, f32[32,384]{1,0:T(8,128)}) custom-call(f32[21]{0:T(128)S(1)} %copy-done.5, f32[60,56,128]{2,1,0:T(8,128)S(1)} %factors.1.factor_ref, bf16[120,1008]{1,0:T(8,128)(2,1)S(1)} %get-tuple-element.9.after_ref.upper_ref, bf16[160,1008]{1,0:T(8,128)(2,1)S(1)} %get-tuple-element.10.lower_ref, f32[56,384]{1,0:T(8,128)S(1)} %main.1.inner_ref, ...), custom_call_target="tpu_custom_call" | custom-call | tf_op jit(solution)/shard_map/rim/pallas_call | solution.py:410
Async XLA Ops:
  0.6 12.5 %collective-permute-start = (bf16[4,32,384]{2,1,0:T(8,128)(2,1)}, bf16[4,32,384]{2,1,0:T(8,128)(2,1)S(1)}, u32[]{:S(2)}, u32[]{:S(2)}) collective-permute-start(bf16[4,32,384]{2,1,0:T(8,128)(2,1)} %refs_3_.1), channel_id=1, source_target_pairs={{0,3},{1,2},{2,1},{3,0},{4,7},{5,6},{6,5},{7,4},{8,11},{9,10},{10,... | collective-permute-start | bytes 294920 | tf_op jit(solution)/shard_map/ppermute | solution.py:370
  6.7 2.1 %copy-start.1 = (f32[4,5,6]{2,0,1:T(4,128)S(1)}, f32[4,5,6]{2,0,1:T(4,128)}, u32[]{:S(2)}) copy-start(f32[4,5,6]{2,0,1:T(4,128)} %param.9) | copy-start | bytes 1444
  6.7 2.1 %copy-start.2 = (s32[4]{0:T(128)S(1)}, s32[4]{0:T(128)}, u32[]{:S(2)}) copy-start(s32[4]{0:T(128)} %start_ref.3) | copy-start | bytes 52
  6.7 2.1 %copy-start.3 = (s32[4]{0:T(128)S(1)}, s32[4]{0:T(128)}, u32[]{:S(2)}) copy-start(s32[4]{0:T(128)} %count_ref.3) | copy-start | bytes 52
  6.7 2.1 %copy-start.4 = (f32[4]{0:T(128)S(1)}, f32[4]{0:T(128)}, u32[]{:S(2)}) copy-start(f32[4]{0:T(128)} %weight_ref.1) | copy-start | bytes 52
  6.7 6.5 %collective-permute-start.1 = (bf16[3,32,384]{2,1,0:T(8,128)(2,1)S(1)}, bf16[3,32,384]{2,1,0:T(8,128)(2,1)S(1)}, u32[]{:S(2)}, u32[]{:S(2)}) collective-permute-start(bf16[3,32,384]{2,1,0:T(8,128)(2,1)S(1)} %slice.3), channel_id=1, source_target_pairs={{0,2},{1,3},{2,0},{3,1},{4,6},{5,7},{6,4},{7,5},{8,10},{9,11},{10,... | collective-permute-start | bytes 221192 | tf_op jit(solution)/shard_map/ppermute | solution.py:370
  6.8 6.4 %collective-permute-start.2 = (bf16[4,32,384]{2,1,0:T(8,128)(2,1)}, bf16[4,32,384]{2,1,0:T(8,128)(2,1)S(1)}, u32[]{:S(2)}, u32[]{:S(2)}) collective-permute-start(bf16[4,32,384]{2,1,0:T(8,128)(2,1)} %refs_3_.1), channel_id=1, source_target_pairs={{0,1},{1,0},{2,3},{3,2},{4,5},{5,4},{6,7},{7,6},{8,9},{9,8},{10,11... | collective-permute-start | bytes 294920 | tf_op jit(solution)/shard_map/ppermute | solution.py:370
  7.4 0.8 %copy-start.6 = (bf16[5,21,21]{2,1,0:T(8,128)(2,1)S(1)}, bf16[5,21,21]{2,1,0:T(8,128)(2,1)}, u32[]{:S(2)}) copy-start(bf16[5,21,21]{2,1,0:T(8,128)(2,1)} %basis_ref.1) | copy-start | bytes 13234
  8.8 4.4 %copy-start = (bf16[4,32,384]{2,1,0:T(8,128)(2,1)S(1)}, bf16[4,32,384]{2,1,0:T(8,128)(2,1)}, u32[]{:S(2)}) copy-start(bf16[4,32,384]{2,1,0:T(8,128)(2,1)} %refs_3_.1) | copy-start | bytes 294916
  13.9 3.3 %collective-permute-start.3 = (bf16[80,128]{1,0:T(8,128)(2,1)S(1)}, bf16[80,128]{1,0:T(8,128)(2,1)S(1)}, u32[]{:S(2)}, u32[]{:S(2)}) collective-permute-start(bf16[80,128]{1,0:T(8,128)(2,1)S(1)} %get-tuple-element.14.to_core_ref), channel_id=1, source_target_pairs={{0,4},{4,0},{8,12},{12,8},{16,20},{20,16},{24,28},{28,24},{1,5},{5... | collective-permute-start | bytes 61448 | tf_op jit(solution)/shard_map/ppermute | solution.py:396
  14.0 3.8 %collective-permute-start.4 = (bf16[80,128]{1,0:T(8,128)(2,1)S(1)}, bf16[80,128]{1,0:T(8,128)(2,1)S(1)}, u32[]{:S(2)}, u32[]{:S(2)}) collective-permute-start(bf16[80,128]{1,0:T(8,128)(2,1)S(1)} %get-tuple-element.15.to_cross_ref), channel_id=1, source_target_pairs={{0,1},{4,8},{8,4},{12,16},{16,12},{20,24},{24,20},{28,29},{1,0},{5... | collective-permute-start | bytes 61448 | tf_op jit(solution)/shard_map/ppermute | solution.py:397
  15.1 2.7 %copy-start.5 = (f32[21]{0:T(128)S(1)}, f32[21]{0:T(128)}, u32[]{:S(2)}) copy-start(f32[21]{0:T(128)} %taps_ref.1) | copy-start | bytes 256

commit v6 on v5

--- a/solution.py
+++ b/solution.py
@@ -47,8 +47,25 @@
 
 
 def factors_kernel(
-    tile_rows, band_rows, half, coef_ref, weight_ref, start_ref, count_ref, after_ref, factor_ref
+    tile_rows,
+    band_rows,
+    half,
+    coef_ref,
+    weight_ref,
+    start_ref,
+    count_ref,
+    taps_ref,
+    after_ref,
+    factor_ref,
+    spread_ref,
+    span_ref,
 ):
+    for tap in range(taps_ref.shape[0]):
+        spread_ref[tap : tap + 1, :] = jnp.full((1, LANES), taps_ref[tap], jnp.float32)
+    for member in range(start_ref.shape[0]):
+        span_ref[member] = jnp.full((16, LANES), start_ref[member], jnp.int32)
+        span_ref[start_ref.shape[0] + member] = jnp.full((16, LANES), count_ref[member], jnp.int32)
+
     kernel_total, members = coef_ref.shape[:2]
     out_rows = factor_ref.shape[1]
     place = lax.broadcasted_iota(jnp.int32, (out_rows, LANES), 0)
@@ -104,7 +121,7 @@
     band_matrix(half, UPPER, base, lower_ref)
 
 
-def prepared(basis_kernels, poly_coef, weight, start, count, tile_rows):
+def prepared(basis_kernels, poly_coef, weight, start, count, taps, tile_rows):
     kernel_total, side = basis_kernels.shape[:2]
     members = poly_coef.shape[0]
     half, out_rows, _ = sizes(tile_rows, side)
@@ -126,16 +143,20 @@
         cost_estimate=pl.CostEstimate(flops=10**9, bytes_accessed=10**6, transcendentals=0),
         name="bands",
     )(basis_kernels)
-    factors = pl.pallas_call(
+    factors, spread, span = pl.pallas_call(
         functools.partial(factors_kernel, tile_rows, band_rows, half),
-        out_shape=jax.ShapeDtypeStruct((3 * members * kernel_total, out_rows, LANES), jnp.float32),
-        in_specs=[smem] * 4 + [pl.BlockSpec(memory_space=pl.ANY)],
-        out_specs=vmem,
+        out_shape=(
+            jax.ShapeDtypeStruct((3 * members * kernel_total, out_rows, LANES), jnp.float32),
+            jax.ShapeDtypeStruct((side, LANES), jnp.float32),
+            jax.ShapeDtypeStruct((2 * members, 16, LANES), jnp.int32),
+        ),
+        in_specs=[smem] * 5 + [pl.BlockSpec(memory_space=pl.ANY)],
+        out_specs=(vmem, vmem, vmem),
         compiler_params=params,
         cost_estimate=pl.CostEstimate(flops=10**8, bytes_accessed=10**6, transcendentals=0),
         name="factors",
-    )(poly_coef.transpose(1, 0, 2), weight, start, count, upper)
-    return factors, upper, lower
+    )(poly_coef.transpose(1, 0, 2), weight, start, count, taps, upper)
+    return spread, span, (factors, upper, lower)
 
 
 def part_rows_of(moved):
@@ -158,10 +179,21 @@
 
 
 def products(band_refs, patch_refs):
-    return [
-        jnp.dot(band_ref[...], patch_ref[...], preferred_element_type=jnp.float32)
-        for band_ref, patch_ref in zip(band_refs, patch_refs, strict=True)
-    ]
+    results = []
+    for band_ref, patch_ref in zip(band_refs, patch_refs, strict=True):
+        depth = band_ref.shape[1]
+        pieces = []
+        for begin in range(0, depth, 256):
+            end = min(begin + 256, depth)
+            pieces.append(
+                jnp.dot(
+                    band_ref[:, begin:end],
+                    patch_ref[begin:end, :],
+                    preferred_element_type=jnp.float32,
+                )
+            )
+        results.append(functools.reduce(jnp.add, pieces))
+    return results
 
 
 def response_of(parts, kernel, kernel_total, lanes):
@@ -172,38 +204,52 @@
     return jnp.concatenate(pieces, axis=0)
 
 
-def place_kernel(sent, start_ref, count_ref, *refs):
+def place_kernel(sent, span_ref, *refs):
     peers = len(sent)
     tiles = refs[:peers][::-1]
-    window_ref, core_ref, cross_ref, frame = refs[peers:]
+    window_ref, core_ref, cross_ref = refs[peers:]
     members, window_rows, tile_cols = window_ref.shape
     tile_rows = tiles[0].shape[1]
     narrow = lax.axis_index("narrow")
     odd = lax.rem(lax.axis_index("wide"), 2) == 1
-    for index in range(peers):
-        frame[jnp.bitwise_xor(narrow, index), sent[index] :] = tiles[index][...]
     lane = lax.broadcasted_iota(jnp.int32, (window_rows, LANES), 1)
-    upper = lax.broadcasted_iota(jnp.int32, (16, tile_cols), 0) < 8
+    place = lax.broadcasted_iota(jnp.int32, (16, tile_cols), 0)
     leftward = jnp.zeros((window_rows, LANES), jnp.bfloat16)
     rightward = jnp.zeros((window_rows, LANES), jnp.bfloat16)
+    none = jnp.zeros((16, tile_cols), jnp.bfloat16)
+
+    def over_columns(array):
+        return jnp.concatenate([array] * (tile_cols // LANES), axis=1)
+
     for member in range(members):
-        slot = narrow - start_ref[member] // tile_rows
-        here = jnp.clip(slot, 0, peers - 1)
-        above = jnp.clip(slot - 1, 0, peers - 1)
-        below = jnp.clip(slot + 1, 0, peers - 1)
-        window = jnp.concatenate(
-            [
-                frame[here, member],
-                frame[below, member, :16],
-                jnp.where(upper, frame[below, member, 16:], frame[above, member, :16]),
-                frame[above, member, 16:],
-            ]
+        lead = over_columns(narrow * tile_rows - span_ref[member])
+        count = over_columns(span_ref[members + member])
+        here, below, above = [none] * 2, [none] * 2, [none] * 2
+        for index in range(peers):
+            if member < sent[index]:
+                continue
+            tile = [tiles[index][member - sent[index], row : row + 16] for row in (0, 16)]
+            base = jnp.bitwise_xor(narrow, index) * tile_rows
+            for parts, offset in ((here, 0), (below, tile_rows), (above, -tile_rows)):
+                chosen = lead + offset == base
+                for part in range(2):
+                    parts[part] = jnp.where(chosen, tile[part], parts[part])
+        upper = place < 8
+        groups = (
+            (here[0], place),
+            (here[1], place + 16),
+            (below[0], place + tile_rows),
+            (
+                jnp.where(upper, below[1], above[0]),
+                place + jnp.where(upper, tile_rows + 16, -tile_rows),
+            ),
+            (above[1], place - 16),
         )
-        place = lax.broadcasted_iota(jnp.int32, window.shape, 0)
-        offset = jnp.where(place < window_rows - 24, place, place - window_rows)
-        frame_row = offset + slot * tile_rows
-        present = (frame_row >= 0) & (frame_row < count_ref[member])
-        window = jnp.where(present, window, jnp.zeros((), window.dtype))
+        kept = []
+        for values, offset in groups:
+            frame_row = lead + offset
+            kept.append(jnp.where((frame_row >= 0) & (frame_row < count), values, none))
+        window = jnp.concatenate(kept, axis=0)
         window_ref[member] = window
         own = lane // 32 == member
         first = pltpu.roll(window[:, :LANES], 32 * member, 1)
@@ -338,12 +384,19 @@
     )
     tall[:, tile_cols:] = jnp.where(lane < LANES // 2, right, left)
     coadd_ref[...] = tall[half : half + tile_rows, :tile_cols]
-    filtered = taps_ref[0] * tall[:tile_rows, :]
+    taps = [
+        jnp.broadcast_to(
+            jnp.concatenate([taps_ref[tap : tap + 1, :]] * (width // LANES), axis=1),
+            (tile_rows, width),
+        )
+        for tap in range(side)
+    ]
+    filtered = taps[0] * tall[:tile_rows, :]
     for tap in range(1, side):
-        filtered = filtered + taps_ref[tap] * tall[tap : tap + tile_rows, :]
-    detection = taps_ref[0] * pltpu.roll(filtered, half, 1)
+        filtered = filtered + taps[tap] * tall[tap : tap + tile_rows, :]
+    detection = taps[0] * pltpu.roll(filtered, half, 1)
     for tap in range(1, side):
-        detection = detection + taps_ref[tap] * pltpu.roll(filtered, (half - tap) % width, 1)
+        detection = detection + taps[tap] * pltpu.roll(filtered, (half - tap) % width, 1)
     detection_ref[...] = detection[:, :tile_cols]
 
 
@@ -354,7 +407,6 @@
     side = basis_kernels.shape[1]
     half, out_rows, in_rows = sizes(tile_rows, side)
     peers, wide_peers = lax.axis_size("narrow"), lax.axis_size("wide")
-    smem = pl.BlockSpec(memory_space=pltpu.SMEM)
     vmem = pl.BlockSpec(memory_space=pltpu.VMEM)
     params = pltpu.CompilerParams(vmem_limit_bytes=VMEM_BYTES)
 
@@ -368,8 +420,14 @@
         pairs = [(i, i ^ index) for i in range(peers)]
         whole = moving if index == 1 else exposures
         tiles[index] = lax.ppermute(latter if sent[index] else whole, "narrow", pairs)
-    tables = prepared(
-        basis_kernels, poly_coef, exposure_weight, row_start, row_count, tile_rows
+    taps, span, tables = prepared(
+        basis_kernels,
+        poly_coef,
+        exposure_weight,
+        row_start,
+        row_count,
+        filter_taps,
+        tile_rows,
     )
     depth = side * PART
     edge_shape = jax.ShapeDtypeStruct((in_rows, LANES), exposures.dtype)
@@ -377,12 +435,11 @@
     window, to_core, to_cross = pl.pallas_call(
         functools.partial(place_kernel, sent),
         out_shape=(window_shape, edge_shape, edge_shape),
-        in_specs=[smem] * 2 + [vmem] * peers,
+        in_specs=[vmem] * (1 + peers),
         out_specs=[vmem] * 3,
-        scratch_shapes=[pltpu.VMEM((peers, members, tile_rows, tile_cols), jnp.bfloat16)],
         compiler_params=params,
         name="place",
-    )(row_start, row_count, *reversed(tiles))
+    )(span, *reversed(tiles))
     core_pairs = [(i, i ^ 1) for i in range(wide_peers)]
     cross_pairs = []
     for row in range(peers):
@@ -410,7 +467,7 @@
     return pl.pallas_call(
         functools.partial(rim_kernel, wide_peers, side, members),
         out_shape=(out, out),
-        in_specs=[smem] + [vmem] * 8,
+        in_specs=[vmem] * 9,
         out_specs=(vmem, vmem),
         scratch_shapes=[
             pltpu.VMEM((depth, members * LANES), jnp.bfloat16),
@@ -419,7 +476,7 @@
         ],
         compiler_params=params,
         name="rim",
-    )(filter_taps, *tables, inner, to_core, to_cross, from_core, from_cross)
+    )(taps, *tables, inner, to_core, to_cross, from_core, from_cross)
 
 
 def solution(mesh):

time: 20.9 us -> 19.7 us (0.943)
  Pallas kernels: 7.3 us -> 6.16 us
    pallas_call x1, Pallas kernels: 2.81 us -> 2.21 us  [on_device(): pl.pallas_call(functools.partial(rim_kernel, wide_peers, side, members),...]
    pallas_call x1, Pallas kernels: 0.72 us -> 0.23 us  [on_device(): pl.pallas_call(functools.partial(place_kernel, sent), out_shape=(window_s...]
  transfers between devices with their start and end apart: 5 -> 5, of which waited for: 2 -> 2; matrix products, arithmetic and copies ran while one was open for 4% -> 5% of each run, Pallas kernels for 18% -> 19%
where the time goes in v6:
time: 19.7 us; the launch traced here: 19.5 us
  starting transfers between devices  6.92 us (35%)
  Pallas kernels  6.16 us (31%)
  waiting for transfers between devices  3.98 us (20%)
  local copies, waits for them, and re-layouts  1.72 us (9%)
  between operations  0.75 us (4%)
    ppermute x3, starting transfers between devices, on_device(): lax.ppermute(latter if sent[index] else whole, 'narrow', pairs)  5.75 us
    ppermute x3, waiting for transfers between devices, on_device(): lax.ppermute(latter if sent[index] else whole, 'narrow', pairs)  3.32 us
    pallas_call x1, Pallas kernels, on_device(): pl.pallas_call(functools.partial(rim_kernel, wide_peers, side, members),...  2.21 us
    pallas_call x1, Pallas kernels, on_device(): pl.pallas_call(functools.partial(main_kernel, wide_peers, side, tile_rows...  2.06 us
    ppermute x1, starting transfers between devices, on_device(): from_cross = lax.ppermute(to_cross, ('wide', 'narrow'), cross_pairs)  1.11 us
    pallas_call x1, Pallas kernels, prepared(): pl.pallas_call(functools.partial(factors_kernel, tile_rows, band_rows, ha...  1 us
    slice x1, local copies, waits for them, and re-layouts, on_device(): moving, latter = lax.optimization_barrier((exposures, exposures[1:]))  0.95 us
    unnamed x14, local copies, waits for them, and re-layouts  0.77 us
  transfers between devices with their start and end apart: 5, of which 2 were waited for; matrix products, arithmetic and copies ran while one was open for 5% of the time, Pallas kernels for 19%

profile of v6, /device:TPU:0, one launch (start us, length us, event | category | flops | bytes accessed | tf_op | source)
XLA Modules:
  0.0 19.5 jit_solution(8573532932237486732)
XLA Ops:
  0.6 5.1 %collective-permute-start = (bf16[4,32,384]{2,1,0:T(8,128)(2,1)}, bf16[4,32,384]{2,1,0:T(8,128)(2,1)S(1)}, u32[]{:S(2)}, u32[]{:S(2)}) collective-permute-start(bf16[4,32,384]{2,1,0:T(8,128)(2,1)} %refs_3_.1), channel_id=1, source_target_pairs={{0,3},{1,2},{2,1},{3,0},{4,7},{5,6},{6,5},{7,4},{8,11},{9,10},{10,... | collective-permute-start | bytes 294920 | tf_op jit(solution)/shard_map/ppermute | solution.py:422
  5.7 0.0 copy-start.2
  5.7 0.0 copy-start.3
  5.8 0.0 copy-start.4
  5.8 0.0 copy-start.5
  5.8 0.0 copy-start.6
  5.8 0.9 %slice.3 = bf16[3,32,384]{2,1,0:T(8,128)(2,1)S(1)} slice(bf16[4,32,384]{2,1,0:T(8,128)(2,1)} %refs_3_.1), slice={[1:4], [0:32], [0:384]} | slice | bytes 147456 | tf_op jit(solution)/shard_map/slice | solution.py:418
  6.7 0.0 copy-start
  6.7 0.1 collective-permute-start.1
  6.8 0.6 %collective-permute-start.2 = (bf16[4,32,384]{2,1,0:T(8,128)(2,1)}, bf16[4,32,384]{2,1,0:T(8,128)(2,1)S(1)}, u32[]{:S(2)}, u32[]{:S(2)}) collective-permute-start(bf16[4,32,384]{2,1,0:T(8,128)(2,1)} %refs_3_.1), channel_id=1, source_target_pairs={{0,1},{1,0},{2,3},{3,2},{4,5},{5,4},{6,7},{7,6},{8,9},{9,8},{10,11... | collective-permute-start | bytes 294920 | tf_op jit(solution)/shard_map/ppermute | solution.py:422
  7.4 0.0 copy-start.1
  7.4 0.8 %copy-done.1 = bf16[5,21,21]{2,1,0:T(8,128)(2,1)S(1)} copy-done((bf16[5,21,21]{2,1,0:T(8,128)(2,1)S(1)}, bf16[5,21,21]{2,1,0:T(8,128)(2,1)}, u32[]{:S(2)}) %copy-start.1) | copy-done | bytes 4434
  8.1 0.7 %bands.1 = (bf16[120,1008]{1,0:T(8,128)(2,1)S(1)}, bf16[160,1008]{1,0:T(8,128)(2,1)S(1)}) custom-call(bf16[5,21,21]{2,1,0:T(8,128)(2,1)S(1)} %copy-done.1), custom_call_target="tpu_custom_call" | custom-call | flops 1000000000 | bytes 1000000 | tf_op jit(solution)/shard_map/bands/pallas_call | solution.py:133
  8.8 0.0 copy-done.2
  8.8 0.0 copy-done.3
  8.8 0.0 copy-done.4
  8.8 0.0 copy-done.5
  8.8 0.0 copy-done.6
  8.9 1.0 %factors.1 = (f32[60,56,128]{2,1,0:T(8,128)S(1)}, f32[21,128]{1,0:T(8,128)S(1)}, s32[8,16,128]{2,1,0:T(8,128)S(1)}) custom-call(f32[5,4,6]{2,1,0:T(4,128)S(1)} %bitcast.1, f32[4]{0:T(128)S(1)} %copy-done.3, s32[4]{0:T(128)S(1)} %copy-done.4, s32[4]{0:T(128)S(1)} %copy-done.5, f32[21]{0:T(128)S(1)} %copy-done.6, ...), custom_call_target="tpu_custom_call" | custom-call | flops 100000000 | bytes 1000000 | tf_op jit(solution)/shard_map/factors/pallas_call | solution.py:146
  9.9 3.3 %collective-permute-done.1.refs_1_ = bf16[3,32,384]{2,1,0:T(8,128)(2,1)S(1)} collective-permute-done((bf16[3,32,384]{2,1,0:T(8,128)(2,1)S(1)}, bf16[3,32,384]{2,1,0:T(8,128)(2,1)S(1)}, u32[]{:S(2)}, u32[]{:S(2)}) %collective-permute-start.1) | collective-permute-done | bytes 73760 | tf_op jit(solution)/shard_map/ppermute | solution.py:422
  13.2 0.0 collective-permute-done.2.refs_2_
  13.2 0.0 collective-permute-done.refs_0_
  13.2 0.0 copy-done
  13.2 0.2 %place.1 = (bf16[4,80,384]{2,1,0:T(8,128)(2,1)S(1)}, bf16[80,128]{1,0:T(8,128)(2,1)S(1)}, bf16[80,128]{1,0:T(8,128)(2,1)S(1)}) custom-call(s32[8,16,128]{2,1,0:T(8,128)S(1)} %get-tuple-element.16.span_ref, bf16[4,32,384]{2,1,0:T(8,128)(2,1)S(1)} %collective-permute-done.refs_0_, bf16[3,32,384]{2,1,0:T(8,128)(2,1)S(1)} %collective-permute-done.1.refs_1_, ...), custom_call_target="tpu_custom_call" | custom-call | tf_op jit(solution)/shard_map/place/pallas_call | solution.py:435
  13.4 0.1 collective-permute-start.3
  13.5 1.1 %collective-permute-start.4 = (bf16[80,128]{1,0:T(8,128)(2,1)S(1)}, bf16[80,128]{1,0:T(8,128)(2,1)S(1)}, u32[]{:S(2)}, u32[]{:S(2)}) collective-permute-start(bf16[80,128]{1,0:T(8,128)(2,1)S(1)} %get-tuple-element.21.to_cross_ref), channel_id=1, source_target_pairs={{0,1},{4,8},{8,4},{12,16},{16,12},{20,24},{24,20},{28,29},{1,0},{5... | collective-permute-start | bytes 61448 | tf_op jit(solution)/shard_map/ppermute | solution.py:454
  14.6 2.1 %main.1.inner_ref = f32[56,384]{1,0:T(8,128)S(1)} custom-call(f32[60,56,128]{2,1,0:T(8,128)S(1)} %get-tuple-element.14.factor_ref, bf16[120,1008]{1,0:T(8,128)(2,1)S(1)} %get-tuple-element.12.after_ref.upper_ref, bf16[160,1008]{1,0:T(8,128)(2,1)S(1)} %get-tuple-element.15.lower_ref, bf16[4,80,384]{2,1,0:T(8,128)(2,1)S(1)} %get-tuple-element.19.window_ref), custom_call_target="tpu_custom_call" | custom-call | flops 2000000000 | bytes 1000000 | tf_op jit(solution)/shard_map/main/pallas_call | solution.py:456
  16.7 0.0 collective-permute-done.3.from_core_ref
  16.7 0.7 %collective-permute-done.4.from_cross_ref = bf16[80,128]{1,0:T(8,128)(2,1)S(1)} collective-permute-done((bf16[80,128]{1,0:T(8,128)(2,1)S(1)}, bf16[80,128]{1,0:T(8,128)(2,1)S(1)}, u32[]{:S(2)}, u32[]{:S(2)}) %collective-permute-start.4) | collective-permute-done | bytes 20512 | tf_op jit(solution)/shard_map/ppermute | solution.py:454
  17.3 2.2 %rim.1 = (f32[32,384]{1,0:T(8,128)}, f32[32,384]{1,0:T(8,128)}) custom-call(f32[21,128]{1,0:T(8,128)S(1)} %get-tuple-element.13.taps_ref, f32[60,56,128]{2,1,0:T(8,128)S(1)} %get-tuple-element.14.factor_ref, bf16[120,1008]{1,0:T(8,128)(2,1)S(1)} %get-tuple-element.12.after_ref.upper_ref, bf16[160,1008]{1,0:T(8,128)(2,1)S(1)} %get-tuple-element.15.lower_ref, ...), custom_call_target="tpu_custom_call" | custom-call | tf_op jit(solution)/shard_map/rim/pallas_call | solution.py:467
Async XLA Ops:
  0.6 12.5 %collective-permute-start = (bf16[4,32,384]{2,1,0:T(8,128)(2,1)}, bf16[4,32,384]{2,1,0:T(8,128)(2,1)S(1)}, u32[]{:S(2)}, u32[]{:S(2)}) collective-permute-start(bf16[4,32,384]{2,1,0:T(8,128)(2,1)} %refs_3_.1), channel_id=1, source_target_pairs={{0,3},{1,2},{2,1},{3,0},{4,7},{5,6},{6,5},{7,4},{8,11},{9,10},{10,... | collective-permute-start | bytes 294920 | tf_op jit(solution)/shard_map/ppermute | solution.py:422
  5.7 3.1 %copy-start.2 = (f32[4,5,6]{2,0,1:T(4,128)S(1)}, f32[4,5,6]{2,0,1:T(4,128)}, u32[]{:S(2)}) copy-start(f32[4,5,6]{2,0,1:T(4,128)} %param.9) | copy-start | bytes 1444
  5.7 3.1 %copy-start.3 = (f32[4]{0:T(128)S(1)}, f32[4]{0:T(128)}, u32[]{:S(2)}) copy-start(f32[4]{0:T(128)} %weight_ref.1) | copy-start | bytes 52
  5.8 3.1 %copy-start.4 = (s32[4]{0:T(128)S(1)}, s32[4]{0:T(128)}, u32[]{:S(2)}) copy-start(s32[4]{0:T(128)} %start_ref.1) | copy-start | bytes 52
  5.8 3.1 %copy-start.5 = (s32[4]{0:T(128)S(1)}, s32[4]{0:T(128)}, u32[]{:S(2)}) copy-start(s32[4]{0:T(128)} %count_ref.1) | copy-start | bytes 52
  5.8 3.1 %copy-start.6 = (f32[21]{0:T(128)S(1)}, f32[21]{0:T(128)}, u32[]{:S(2)}) copy-start(f32[21]{0:T(128)} %taps_ref.1) | copy-start | bytes 256
  6.7 6.5 %copy-start = (bf16[4,32,384]{2,1,0:T(8,128)(2,1)S(1)}, bf16[4,32,384]{2,1,0:T(8,128)(2,1)}, u32[]{:S(2)}) copy-start(bf16[4,32,384]{2,1,0:T(8,128)(2,1)} %refs_3_.1) | copy-start | bytes 294916
  6.7 6.4 %collective-permute-start.1 = (bf16[3,32,384]{2,1,0:T(8,128)(2,1)S(1)}, bf16[3,32,384]{2,1,0:T(8,128)(2,1)S(1)}, u32[]{:S(2)}, u32[]{:S(2)}) collective-permute-start(bf16[3,32,384]{2,1,0:T(8,128)(2,1)S(1)} %slice.3), channel_id=1, source_target_pairs={{0,2},{1,3},{2,0},{3,1},{4,6},{5,7},{6,4},{7,5},{8,10},{9,11},{10,... | collective-permute-start | bytes 221192 | tf_op jit(solution)/shard_map/ppermute | solution.py:422
  6.8 6.4 %collective-permute-start.2 = (bf16[4,32,384]{2,1,0:T(8,128)(2,1)}, bf16[4,32,384]{2,1,0:T(8,128)(2,1)S(1)}, u32[]{:S(2)}, u32[]{:S(2)}) collective-permute-start(bf16[4,32,384]{2,1,0:T(8,128)(2,1)} %refs_3_.1), channel_id=1, source_target_pairs={{0,1},{1,0},{2,3},{3,2},{4,5},{5,4},{6,7},{7,6},{8,9},{9,8},{10,11... | collective-permute-start | bytes 294920 | tf_op jit(solution)/shard_map/ppermute | solution.py:422
  7.4 0.8 %copy-start.1 = (bf16[5,21,21]{2,1,0:T(8,128)(2,1)S(1)}, bf16[5,21,21]{2,1,0:T(8,128)(2,1)}, u32[]{:S(2)}) copy-start(bf16[5,21,21]{2,1,0:T(8,128)(2,1)} %basis_ref.1) | copy-start | bytes 13234
  13.4 3.2 %collective-permute-start.3 = (bf16[80,128]{1,0:T(8,128)(2,1)S(1)}, bf16[80,128]{1,0:T(8,128)(2,1)S(1)}, u32[]{:S(2)}, u32[]{:S(2)}) collective-permute-start(bf16[80,128]{1,0:T(8,128)(2,1)S(1)} %get-tuple-element.20.to_core_ref), channel_id=1, source_target_pairs={{0,4},{4,0},{8,12},{12,8},{16,20},{20,16},{24,28},{28,24},{1,5},{5... | collective-permute-start | bytes 61448 | tf_op jit(solution)/shard_map/ppermute | solution.py:453
  13.5 3.8 %collective-permute-start.4 = (bf16[80,128]{1,0:T(8,128)(2,1)S(1)}, bf16[80,128]{1,0:T(8,128)(2,1)S(1)}, u32[]{:S(2)}, u32[]{:S(2)}) collective-permute-start(bf16[80,128]{1,0:T(8,128)(2,1)S(1)} %get-tuple-element.21.to_cross_ref), channel_id=1, source_target_pairs={{0,1},{4,8},{8,4},{12,16},{16,12},{20,24},{24,20},{28,29},{1,0},{5... | collective-permute-start | bytes 61448 | tf_op jit(solution)/shard_map/ppermute | solution.py:454

commit v7 on v6

--- a/solution.py
+++ b/solution.py
@@ -272,15 +272,36 @@
     return (2 * column + 1).astype(jnp.float32) / band_cols - 1.0
 
 
+def filtered(taps_ref, side, tall, tile_rows):
+    half = side // 2
+    width = tall.shape[1]
+    taps = [
+        jnp.broadcast_to(
+            jnp.concatenate([taps_ref[tap : tap + 1, :]] * (width // LANES), axis=1),
+            (tile_rows, width),
+        )
+        for tap in range(side)
+    ]
+    across = taps[0] * tall[:tile_rows, :]
+    for tap in range(1, side):
+        across = across + taps[tap] * tall[tap : tap + tile_rows, :]
+    result = taps[0] * pltpu.roll(across, half, 1)
+    for tap in range(1, side):
+        result = result + taps[tap] * pltpu.roll(across, (half - tap) % width, 1)
+    return result
+
+
 def main_kernel(
     wide_peers,
     side,
     tile_rows,
+    taps_ref,
     factor_ref,
     upper_ref,
     lower_ref,
     window_ref,
     out_ref,
+    inner_detection_ref,
     upper_patches,
     lower_patches,
 ):
@@ -307,6 +328,7 @@
     )
     x_coord = column_position(column, wide_peers * tile_cols)[:1]
     out_ref[...] = sums[0] + x_coord * (sums[1] + x_coord * sums[2])
+    inner_detection_ref[...] = filtered(taps_ref, side, out_ref, tile_rows)
 
 
 def rim_kernel(
@@ -318,6 +340,7 @@
     upper_ref,
     lower_ref,
     inner_ref,
+    inner_detection_ref,
     to_core_ref,
     to_cross_ref,
     from_core_ref,
@@ -372,32 +395,34 @@
     border = sums[0] + x_coord * (sums[1] + x_coord * sums[2])
     border = jnp.where((column >= 0) & (column < band_cols), border, 0.0)
 
-    width = tile_cols + LANES
-    head = pltpu.roll(border, LANES - rim, 1)
-    tail = pltpu.roll(border, LANES - 3 * rim, 1)
-    left = pltpu.roll(border, LANES - rim, 1)
-    right = pltpu.roll(border, LANES - 3 * rim, 1)
-    tall[:, :LANES] = jnp.where(lane < half, head, inner_ref[:, :LANES])
-    tall[:, LANES : tile_cols - LANES] = inner_ref[:, LANES : tile_cols - LANES]
-    tall[:, tile_cols - LANES : tile_cols] = jnp.where(
-        lane >= LANES - half, tail, inner_ref[:, tile_cols - LANES :]
+    middle = LANES // 2
+    first_inner = inner_ref[:, :LANES]
+    last_inner = inner_ref[:, tile_cols - LANES :]
+    edge = jnp.where(
+        lane < middle,
+        jnp.where(lane < rim + half, border, pltpu.roll(first_inner, rim, 1)),
+        jnp.where(
+            lane >= LANES - rim - half,
+            pltpu.roll(border, LANES - 4 * rim, 1),
+            pltpu.roll(last_inner, LANES - rim, 1),
+        ),
     )
-    tall[:, tile_cols:] = jnp.where(lane < LANES // 2, right, left)
-    coadd_ref[...] = tall[half : half + tile_rows, :tile_cols]
-    taps = [
-        jnp.broadcast_to(
-            jnp.concatenate([taps_ref[tap : tap + 1, :]] * (width // LANES), axis=1),
-            (tile_rows, width),
+    tall[...] = edge
+    coadd_ref[...] = inner_ref[half : half + tile_rows, :]
+    edge_detection = filtered(taps_ref, side, tall, tile_rows)
+    edge_coadd = tall[half : half + tile_rows, :]
+    detection_ref[...] = inner_detection_ref[...]
+    lane = lane[:tile_rows]
+    for out_ref, values, reach in (
+        (coadd_ref, edge_coadd, half),
+        (detection_ref, edge_detection, rim),
+    ):
+        head = pltpu.roll(values, LANES - rim, 1)
+        tail = pltpu.roll(values, rim, 1)
+        out_ref[:, :LANES] = jnp.where(lane < reach, head, out_ref[:, :LANES])
+        out_ref[:, tile_cols - LANES :] = jnp.where(
+            lane >= LANES - reach, tail, out_ref[:, tile_cols - LANES :]
         )
-        for tap in range(side)
-    ]
-    filtered = taps[0] * tall[:tile_rows, :]
-    for tap in range(1, side):
-        filtered = filtered + taps[tap] * tall[tap : tap + tile_rows, :]
-    detection = taps[0] * pltpu.roll(filtered, half, 1)
-    for tap in range(1, side):
-        detection = detection + taps[tap] * pltpu.roll(filtered, (half - tap) % width, 1)
-    detection_ref[...] = detection[:, :tile_cols]
 
 
 def on_device(
@@ -415,11 +440,9 @@
 
     sent = [skipped(index) for index in range(peers)]
     tiles = [exposures] * peers
-    moving, latter = lax.optimization_barrier((exposures, exposures[1:]))
     for index in reversed(range(1, peers)):
         pairs = [(i, i ^ index) for i in range(peers)]
-        whole = moving if index == 1 else exposures
-        tiles[index] = lax.ppermute(latter if sent[index] else whole, "narrow", pairs)
+        tiles[index] = lax.ppermute(exposures[sent[index] :], "narrow", pairs)
     taps, span, tables = prepared(
         basis_kernels,
         poly_coef,
@@ -453,30 +476,33 @@
     from_core = lax.ppermute(to_core, "wide", core_pairs)
     from_cross = lax.ppermute(to_cross, ("wide", "narrow"), cross_pairs)
 
-    inner = pl.pallas_call(
+    inner, inner_detection = pl.pallas_call(
         functools.partial(main_kernel, wide_peers, side, tile_rows),
-        out_shape=jax.ShapeDtypeStruct((out_rows, tile_cols), jnp.float32),
-        in_specs=[vmem] * 4,
-        out_specs=vmem,
+        out_shape=(
+            jax.ShapeDtypeStruct((out_rows, tile_cols), jnp.float32),
+            jax.ShapeDtypeStruct((tile_rows, tile_cols), jnp.float32),
+        ),
+        in_specs=[vmem] * 5,
+        out_specs=(vmem, vmem),
         scratch_shapes=[pltpu.VMEM((members // 2, depth, 2 * tile_cols), jnp.bfloat16)] * 2,
         compiler_params=params,
         cost_estimate=pl.CostEstimate(flops=2 * 10**9, bytes_accessed=10**6, transcendentals=0),
         name="main",
-    )(*tables, window)
+    )(taps, *tables, window)
     out = jax.ShapeDtypeStruct((tile_rows, tile_cols), jnp.float32)
     return pl.pallas_call(
         functools.partial(rim_kernel, wide_peers, side, members),
         out_shape=(out, out),
-        in_specs=[vmem] * 9,
+        in_specs=[vmem] * 10,
         out_specs=(vmem, vmem),
         scratch_shapes=[
             pltpu.VMEM((depth, members * LANES), jnp.bfloat16),
             pltpu.VMEM((depth, members * LANES), jnp.bfloat16),
-            pltpu.VMEM((out_rows, tile_cols + LANES), jnp.float32),
+            pltpu.VMEM((out_rows, LANES), jnp.float32),
         ],
         compiler_params=params,
         name="rim",
-    )(taps, *tables, inner, to_core, to_cross, from_core, from_cross)
+    )(taps, *tables, inner, inner_detection, to_core, to_cross, from_core, from_cross)
 
 
 def solution(mesh):

time: 19.7 us -> 19 us (0.964)
  waiting for transfers between devices: 3.98 us -> 2.66 us
  starting transfers between devices: 6.92 us -> 7.39 us
    ppermute x3, waiting for transfers between devices: 3.32 us -> 2.66 us  [on_device(): tiles[index] = lax.ppermute(exposures[sent[index]:], 'narrow', pairs)]
    ppermute x1, waiting for transfers between devices: 0.66 us -> 0.01 us  [on_device(): from_cross = lax.ppermute(to_cross, ('wide', 'narrow'), cross_pairs)]
    ppermute x1, starting transfers between devices: 1.11 us -> 1.53 us  [on_device(): from_cross = lax.ppermute(to_cross, ('wide', 'narrow'), cross_pairs)]
    pallas_call x1, Pallas kernels: 2.06 us -> 2.43 us  [on_device(): pl.pallas_call(functools.partial(main_kernel, wide_peers, side, tile_rows...]
    pallas_call x1, Pallas kernels: 2.21 us -> 1.88 us  [on_device(): pl.pallas_call(functools.partial(rim_kernel, wide_peers, side, members),...]
  transfers between devices with their start and end apart: 5 -> 5, of which waited for: 2 -> 1; matrix products, arithmetic and copies ran while one was open for 5% -> 5% of each run, Pallas kernels for 19% -> 22%
where the time goes in v7:
time: 19 us; the launch traced here: 18.7 us
  starting transfers between devices  7.39 us (39%)
  Pallas kernels  6.2 us (33%)
  waiting for transfers between devices  2.66 us (14%)
  local copies, waits for them, and re-layouts  1.73 us (9%)
  between operations  0.74 us (4%)
    ppermute x3, starting transfers between devices, on_device(): tiles[index] = lax.ppermute(exposures[sent[index]:], 'narrow', pairs)  5.79 us
    ppermute x3, waiting for transfers between devices, on_device(): tiles[index] = lax.ppermute(exposures[sent[index]:], 'narrow', pairs)  2.66 us
    pallas_call x1, Pallas kernels, on_device(): pl.pallas_call(functools.partial(main_kernel, wide_peers, side, tile_rows...  2.43 us
    pallas_call x1, Pallas kernels, on_device(): pl.pallas_call(functools.partial(rim_kernel, wide_peers, side, members),...  1.88 us
    ppermute x1, starting transfers between devices, on_device(): from_cross = lax.ppermute(to_cross, ('wide', 'narrow'), cross_pairs)  1.53 us
    pallas_call x1, Pallas kernels, prepared(): pl.pallas_call(functools.partial(factors_kernel, tile_rows, band_rows, ha...  1 us
    slice x1, local copies, waits for them, and re-layouts, on_device(): tiles[index] = lax.ppermute(exposures[sent[index]:], 'narrow', pairs)  0.96 us
    unnamed x14, local copies, waits for them, and re-layouts  0.78 us
  transfers between devices with their start and end apart: 5, of which 1 were waited for; matrix products, arithmetic and copies ran while one was open for 5% of the time, Pallas kernels for 22%

profile of v7, /device:TPU:0, one launch (start us, length us, event | category | flops | bytes accessed | tf_op | source)
XLA Modules:
  0.0 18.7 jit_solution(18138430426879004157)
XLA Ops:
  0.6 5.1 %collective-permute-start = (bf16[4,32,384]{2,1,0:T(8,128)(2,1)}, bf16[4,32,384]{2,1,0:T(8,128)(2,1)S(1)}, u32[]{:S(2)}, u32[]{:S(2)}) collective-permute-start(bf16[4,32,384]{2,1,0:T(8,128)(2,1)} %refs_3_.1), channel_id=1, source_target_pairs={{0,3},{1,2},{2,1},{3,0},{4,7},{5,6},{6,5},{7,4},{8,11},{9,10},{10,... | collective-permute-start | bytes 294920 | tf_op jit(solution)/shard_map/ppermute | solution.py:445
  5.7 0.0 collective-permute-start.2
  5.7 1.0 %slice.3 = bf16[3,32,384]{2,1,0:T(8,128)(2,1)S(1)} slice(bf16[4,32,384]{2,1,0:T(8,128)(2,1)} %refs_3_.1), slice={[1:4], [0:32], [0:384]} | slice | bytes 147456 | tf_op jit(solution)/shard_map/slice | solution.py:445
  6.7 0.0 copy-start
  6.7 0.7 %collective-permute-start.1 = (bf16[3,32,384]{2,1,0:T(8,128)(2,1)S(1)}, bf16[3,32,384]{2,1,0:T(8,128)(2,1)S(1)}, u32[]{:S(2)}, u32[]{:S(2)}) collective-permute-start(bf16[3,32,384]{2,1,0:T(8,128)(2,1)S(1)} %slice.3), channel_id=1, source_target_pairs={{0,2},{1,3},{2,0},{3,1},{4,6},{5,7},{6,4},{7,5},{8,10},{9,11},{10,... | collective-permute-start | bytes 221192 | tf_op jit(solution)/shard_map/ppermute | solution.py:445
  7.4 0.0 copy-start.1
  7.4 0.8 %copy-done.1 = bf16[5,21,21]{2,1,0:T(8,128)(2,1)S(1)} copy-done((bf16[5,21,21]{2,1,0:T(8,128)(2,1)S(1)}, bf16[5,21,21]{2,1,0:T(8,128)(2,1)}, u32[]{:S(2)}) %copy-start.1) | copy-done | bytes 4434
  8.1 0.0 copy-start.2
  8.1 0.0 copy-start.3
  8.1 0.0 copy-start.4
  8.1 0.0 copy-start.5
  8.2 0.0 copy-start.6
  8.2 0.7 %bands.1 = (bf16[120,1008]{1,0:T(8,128)(2,1)S(1)}, bf16[160,1008]{1,0:T(8,128)(2,1)S(1)}) custom-call(bf16[5,21,21]{2,1,0:T(8,128)(2,1)S(1)} %copy-done.1), custom_call_target="tpu_custom_call" | custom-call | flops 1000000000 | bytes 1000000 | tf_op jit(solution)/shard_map/bands/pallas_call | solution.py:133
  8.8 0.0 copy-done.2
  8.9 0.0 copy-done.3
  8.9 0.0 copy-done.4
  8.9 0.0 copy-done.5
  8.9 0.0 copy-done.6
  8.9 1.0 %factors.1 = (f32[60,56,128]{2,1,0:T(8,128)S(1)}, f32[21,128]{1,0:T(8,128)S(1)}, s32[8,16,128]{2,1,0:T(8,128)S(1)}) custom-call(f32[5,4,6]{2,1,0:T(4,128)S(1)} %bitcast.1, f32[4]{0:T(128)S(1)} %copy-done.3, s32[4]{0:T(128)S(1)} %copy-done.4, s32[4]{0:T(128)S(1)} %copy-done.5, f32[21]{0:T(128)S(1)} %copy-done.6, ...), custom_call_target="tpu_custom_call" | custom-call | flops 100000000 | bytes 1000000 | tf_op jit(solution)/shard_map/factors/pallas_call | solution.py:146
  9.9 2.7 %collective-permute-done.1.refs_1_ = bf16[3,32,384]{2,1,0:T(8,128)(2,1)S(1)} collective-permute-done((bf16[3,32,384]{2,1,0:T(8,128)(2,1)S(1)}, bf16[3,32,384]{2,1,0:T(8,128)(2,1)S(1)}, u32[]{:S(2)}, u32[]{:S(2)}) %collective-permute-start.1) | collective-permute-done | bytes 73760 | tf_op jit(solution)/shard_map/ppermute | solution.py:445
  12.6 0.0 collective-permute-done.refs_0_
  12.6 0.0 collective-permute-done.2.refs_2_
  12.6 0.0 copy-done
  12.6 0.2 %place.1 = (bf16[4,80,384]{2,1,0:T(8,128)(2,1)S(1)}, bf16[80,128]{1,0:T(8,128)(2,1)S(1)}, bf16[80,128]{1,0:T(8,128)(2,1)S(1)}) custom-call(s32[8,16,128]{2,1,0:T(8,128)S(1)} %get-tuple-element.16.span_ref, bf16[4,32,384]{2,1,0:T(8,128)(2,1)S(1)} %collective-permute-done.refs_0_, bf16[3,32,384]{2,1,0:T(8,128)(2,1)S(1)} %collective-permute-done.1.refs_1_, ...), custom_call_target="tpu_custom_call" | custom-call | tf_op jit(solution)/shard_map/place/pallas_call | solution.py:458
  12.8 0.1 collective-permute-start.3
  12.9 1.5 %collective-permute-start.4 = (bf16[80,128]{1,0:T(8,128)(2,1)S(1)}, bf16[80,128]{1,0:T(8,128)(2,1)S(1)}, u32[]{:S(2)}, u32[]{:S(2)}) collective-permute-start(bf16[80,128]{1,0:T(8,128)(2,1)S(1)} %get-tuple-element.21.to_cross_ref), channel_id=1, source_target_pairs={{0,1},{4,8},{8,4},{12,16},{16,12},{20,24},{24,20},{28,29},{1,0},{5... | collective-permute-start | bytes 61448 | tf_op jit(solution)/shard_map/ppermute | solution.py:477
  14.4 2.4 %main.1 = (f32[56,384]{1,0:T(8,128)S(1)}, f32[32,384]{1,0:T(8,128)S(1)}) custom-call(f32[21,128]{1,0:T(8,128)S(1)} %get-tuple-element.13.taps_ref, f32[60,56,128]{2,1,0:T(8,128)S(1)} %get-tuple-element.14.factor_ref, bf16[120,1008]{1,0:T(8,128)(2,1)S(1)} %get-tuple-element.12.after_ref.upper_ref, bf16[160,1008]{1,0:T(8,128)(2,1)S(1)} %get-tuple-element.15.lower_ref, ...), custom_call_target="tpu_custom_call" | custom-call | flops 2000000000 | bytes 1000000 | tf_op jit(solution)/shard_map/main/pallas_call | solution.py:479
  16.8 0.0 collective-permute-done.3.from_core_ref
  16.8 0.0 collective-permute-done.4.from_cross_ref
  16.8 1.9 %rim.1 = (f32[32,384]{1,0:T(8,128)}, f32[32,384]{1,0:T(8,128)}) custom-call(f32[21,128]{1,0:T(8,128)S(1)} %get-tuple-element.13.taps_ref, f32[60,56,128]{2,1,0:T(8,128)S(1)} %get-tuple-element.14.factor_ref, bf16[120,1008]{1,0:T(8,128)(2,1)S(1)} %get-tuple-element.12.after_ref.upper_ref, bf16[160,1008]{1,0:T(8,128)(2,1)S(1)} %get-tuple-element.15.lower_ref, ...), custom_call_target="tpu_custom_call" | custom-call | tf_op jit(solution)/shard_map/rim/pallas_call | solution.py:493
Async XLA Ops:
  0.6 11.9 %collective-permute-start = (bf16[4,32,384]{2,1,0:T(8,128)(2,1)}, bf16[4,32,384]{2,1,0:T(8,128)(2,1)S(1)}, u32[]{:S(2)}, u32[]{:S(2)}) collective-permute-start(bf16[4,32,384]{2,1,0:T(8,128)(2,1)} %refs_3_.1), channel_id=1, source_target_pairs={{0,3},{1,2},{2,1},{3,0},{4,7},{5,6},{6,5},{7,4},{8,11},{9,10},{10,... | collective-permute-start | bytes 294920 | tf_op jit(solution)/shard_map/ppermute | solution.py:445
  5.7 6.8 %collective-permute-start.2 = (bf16[4,32,384]{2,1,0:T(8,128)(2,1)}, bf16[4,32,384]{2,1,0:T(8,128)(2,1)S(1)}, u32[]{:S(2)}, u32[]{:S(2)}) collective-permute-start(bf16[4,32,384]{2,1,0:T(8,128)(2,1)} %refs_3_.1), channel_id=1, source_target_pairs={{0,1},{1,0},{2,3},{3,2},{4,5},{5,4},{6,7},{7,6},{8,9},{9,8},{10,11... | collective-permute-start | bytes 294920 | tf_op jit(solution)/shard_map/ppermute | solution.py:445
  6.7 5.9 %copy-start = (bf16[4,32,384]{2,1,0:T(8,128)(2,1)S(1)}, bf16[4,32,384]{2,1,0:T(8,128)(2,1)}, u32[]{:S(2)}) copy-start(bf16[4,32,384]{2,1,0:T(8,128)(2,1)} %refs_3_.1) | copy-start | bytes 294916
  6.7 5.8 %collective-permute-start.1 = (bf16[3,32,384]{2,1,0:T(8,128)(2,1)S(1)}, bf16[3,32,384]{2,1,0:T(8,128)(2,1)S(1)}, u32[]{:S(2)}, u32[]{:S(2)}) collective-permute-start(bf16[3,32,384]{2,1,0:T(8,128)(2,1)S(1)} %slice.3), channel_id=1, source_target_pairs={{0,2},{1,3},{2,0},{3,1},{4,6},{5,7},{6,4},{7,5},{8,10},{9,11},{10,... | collective-permute-start | bytes 221192 | tf_op jit(solution)/shard_map/ppermute | solution.py:445
  7.4 0.8 %copy-start.1 = (bf16[5,21,21]{2,1,0:T(8,128)(2,1)S(1)}, bf16[5,21,21]{2,1,0:T(8,128)(2,1)}, u32[]{:S(2)}) copy-start(bf16[5,21,21]{2,1,0:T(8,128)(2,1)} %basis_ref.1) | copy-start | bytes 13234
  8.1 0.7 %copy-start.2 = (f32[4,5,6]{2,0,1:T(4,128)S(1)}, f32[4,5,6]{2,0,1:T(4,128)}, u32[]{:S(2)}) copy-start(f32[4,5,6]{2,0,1:T(4,128)} %param.9) | copy-start | bytes 1444
  8.1 0.7 %copy-start.3 = (f32[4]{0:T(128)S(1)}, f32[4]{0:T(128)}, u32[]{:S(2)}) copy-start(f32[4]{0:T(128)} %weight_ref.1) | copy-start | bytes 52
  8.1 0.7 %copy-start.4 = (s32[4]{0:T(128)S(1)}, s32[4]{0:T(128)}, u32[]{:S(2)}) copy-start(s32[4]{0:T(128)} %start_ref.1) | copy-start | bytes 52
  8.1 0.7 %copy-start.5 = (s32[4]{0:T(128)S(1)}, s32[4]{0:T(128)}, u32[]{:S(2)}) copy-start(s32[4]{0:T(128)} %count_ref.1) | copy-start | bytes 52
  8.2 0.7 %copy-start.6 = (f32[21]{0:T(128)S(1)}, f32[21]{0:T(128)}, u32[]{:S(2)}) copy-start(f32[21]{0:T(128)} %taps_ref.1) | copy-start | bytes 256
  12.8 4.0 %collective-permute-start.3 = (bf16[80,128]{1,0:T(8,128)(2,1)S(1)}, bf16[80,128]{1,0:T(8,128)(2,1)S(1)}, u32[]{:S(2)}, u32[]{:S(2)}) collective-permute-start(bf16[80,128]{1,0:T(8,128)(2,1)S(1)} %get-tuple-element.20.to_core_ref), channel_id=1, source_target_pairs={{0,4},{4,0},{8,12},{12,8},{16,20},{20,16},{24,28},{28,24},{1,5},{5... | collective-permute-start | bytes 61448 | tf_op jit(solution)/shard_map/ppermute | solution.py:476
  12.9 4.0 %collective-permute-start.4 = (bf16[80,128]{1,0:T(8,128)(2,1)S(1)}, bf16[80,128]{1,0:T(8,128)(2,1)S(1)}, u32[]{:S(2)}, u32[]{:S(2)}) collective-permute-start(bf16[80,128]{1,0:T(8,128)(2,1)S(1)} %get-tuple-element.21.to_cross_ref), channel_id=1, source_target_pairs={{0,1},{4,8},{8,4},{12,16},{16,12},{20,24},{24,20},{28,29},{1,0},{5... | collective-permute-start | bytes 61448 | tf_op jit(solution)/shard_map/ppermute | solution.py:477

commit v8 on v7

--- a/solution.py
+++ b/solution.py
@@ -59,7 +59,18 @@
     factor_ref,
     spread_ref,
     span_ref,
+    rows_ref,
 ):
+    wide = lax.broadcasted_iota(jnp.int32, (8, LANES), 1)
+    line = jnp.zeros((8, LANES), jnp.float32)
+    for tap in range(taps_ref.shape[0]):
+        line = jnp.where(wide == tap, taps_ref[tap], line)
+    tile = pltpu.roll(line, 0, 1, stride=1, stride_axis=0)
+    grid = [pltpu.roll(tile, first, 1) for first in range(0, rows_ref.shape[0] // 2, 8)]
+    grid = jnp.concatenate(grid, axis=0)
+    high = grid.astype(jnp.bfloat16).astype(jnp.float32)
+    both = high + pltpu.roll(high, LANES // 2, 1)
+    rows_ref[...] = jnp.concatenate([both, grid - high], axis=0).astype(jnp.bfloat16)
     for tap in range(taps_ref.shape[0]):
         spread_ref[tap : tap + 1, :] = jnp.full((1, LANES), taps_ref[tap], jnp.float32)
     for member in range(start_ref.shape[0]):
@@ -143,20 +154,21 @@
         cost_estimate=pl.CostEstimate(flops=10**9, bytes_accessed=10**6, transcendentals=0),
         name="bands",
     )(basis_kernels)
-    factors, spread, span = pl.pallas_call(
+    factors, spread, span, rows = pl.pallas_call(
         functools.partial(factors_kernel, tile_rows, band_rows, half),
         out_shape=(
             jax.ShapeDtypeStruct((3 * members * kernel_total, out_rows, LANES), jnp.float32),
             jax.ShapeDtypeStruct((side, LANES), jnp.float32),
             jax.ShapeDtypeStruct((2 * members, 16, LANES), jnp.int32),
+            jax.ShapeDtypeStruct((2 * tile_rows, LANES), jnp.bfloat16),
         ),
         in_specs=[smem] * 5 + [pl.BlockSpec(memory_space=pl.ANY)],
-        out_specs=(vmem, vmem, vmem),
+        out_specs=(vmem, vmem, vmem, vmem),
         compiler_params=params,
         cost_estimate=pl.CostEstimate(flops=10**8, bytes_accessed=10**6, transcendentals=0),
         name="factors",
     )(poly_coef.transpose(1, 0, 2), weight, start, count, taps, upper)
-    return spread, span, (factors, upper, lower)
+    return (spread, rows), span, (factors, upper, lower)
 
 
 def part_rows_of(moved):
@@ -272,7 +284,7 @@
     return (2 * column + 1).astype(jnp.float32) / band_cols - 1.0
 
 
-def filtered(taps_ref, side, tall, tile_rows):
+def filtered(taps_ref, rows_ref, side, tall, tile_rows):
     half = side // 2
     width = tall.shape[1]
     taps = [
@@ -282,9 +294,19 @@
         )
         for tap in range(side)
     ]
-    across = taps[0] * tall[:tile_rows, :]
-    for tap in range(1, side):
-        across = across + taps[tap] * tall[tap : tap + tile_rows, :]
+    if rows_ref is None:
+        across = taps[0] * tall[:tile_rows, :]
+        for tap in range(1, side):
+            across = across + taps[tap] * tall[tap : tap + tile_rows, :]
+    else:
+        coadded = jnp.concatenate(
+            [tall, jnp.zeros((LANES // 2 - tall.shape[0], width), jnp.float32)], axis=0
+        )
+        high = coadded.astype(jnp.bfloat16)
+        low = (coadded - high.astype(jnp.float32)).astype(jnp.bfloat16)
+        split = jnp.concatenate([high, low], axis=0)
+        across = jnp.dot(rows_ref[...], split, preferred_element_type=jnp.float32)
+        across = across[:tile_rows] + across[tile_rows:]
     result = taps[0] * pltpu.roll(across, half, 1)
     for tap in range(1, side):
         result = result + taps[tap] * pltpu.roll(across, (half - tap) % width, 1)
@@ -296,6 +318,7 @@
     side,
     tile_rows,
     taps_ref,
+    rows_ref,
     factor_ref,
     upper_ref,
     lower_ref,
@@ -327,8 +350,9 @@
         jnp.int32, (8, tile_cols), 1
     )
     x_coord = column_position(column, wide_peers * tile_cols)[:1]
-    out_ref[...] = sums[0] + x_coord * (sums[1] + x_coord * sums[2])
-    inner_detection_ref[...] = filtered(taps_ref, side, out_ref, tile_rows)
+    coadded = sums[0] + x_coord * (sums[1] + x_coord * sums[2])
+    out_ref[...] = coadded
+    inner_detection_ref[...] = filtered(taps_ref, rows_ref, side, coadded, tile_rows)
 
 
 def rim_kernel(
@@ -409,7 +433,7 @@
     )
     tall[...] = edge
     coadd_ref[...] = inner_ref[half : half + tile_rows, :]
-    edge_detection = filtered(taps_ref, side, tall, tile_rows)
+    edge_detection = filtered(taps_ref, None, side, tall, tile_rows)
     edge_coadd = tall[half : half + tile_rows, :]
     detection_ref[...] = inner_detection_ref[...]
     lane = lane[:tile_rows]
@@ -482,13 +506,13 @@
             jax.ShapeDtypeStruct((out_rows, tile_cols), jnp.float32),
             jax.ShapeDtypeStruct((tile_rows, tile_cols), jnp.float32),
         ),
-        in_specs=[vmem] * 5,
+        in_specs=[vmem] * 6,
         out_specs=(vmem, vmem),
         scratch_shapes=[pltpu.VMEM((members // 2, depth, 2 * tile_cols), jnp.bfloat16)] * 2,
         compiler_params=params,
         cost_estimate=pl.CostEstimate(flops=2 * 10**9, bytes_accessed=10**6, transcendentals=0),
         name="main",
-    )(taps, *tables, window)
+    )(*taps, *tables, window)
     out = jax.ShapeDtypeStruct((tile_rows, tile_cols), jnp.float32)
     return pl.pallas_call(
         functools.partial(rim_kernel, wide_peers, side, members),
@@ -502,7 +526,7 @@
         ],
         compiler_params=params,
         name="rim",
-    )(taps, *tables, inner, inner_detection, to_core, to_cross, from_core, from_cross)
+    )(taps[0], *tables, inner, inner_detection, to_core, to_cross, from_core, from_cross)
 
 
 def solution(mesh):

time: 19 us -> 18.9 us (level)
  no operation moved by 1% of the time
where the time goes in v8:
time: 18.9 us; the launch traced here: 18.7 us
  starting transfers between devices  7.39 us (39%)
  Pallas kernels  6.26 us (33%)
  waiting for transfers between devices  2.54 us (13%)
  local copies, waits for them, and re-layouts  1.73 us (9%)
  between operations  0.74 us (4%)
    ppermute x3, starting transfers between devices, on_device(): tiles[index] = lax.ppermute(exposures[sent[index]:], 'narrow', pairs)  5.79 us
    ppermute x3, waiting for transfers between devices, on_device(): tiles[index] = lax.ppermute(exposures[sent[index]:], 'narrow', pairs)  2.54 us
    pallas_call x1, Pallas kernels, on_device(): pl.pallas_call(functools.partial(main_kernel, wide_peers, side, tile_rows...  2.36 us
    pallas_call x1, Pallas kernels, on_device(): pl.pallas_call(functools.partial(rim_kernel, wide_peers, side, members),...  1.87 us
    ppermute x1, starting transfers between devices, on_device(): from_cross = lax.ppermute(to_cross, ('wide', 'narrow'), cross_pairs)  1.53 us
    pallas_call x1, Pallas kernels, prepared(): pl.pallas_call(functools.partial(factors_kernel, tile_rows, band_rows, ha...  1.12 us
    slice x1, local copies, waits for them, and re-layouts, on_device(): tiles[index] = lax.ppermute(exposures[sent[index]:], 'narrow', pairs)  0.96 us
    unnamed x14, local copies, waits for them, and re-layouts  0.78 us
  transfers between devices with their start and end apart: 5, of which 1 were waited for; matrix products, arithmetic and copies ran while one was open for 5% of the time, Pallas kernels for 22%

profile of v8, /device:TPU:0, one launch (start us, length us, event | category | flops | bytes accessed | tf_op | source)
XLA Modules:
  0.0 18.7 jit_solution(15992252270017650667)
XLA Ops:
  0.6 5.1 %collective-permute-start = (bf16[4,32,384]{2,1,0:T(8,128)(2,1)}, bf16[4,32,384]{2,1,0:T(8,128)(2,1)S(1)}, u32[]{:S(2)}, u32[]{:S(2)}) collective-permute-start(bf16[4,32,384]{2,1,0:T(8,128)(2,1)} %refs_3_.1), channel_id=1, source_target_pairs={{0,3},{1,2},{2,1},{3,0},{4,7},{5,6},{6,5},{7,4},{8,11},{9,10},{10,... | collective-permute-start | bytes 294920 | tf_op jit(solution)/shard_map/ppermute | solution.py:469
  5.7 0.0 collective-permute-start.2
  5.7 1.0 %slice.3 = bf16[3,32,384]{2,1,0:T(8,128)(2,1)S(1)} slice(bf16[4,32,384]{2,1,0:T(8,128)(2,1)} %refs_3_.1), slice={[1:4], [0:32], [0:384]} | slice | bytes 147456 | tf_op jit(solution)/shard_map/slice | solution.py:469
  6.7 0.0 copy-start
  6.7 0.7 %collective-permute-start.1 = (bf16[3,32,384]{2,1,0:T(8,128)(2,1)S(1)}, bf16[3,32,384]{2,1,0:T(8,128)(2,1)S(1)}, u32[]{:S(2)}, u32[]{:S(2)}) collective-permute-start(bf16[3,32,384]{2,1,0:T(8,128)(2,1)S(1)} %slice.3), channel_id=1, source_target_pairs={{0,2},{1,3},{2,0},{3,1},{4,6},{5,7},{6,4},{7,5},{8,10},{9,11},{10,... | collective-permute-start | bytes 221192 | tf_op jit(solution)/shard_map/ppermute | solution.py:469
  7.4 0.0 copy-start.1
  7.4 0.8 %copy-done.1 = bf16[5,21,21]{2,1,0:T(8,128)(2,1)S(1)} copy-done((bf16[5,21,21]{2,1,0:T(8,128)(2,1)S(1)}, bf16[5,21,21]{2,1,0:T(8,128)(2,1)}, u32[]{:S(2)}) %copy-start.1) | copy-done | bytes 4434
  8.1 0.0 copy-start.2
  8.1 0.0 copy-start.3
  8.1 0.0 copy-start.4
  8.1 0.0 copy-start.5
  8.2 0.0 copy-start.6
  8.2 0.7 %bands.1 = (bf16[120,1008]{1,0:T(8,128)(2,1)S(1)}, bf16[160,1008]{1,0:T(8,128)(2,1)S(1)}) custom-call(bf16[5,21,21]{2,1,0:T(8,128)(2,1)S(1)} %copy-done.1), custom_call_target="tpu_custom_call" | custom-call | flops 1000000000 | bytes 1000000 | tf_op jit(solution)/shard_map/bands/pallas_call | solution.py:144
  8.8 0.0 copy-done.2
  8.9 0.0 copy-done.3
  8.9 0.0 copy-done.4
  8.9 0.0 copy-done.5
  8.9 0.0 copy-done.6
  8.9 1.1 %factors.1 = (f32[60,56,128]{2,1,0:T(8,128)S(1)}, f32[21,128]{1,0:T(8,128)S(1)}, s32[8,16,128]{2,1,0:T(8,128)S(1)}, bf16[64,128]{1,0:T(8,128)(2,1)S(1)}) custom-call(f32[5,4,6]{2,1,0:T(4,128)S(1)} %bitcast.1, f32[4]{0:T(128)S(1)} %copy-done.3, s32[4]{0:T(128)S(1)} %copy-done.4, s32[4]{0:T(128)S(1)} %copy-done.5, f32[21]{0:T(128)S(1)} %copy-done.6, ...), custom_call_target="tpu_custom_call" | custom-call | flops 100000000 | bytes 1000000 | tf_op jit(solution)/shard_map/factors/pallas_call | solution.py:157
  10.0 2.5 %collective-permute-done.1.refs_1_ = bf16[3,32,384]{2,1,0:T(8,128)(2,1)S(1)} collective-permute-done((bf16[3,32,384]{2,1,0:T(8,128)(2,1)S(1)}, bf16[3,32,384]{2,1,0:T(8,128)(2,1)S(1)}, u32[]{:S(2)}, u32[]{:S(2)}) %collective-permute-start.1) | collective-permute-done | bytes 73760 | tf_op jit(solution)/shard_map/ppermute | solution.py:469
  12.6 0.0 collective-permute-done.refs_0_
  12.6 0.0 collective-permute-done.2.refs_2_
  12.6 0.0 copy-done
  12.6 0.2 %place.1 = (bf16[4,80,384]{2,1,0:T(8,128)(2,1)S(1)}, bf16[80,128]{1,0:T(8,128)(2,1)S(1)}, bf16[80,128]{1,0:T(8,128)(2,1)S(1)}) custom-call(s32[8,16,128]{2,1,0:T(8,128)S(1)} %get-tuple-element.18.span_ref, bf16[4,32,384]{2,1,0:T(8,128)(2,1)S(1)} %collective-permute-done.refs_0_, bf16[3,32,384]{2,1,0:T(8,128)(2,1)S(1)} %collective-permute-done.1.refs_1_, ...), custom_call_target="tpu_custom_call" | custom-call | tf_op jit(solution)/shard_map/place/pallas_call | solution.py:482
  12.8 0.1 collective-permute-start.3
  12.9 1.5 %collective-permute-start.4 = (bf16[80,128]{1,0:T(8,128)(2,1)S(1)}, bf16[80,128]{1,0:T(8,128)(2,1)S(1)}, u32[]{:S(2)}, u32[]{:S(2)}) collective-permute-start(bf16[80,128]{1,0:T(8,128)(2,1)S(1)} %get-tuple-element.23.to_cross_ref), channel_id=1, source_target_pairs={{0,1},{4,8},{8,4},{12,16},{16,12},{20,24},{24,20},{28,29},{1,0},{5... | collective-permute-start | bytes 61448 | tf_op jit(solution)/shard_map/ppermute | solution.py:501
  14.4 2.4 %main.1 = (f32[56,384]{1,0:T(8,128)S(1)}, f32[32,384]{1,0:T(8,128)S(1)}) custom-call(f32[21,128]{1,0:T(8,128)S(1)} %get-tuple-element.14.taps_ref, bf16[64,128]{1,0:T(8,128)(2,1)S(1)} %get-tuple-element.17.rows_ref, f32[60,56,128]{2,1,0:T(8,128)S(1)} %get-tuple-element.15.factor_ref, bf16[120,1008]{1,0:T(8,128)(2,1)S(1)} %get-tuple-element.13.after_ref.upper_ref, ...), custom_call_target="tpu_custom_call" | custom-call | flops 2000000000 | bytes 1000000 | tf_op jit(solution)/shard_map/main/pallas_call | solution.py:503
  16.8 0.0 collective-permute-done.3.from_core_ref
  16.8 0.0 collective-permute-done.4.from_cross_ref
  16.8 1.9 %rim.1 = (f32[32,384]{1,0:T(8,128)}, f32[32,384]{1,0:T(8,128)}) custom-call(f32[21,128]{1,0:T(8,128)S(1)} %get-tuple-element.14.taps_ref, f32[60,56,128]{2,1,0:T(8,128)S(1)} %get-tuple-element.15.factor_ref, bf16[120,1008]{1,0:T(8,128)(2,1)S(1)} %get-tuple-element.13.after_ref.upper_ref, bf16[160,1008]{1,0:T(8,128)(2,1)S(1)} %get-tuple-element.16.lower_ref, ...), custom_call_target="tpu_custom_call" | custom-call | tf_op jit(solution)/shard_map/rim/pallas_call | solution.py:517
Async XLA Ops:
  0.6 11.9 %collective-permute-start = (bf16[4,32,384]{2,1,0:T(8,128)(2,1)}, bf16[4,32,384]{2,1,0:T(8,128)(2,1)S(1)}, u32[]{:S(2)}, u32[]{:S(2)}) collective-permute-start(bf16[4,32,384]{2,1,0:T(8,128)(2,1)} %refs_3_.1), channel_id=1, source_target_pairs={{0,3},{1,2},{2,1},{3,0},{4,7},{5,6},{6,5},{7,4},{8,11},{9,10},{10,... | collective-permute-start | bytes 294920 | tf_op jit(solution)/shard_map/ppermute | solution.py:469
  5.7 6.8 %collective-permute-start.2 = (bf16[4,32,384]{2,1,0:T(8,128)(2,1)}, bf16[4,32,384]{2,1,0:T(8,128)(2,1)S(1)}, u32[]{:S(2)}, u32[]{:S(2)}) collective-permute-start(bf16[4,32,384]{2,1,0:T(8,128)(2,1)} %refs_3_.1), channel_id=1, source_target_pairs={{0,1},{1,0},{2,3},{3,2},{4,5},{5,4},{6,7},{7,6},{8,9},{9,8},{10,11... | collective-permute-start | bytes 294920 | tf_op jit(solution)/shard_map/ppermute | solution.py:469
  6.7 5.9 %copy-start = (bf16[4,32,384]{2,1,0:T(8,128)(2,1)S(1)}, bf16[4,32,384]{2,1,0:T(8,128)(2,1)}, u32[]{:S(2)}) copy-start(bf16[4,32,384]{2,1,0:T(8,128)(2,1)} %refs_3_.1) | copy-start | bytes 294916
  6.7 5.8 %collective-permute-start.1 = (bf16[3,32,384]{2,1,0:T(8,128)(2,1)S(1)}, bf16[3,32,384]{2,1,0:T(8,128)(2,1)S(1)}, u32[]{:S(2)}, u32[]{:S(2)}) collective-permute-start(bf16[3,32,384]{2,1,0:T(8,128)(2,1)S(1)} %slice.3), channel_id=1, source_target_pairs={{0,2},{1,3},{2,0},{3,1},{4,6},{5,7},{6,4},{7,5},{8,10},{9,11},{10,... | collective-permute-start | bytes 221192 | tf_op jit(solution)/shard_map/ppermute | solution.py:469
  7.4 0.8 %copy-start.1 = (bf16[5,21,21]{2,1,0:T(8,128)(2,1)S(1)}, bf16[5,21,21]{2,1,0:T(8,128)(2,1)}, u32[]{:S(2)}) copy-start(bf16[5,21,21]{2,1,0:T(8,128)(2,1)} %basis_ref.1) | copy-start | bytes 13234
  8.1 0.7 %copy-start.2 = (f32[4,5,6]{2,0,1:T(4,128)S(1)}, f32[4,5,6]{2,0,1:T(4,128)}, u32[]{:S(2)}) copy-start(f32[4,5,6]{2,0,1:T(4,128)} %param.9) | copy-start | bytes 1444
  8.1 0.7 %copy-start.3 = (f32[4]{0:T(128)S(1)}, f32[4]{0:T(128)}, u32[]{:S(2)}) copy-start(f32[4]{0:T(128)} %weight_ref.1) | copy-start | bytes 52
  8.1 0.7 %copy-start.4 = (s32[4]{0:T(128)S(1)}, s32[4]{0:T(128)}, u32[]{:S(2)}) copy-start(s32[4]{0:T(128)} %start_ref.1) | copy-start | bytes 52
  8.1 0.7 %copy-start.5 = (s32[4]{0:T(128)S(1)}, s32[4]{0:T(128)}, u32[]{:S(2)}) copy-start(s32[4]{0:T(128)} %count_ref.1) | copy-start | bytes 52
  8.2 0.7 %copy-start.6 = (f32[21]{0:T(128)S(1)}, f32[21]{0:T(128)}, u32[]{:S(2)}) copy-start(f32[21]{0:T(128)} %taps_ref.1) | copy-start | bytes 256
  12.8 4.0 %collective-permute-start.3 = (bf16[80,128]{1,0:T(8,128)(2,1)S(1)}, bf16[80,128]{1,0:T(8,128)(2,1)S(1)}, u32[]{:S(2)}, u32[]{:S(2)}) collective-permute-start(bf16[80,128]{1,0:T(8,128)(2,1)S(1)} %get-tuple-element.22.to_core_ref), channel_id=1, source_target_pairs={{0,4},{4,0},{8,12},{12,8},{16,20},{20,16},{24,28},{28,24},{1,5},{5... | collective-permute-start | bytes 61448 | tf_op jit(solution)/shard_map/ppermute | solution.py:500
  12.9 3.9 %collective-permute-start.4 = (bf16[80,128]{1,0:T(8,128)(2,1)S(1)}, bf16[80,128]{1,0:T(8,128)(2,1)S(1)}, u32[]{:S(2)}, u32[]{:S(2)}) collective-permute-start(bf16[80,128]{1,0:T(8,128)(2,1)S(1)} %get-tuple-element.23.to_cross_ref), channel_id=1, source_target_pairs={{0,1},{4,8},{8,4},{12,16},{16,12},{20,24},{24,20},{28,29},{1,0},{5... | collective-permute-start | bytes 61448 | tf_op jit(solution)/shard_map/ppermute | solution.py:501

commit v9 on v7

--- a/solution.py
+++ b/solution.py
@@ -408,21 +408,19 @@
         ),
     )
     tall[...] = edge
-    coadd_ref[...] = inner_ref[half : half + tile_rows, :]
     edge_detection = filtered(taps_ref, side, tall, tile_rows)
     edge_coadd = tall[half : half + tile_rows, :]
-    detection_ref[...] = inner_detection_ref[...]
     lane = lane[:tile_rows]
-    for out_ref, values, reach in (
-        (coadd_ref, edge_coadd, half),
-        (detection_ref, edge_detection, rim),
+    for out_ref, inner, values, reach in (
+        (coadd_ref, inner_ref[half : half + tile_rows, :], edge_coadd, half),
+        (detection_ref, inner_detection_ref[...], edge_detection, rim),
     ):
         head = pltpu.roll(values, LANES - rim, 1)
         tail = pltpu.roll(values, rim, 1)
-        out_ref[:, :LANES] = jnp.where(lane < reach, head, out_ref[:, :LANES])
-        out_ref[:, tile_cols - LANES :] = jnp.where(
-            lane >= LANES - reach, tail, out_ref[:, tile_cols - LANES :]
-        )
+        last = tile_cols - LANES
+        out_ref[:, :LANES] = jnp.where(lane < reach, head, inner[:, :LANES])
+        out_ref[:, LANES:last] = inner[:, LANES:last]
+        out_ref[:, last:] = jnp.where(lane >= LANES - reach, tail, inner[:, last:])
 
 
 def on_device(

time: 19 us -> 19 us (level)
  no operation moved by 1% of the time
where the time goes in v9:
time: 19 us; the launch traced here: 18.7 us
  starting transfers between devices  7.39 us (39%)
  Pallas kernels  6.2 us (33%)
  waiting for transfers between devices  2.66 us (14%)
  local copies, waits for them, and re-layouts  1.73 us (9%)
  between operations  0.74 us (4%)
    ppermute x3, starting transfers between devices, on_device(): tiles[index] = lax.ppermute(exposures[sent[index]:], 'narrow', pairs)  5.79 us
    ppermute x3, waiting for transfers between devices, on_device(): tiles[index] = lax.ppermute(exposures[sent[index]:], 'narrow', pairs)  2.66 us
    pallas_call x1, Pallas kernels, on_device(): pl.pallas_call(functools.partial(main_kernel, wide_peers, side, tile_rows...  2.43 us
    pallas_call x1, Pallas kernels, on_device(): pl.pallas_call(functools.partial(rim_kernel, wide_peers, side, members),...  1.88 us
    ppermute x1, starting transfers between devices, on_device(): from_cross = lax.ppermute(to_cross, ('wide', 'narrow'), cross_pairs)  1.53 us
    pallas_call x1, Pallas kernels, prepared(): pl.pallas_call(functools.partial(factors_kernel, tile_rows, band_rows, ha...  1 us
    slice x1, local copies, waits for them, and re-layouts, on_device(): tiles[index] = lax.ppermute(exposures[sent[index]:], 'narrow', pairs)  0.96 us
    unnamed x14, local copies, waits for them, and re-layouts  0.78 us
  transfers between devices with their start and end apart: 5, of which 1 were waited for; matrix products, arithmetic and copies ran while one was open for 5% of the time, Pallas kernels for 22%

profile of v9, /device:TPU:0, one launch (start us, length us, event | category | flops | bytes accessed | tf_op | source)
XLA Modules:
  0.0 18.7 jit_solution(7509875697007762309)
XLA Ops:
  0.6 5.1 %collective-permute-start = (bf16[4,32,384]{2,1,0:T(8,128)(2,1)}, bf16[4,32,384]{2,1,0:T(8,128)(2,1)S(1)}, u32[]{:S(2)}, u32[]{:S(2)}) collective-permute-start(bf16[4,32,384]{2,1,0:T(8,128)(2,1)} %refs_3_.1), channel_id=1, source_target_pairs={{0,3},{1,2},{2,1},{3,0},{4,7},{5,6},{6,5},{7,4},{8,11},{9,10},{10,... | collective-permute-start | bytes 294920 | tf_op jit(solution)/shard_map/ppermute | solution.py:443
  5.7 0.0 collective-permute-start.2
  5.7 1.0 %slice.3 = bf16[3,32,384]{2,1,0:T(8,128)(2,1)S(1)} slice(bf16[4,32,384]{2,1,0:T(8,128)(2,1)} %refs_3_.1), slice={[1:4], [0:32], [0:384]} | slice | bytes 147456 | tf_op jit(solution)/shard_map/slice | solution.py:443
  6.7 0.0 copy-start
  6.7 0.7 %collective-permute-start.1 = (bf16[3,32,384]{2,1,0:T(8,128)(2,1)S(1)}, bf16[3,32,384]{2,1,0:T(8,128)(2,1)S(1)}, u32[]{:S(2)}, u32[]{:S(2)}) collective-permute-start(bf16[3,32,384]{2,1,0:T(8,128)(2,1)S(1)} %slice.3), channel_id=1, source_target_pairs={{0,2},{1,3},{2,0},{3,1},{4,6},{5,7},{6,4},{7,5},{8,10},{9,11},{10,... | collective-permute-start | bytes 221192 | tf_op jit(solution)/shard_map/ppermute | solution.py:443
  7.4 0.0 copy-start.1
  7.4 0.8 %copy-done.1 = bf16[5,21,21]{2,1,0:T(8,128)(2,1)S(1)} copy-done((bf16[5,21,21]{2,1,0:T(8,128)(2,1)S(1)}, bf16[5,21,21]{2,1,0:T(8,128)(2,1)}, u32[]{:S(2)}) %copy-start.1) | copy-done | bytes 4434
  8.1 0.0 copy-start.2
  8.1 0.0 copy-start.3
  8.1 0.0 copy-start.4
  8.1 0.0 copy-start.5
  8.2 0.0 copy-start.6
  8.2 0.7 %bands.1 = (bf16[120,1008]{1,0:T(8,128)(2,1)S(1)}, bf16[160,1008]{1,0:T(8,128)(2,1)S(1)}) custom-call(bf16[5,21,21]{2,1,0:T(8,128)(2,1)S(1)} %copy-done.1), custom_call_target="tpu_custom_call" | custom-call | flops 1000000000 | bytes 1000000 | tf_op jit(solution)/shard_map/bands/pallas_call | solution.py:133
  8.8 0.0 copy-done.2
  8.9 0.0 copy-done.3
  8.9 0.0 copy-done.4
  8.9 0.0 copy-done.5
  8.9 0.0 copy-done.6
  8.9 1.0 %factors.1 = (f32[60,56,128]{2,1,0:T(8,128)S(1)}, f32[21,128]{1,0:T(8,128)S(1)}, s32[8,16,128]{2,1,0:T(8,128)S(1)}) custom-call(f32[5,4,6]{2,1,0:T(4,128)S(1)} %bitcast.1, f32[4]{0:T(128)S(1)} %copy-done.3, s32[4]{0:T(128)S(1)} %copy-done.4, s32[4]{0:T(128)S(1)} %copy-done.5, f32[21]{0:T(128)S(1)} %copy-done.6, ...), custom_call_target="tpu_custom_call" | custom-call | flops 100000000 | bytes 1000000 | tf_op jit(solution)/shard_map/factors/pallas_call | solution.py:146
  9.9 2.7 %collective-permute-done.1.refs_1_ = bf16[3,32,384]{2,1,0:T(8,128)(2,1)S(1)} collective-permute-done((bf16[3,32,384]{2,1,0:T(8,128)(2,1)S(1)}, bf16[3,32,384]{2,1,0:T(8,128)(2,1)S(1)}, u32[]{:S(2)}, u32[]{:S(2)}) %collective-permute-start.1) | collective-permute-done | bytes 73760 | tf_op jit(solution)/shard_map/ppermute | solution.py:443
  12.6 0.0 collective-permute-done.refs_0_
  12.6 0.0 collective-permute-done.2.refs_2_
  12.6 0.0 copy-done
  12.6 0.2 %place.1 = (bf16[4,80,384]{2,1,0:T(8,128)(2,1)S(1)}, bf16[80,128]{1,0:T(8,128)(2,1)S(1)}, bf16[80,128]{1,0:T(8,128)(2,1)S(1)}) custom-call(s32[8,16,128]{2,1,0:T(8,128)S(1)} %get-tuple-element.16.span_ref, bf16[4,32,384]{2,1,0:T(8,128)(2,1)S(1)} %collective-permute-done.refs_0_, bf16[3,32,384]{2,1,0:T(8,128)(2,1)S(1)} %collective-permute-done.1.refs_1_, ...), custom_call_target="tpu_custom_call" | custom-call | tf_op jit(solution)/shard_map/place/pallas_call | solution.py:456
  12.8 0.1 collective-permute-start.3
  12.9 1.5 %collective-permute-start.4 = (bf16[80,128]{1,0:T(8,128)(2,1)S(1)}, bf16[80,128]{1,0:T(8,128)(2,1)S(1)}, u32[]{:S(2)}, u32[]{:S(2)}) collective-permute-start(bf16[80,128]{1,0:T(8,128)(2,1)S(1)} %get-tuple-element.21.to_cross_ref), channel_id=1, source_target_pairs={{0,1},{4,8},{8,4},{12,16},{16,12},{20,24},{24,20},{28,29},{1,0},{5... | collective-permute-start | bytes 61448 | tf_op jit(solution)/shard_map/ppermute | solution.py:475
  14.4 2.4 %main.1 = (f32[56,384]{1,0:T(8,128)S(1)}, f32[32,384]{1,0:T(8,128)S(1)}) custom-call(f32[21,128]{1,0:T(8,128)S(1)} %get-tuple-element.13.taps_ref, f32[60,56,128]{2,1,0:T(8,128)S(1)} %get-tuple-element.14.factor_ref, bf16[120,1008]{1,0:T(8,128)(2,1)S(1)} %get-tuple-element.12.after_ref.upper_ref, bf16[160,1008]{1,0:T(8,128)(2,1)S(1)} %get-tuple-element.15.lower_ref, ...), custom_call_target="tpu_custom_call" | custom-call | flops 2000000000 | bytes 1000000 | tf_op jit(solution)/shard_map/main/pallas_call | solution.py:477
  16.8 0.0 collective-permute-done.3.from_core_ref
  16.8 0.0 collective-permute-done.4.from_cross_ref
  16.8 1.9 %rim.1 = (f32[32,384]{1,0:T(8,128)}, f32[32,384]{1,0:T(8,128)}) custom-call(f32[21,128]{1,0:T(8,128)S(1)} %get-tuple-element.13.taps_ref, f32[60,56,128]{2,1,0:T(8,128)S(1)} %get-tuple-element.14.factor_ref, bf16[120,1008]{1,0:T(8,128)(2,1)S(1)} %get-tuple-element.12.after_ref.upper_ref, bf16[160,1008]{1,0:T(8,128)(2,1)S(1)} %get-tuple-element.15.lower_ref, ...), custom_call_target="tpu_custom_call" | custom-call | tf_op jit(solution)/shard_map/rim/pallas_call | solution.py:491
Async XLA Ops:
  0.6 11.9 %collective-permute-start = (bf16[4,32,384]{2,1,0:T(8,128)(2,1)}, bf16[4,32,384]{2,1,0:T(8,128)(2,1)S(1)}, u32[]{:S(2)}, u32[]{:S(2)}) collective-permute-start(bf16[4,32,384]{2,1,0:T(8,128)(2,1)} %refs_3_.1), channel_id=1, source_target_pairs={{0,3},{1,2},{2,1},{3,0},{4,7},{5,6},{6,5},{7,4},{8,11},{9,10},{10,... | collective-permute-start | bytes 294920 | tf_op jit(solution)/shard_map/ppermute | solution.py:443
  5.7 6.8 %collective-permute-start.2 = (bf16[4,32,384]{2,1,0:T(8,128)(2,1)}, bf16[4,32,384]{2,1,0:T(8,128)(2,1)S(1)}, u32[]{:S(2)}, u32[]{:S(2)}) collective-permute-start(bf16[4,32,384]{2,1,0:T(8,128)(2,1)} %refs_3_.1), channel_id=1, source_target_pairs={{0,1},{1,0},{2,3},{3,2},{4,5},{5,4},{6,7},{7,6},{8,9},{9,8},{10,11... | collective-permute-start | bytes 294920 | tf_op jit(solution)/shard_map/ppermute | solution.py:443
  6.7 5.9 %copy-start = (bf16[4,32,384]{2,1,0:T(8,128)(2,1)S(1)}, bf16[4,32,384]{2,1,0:T(8,128)(2,1)}, u32[]{:S(2)}) copy-start(bf16[4,32,384]{2,1,0:T(8,128)(2,1)} %refs_3_.1) | copy-start | bytes 294916
  6.7 5.8 %collective-permute-start.1 = (bf16[3,32,384]{2,1,0:T(8,128)(2,1)S(1)}, bf16[3,32,384]{2,1,0:T(8,128)(2,1)S(1)}, u32[]{:S(2)}, u32[]{:S(2)}) collective-permute-start(bf16[3,32,384]{2,1,0:T(8,128)(2,1)S(1)} %slice.3), channel_id=1, source_target_pairs={{0,2},{1,3},{2,0},{3,1},{4,6},{5,7},{6,4},{7,5},{8,10},{9,11},{10,... | collective-permute-start | bytes 221192 | tf_op jit(solution)/shard_map/ppermute | solution.py:443
  7.4 0.8 %copy-start.1 = (bf16[5,21,21]{2,1,0:T(8,128)(2,1)S(1)}, bf16[5,21,21]{2,1,0:T(8,128)(2,1)}, u32[]{:S(2)}) copy-start(bf16[5,21,21]{2,1,0:T(8,128)(2,1)} %basis_ref.1) | copy-start | bytes 13234
  8.1 0.7 %copy-start.2 = (f32[4,5,6]{2,0,1:T(4,128)S(1)}, f32[4,5,6]{2,0,1:T(4,128)}, u32[]{:S(2)}) copy-start(f32[4,5,6]{2,0,1:T(4,128)} %param.9) | copy-start | bytes 1444
  8.1 0.7 %copy-start.3 = (f32[4]{0:T(128)S(1)}, f32[4]{0:T(128)}, u32[]{:S(2)}) copy-start(f32[4]{0:T(128)} %weight_ref.1) | copy-start | bytes 52
  8.1 0.7 %copy-start.4 = (s32[4]{0:T(128)S(1)}, s32[4]{0:T(128)}, u32[]{:S(2)}) copy-start(s32[4]{0:T(128)} %start_ref.1) | copy-start | bytes 52
  8.1 0.7 %copy-start.5 = (s32[4]{0:T(128)S(1)}, s32[4]{0:T(128)}, u32[]{:S(2)}) copy-start(s32[4]{0:T(128)} %count_ref.1) | copy-start | bytes 52
  8.2 0.7 %copy-start.6 = (f32[21]{0:T(128)S(1)}, f32[21]{0:T(128)}, u32[]{:S(2)}) copy-start(f32[21]{0:T(128)} %taps_ref.1) | copy-start | bytes 256
  12.8 4.0 %collective-permute-start.3 = (bf16[80,128]{1,0:T(8,128)(2,1)S(1)}, bf16[80,128]{1,0:T(8,128)(2,1)S(1)}, u32[]{:S(2)}, u32[]{:S(2)}) collective-permute-start(bf16[80,128]{1,0:T(8,128)(2,1)S(1)} %get-tuple-element.20.to_core_ref), channel_id=1, source_target_pairs={{0,4},{4,0},{8,12},{12,8},{16,20},{20,16},{24,28},{28,24},{1,5},{5... | collective-permute-start | bytes 61448 | tf_op jit(solution)/shard_map/ppermute | solution.py:474
  12.9 4.0 %collective-permute-start.4 = (bf16[80,128]{1,0:T(8,128)(2,1)S(1)}, bf16[80,128]{1,0:T(8,128)(2,1)S(1)}, u32[]{:S(2)}, u32[]{:S(2)}) collective-permute-start(bf16[80,128]{1,0:T(8,128)(2,1)S(1)} %get-tuple-element.21.to_cross_ref), channel_id=1, source_target_pairs={{0,1},{4,8},{8,4},{12,16},{16,12},{20,24},{24,20},{28,29},{1,0},{5... | collective-permute-start | bytes 61448 | tf_op jit(solution)/shard_map/ppermute | solution.py:475

commit v10 on v8

--- a/solution.py
+++ b/solution.py
@@ -432,21 +432,19 @@
         ),
     )
     tall[...] = edge
-    coadd_ref[...] = inner_ref[half : half + tile_rows, :]
     edge_detection = filtered(taps_ref, None, side, tall, tile_rows)
     edge_coadd = tall[half : half + tile_rows, :]
-    detection_ref[...] = inner_detection_ref[...]
     lane = lane[:tile_rows]
-    for out_ref, values, reach in (
-        (coadd_ref, edge_coadd, half),
-        (detection_ref, edge_detection, rim),
+    for out_ref, inner, values, reach in (
+        (coadd_ref, inner_ref[half : half + tile_rows, :], edge_coadd, half),
+        (detection_ref, inner_detection_ref[...], edge_detection, rim),
     ):
         head = pltpu.roll(values, LANES - rim, 1)
         tail = pltpu.roll(values, rim, 1)
-        out_ref[:, :LANES] = jnp.where(lane < reach, head, out_ref[:, :LANES])
-        out_ref[:, tile_cols - LANES :] = jnp.where(
-            lane >= LANES - reach, tail, out_ref[:, tile_cols - LANES :]
-        )
+        last = tile_cols - LANES
+        out_ref[:, :LANES] = jnp.where(lane < reach, head, inner[:, :LANES])
+        out_ref[:, LANES:last] = inner[:, LANES:last]
+        out_ref[:, last:] = jnp.where(lane >= LANES - reach, tail, inner[:, last:])
 
 
 def on_device(

time: 18.9 us -> 18.9 us (level)
  no operation moved by 1% of the time
where the time goes in v10:
time: 18.9 us; the launch traced here: 18.7 us
  starting transfers between devices  7.39 us (39%)
  Pallas kernels  6.26 us (33%)
  waiting for transfers between devices  2.54 us (13%)
  local copies, waits for them, and re-layouts  1.73 us (9%)
  between operations  0.74 us (4%)
    ppermute x3, starting transfers between devices, on_device(): tiles[index] = lax.ppermute(exposures[sent[index]:], 'narrow', pairs)  5.79 us
    ppermute x3, waiting for transfers between devices, on_device(): tiles[index] = lax.ppermute(exposures[sent[index]:], 'narrow', pairs)  2.54 us
    pallas_call x1, Pallas kernels, on_device(): pl.pallas_call(functools.partial(main_kernel, wide_peers, side, tile_rows...  2.36 us
    pallas_call x1, Pallas kernels, on_device(): pl.pallas_call(functools.partial(rim_kernel, wide_peers, side, members),...  1.87 us
    ppermute x1, starting transfers between devices, on_device(): from_cross = lax.ppermute(to_cross, ('wide', 'narrow'), cross_pairs)  1.53 us
    pallas_call x1, Pallas kernels, prepared(): pl.pallas_call(functools.partial(factors_kernel, tile_rows, band_rows, ha...  1.12 us
    slice x1, local copies, waits for them, and re-layouts, on_device(): tiles[index] = lax.ppermute(exposures[sent[index]:], 'narrow', pairs)  0.96 us
    unnamed x14, local copies, waits for them, and re-layouts  0.78 us
  transfers between devices with their start and end apart: 5, of which 1 were waited for; matrix products, arithmetic and copies ran while one was open for 5% of the time, Pallas kernels for 22%

profile of v10, /device:TPU:0, one launch (start us, length us, event | category | flops | bytes accessed | tf_op | source)
XLA Modules:
  0.0 18.7 jit_solution(5102612909799598478)
XLA Ops:
  0.6 5.1 %collective-permute-start = (bf16[4,32,384]{2,1,0:T(8,128)(2,1)}, bf16[4,32,384]{2,1,0:T(8,128)(2,1)S(1)}, u32[]{:S(2)}, u32[]{:S(2)}) collective-permute-start(bf16[4,32,384]{2,1,0:T(8,128)(2,1)} %refs_3_.1), channel_id=1, source_target_pairs={{0,3},{1,2},{2,1},{3,0},{4,7},{5,6},{6,5},{7,4},{8,11},{9,10},{10,... | collective-permute-start | bytes 294920 | tf_op jit(solution)/shard_map/ppermute | solution.py:467
  5.7 0.0 collective-permute-start.2
  5.7 1.0 %slice.3 = bf16[3,32,384]{2,1,0:T(8,128)(2,1)S(1)} slice(bf16[4,32,384]{2,1,0:T(8,128)(2,1)} %refs_3_.1), slice={[1:4], [0:32], [0:384]} | slice | bytes 147456 | tf_op jit(solution)/shard_map/slice | solution.py:467
  6.7 0.0 copy-start
  6.7 0.7 %collective-permute-start.1 = (bf16[3,32,384]{2,1,0:T(8,128)(2,1)S(1)}, bf16[3,32,384]{2,1,0:T(8,128)(2,1)S(1)}, u32[]{:S(2)}, u32[]{:S(2)}) collective-permute-start(bf16[3,32,384]{2,1,0:T(8,128)(2,1)S(1)} %slice.3), channel_id=1, source_target_pairs={{0,2},{1,3},{2,0},{3,1},{4,6},{5,7},{6,4},{7,5},{8,10},{9,11},{10,... | collective-permute-start | bytes 221192 | tf_op jit(solution)/shard_map/ppermute | solution.py:467
  7.4 0.0 copy-start.1
  7.4 0.8 %copy-done.1 = bf16[5,21,21]{2,1,0:T(8,128)(2,1)S(1)} copy-done((bf16[5,21,21]{2,1,0:T(8,128)(2,1)S(1)}, bf16[5,21,21]{2,1,0:T(8,128)(2,1)}, u32[]{:S(2)}) %copy-start.1) | copy-done | bytes 4434
  8.1 0.0 copy-start.2
  8.1 0.0 copy-start.3
  8.1 0.0 copy-start.4
  8.1 0.0 copy-start.5
  8.2 0.0 copy-start.6
  8.2 0.7 %bands.1 = (bf16[120,1008]{1,0:T(8,128)(2,1)S(1)}, bf16[160,1008]{1,0:T(8,128)(2,1)S(1)}) custom-call(bf16[5,21,21]{2,1,0:T(8,128)(2,1)S(1)} %copy-done.1), custom_call_target="tpu_custom_call" | custom-call | flops 1000000000 | bytes 1000000 | tf_op jit(solution)/shard_map/bands/pallas_call | solution.py:144
  8.8 0.0 copy-done.2
  8.9 0.0 copy-done.3
  8.9 0.0 copy-done.4
  8.9 0.0 copy-done.5
  8.9 0.0 copy-done.6
  8.9 1.1 %factors.1 = (f32[60,56,128]{2,1,0:T(8,128)S(1)}, f32[21,128]{1,0:T(8,128)S(1)}, s32[8,16,128]{2,1,0:T(8,128)S(1)}, bf16[64,128]{1,0:T(8,128)(2,1)S(1)}) custom-call(f32[5,4,6]{2,1,0:T(4,128)S(1)} %bitcast.1, f32[4]{0:T(128)S(1)} %copy-done.3, s32[4]{0:T(128)S(1)} %copy-done.4, s32[4]{0:T(128)S(1)} %copy-done.5, f32[21]{0:T(128)S(1)} %copy-done.6, ...), custom_call_target="tpu_custom_call" | custom-call | flops 100000000 | bytes 1000000 | tf_op jit(solution)/shard_map/factors/pallas_call | solution.py:157
  10.0 2.5 %collective-permute-done.1.refs_1_ = bf16[3,32,384]{2,1,0:T(8,128)(2,1)S(1)} collective-permute-done((bf16[3,32,384]{2,1,0:T(8,128)(2,1)S(1)}, bf16[3,32,384]{2,1,0:T(8,128)(2,1)S(1)}, u32[]{:S(2)}, u32[]{:S(2)}) %collective-permute-start.1) | collective-permute-done | bytes 73760 | tf_op jit(solution)/shard_map/ppermute | solution.py:467
  12.6 0.0 collective-permute-done.refs_0_
  12.6 0.0 collective-permute-done.2.refs_2_
  12.6 0.0 copy-done
  12.6 0.2 %place.1 = (bf16[4,80,384]{2,1,0:T(8,128)(2,1)S(1)}, bf16[80,128]{1,0:T(8,128)(2,1)S(1)}, bf16[80,128]{1,0:T(8,128)(2,1)S(1)}) custom-call(s32[8,16,128]{2,1,0:T(8,128)S(1)} %get-tuple-element.18.span_ref, bf16[4,32,384]{2,1,0:T(8,128)(2,1)S(1)} %collective-permute-done.refs_0_, bf16[3,32,384]{2,1,0:T(8,128)(2,1)S(1)} %collective-permute-done.1.refs_1_, ...), custom_call_target="tpu_custom_call" | custom-call | tf_op jit(solution)/shard_map/place/pallas_call | solution.py:480
  12.8 0.1 collective-permute-start.3
  12.9 1.5 %collective-permute-start.4 = (bf16[80,128]{1,0:T(8,128)(2,1)S(1)}, bf16[80,128]{1,0:T(8,128)(2,1)S(1)}, u32[]{:S(2)}, u32[]{:S(2)}) collective-permute-start(bf16[80,128]{1,0:T(8,128)(2,1)S(1)} %get-tuple-element.23.to_cross_ref), channel_id=1, source_target_pairs={{0,1},{4,8},{8,4},{12,16},{16,12},{20,24},{24,20},{28,29},{1,0},{5... | collective-permute-start | bytes 61448 | tf_op jit(solution)/shard_map/ppermute | solution.py:499
  14.4 2.4 %main.1 = (f32[56,384]{1,0:T(8,128)S(1)}, f32[32,384]{1,0:T(8,128)S(1)}) custom-call(f32[21,128]{1,0:T(8,128)S(1)} %get-tuple-element.14.taps_ref, bf16[64,128]{1,0:T(8,128)(2,1)S(1)} %get-tuple-element.17.rows_ref, f32[60,56,128]{2,1,0:T(8,128)S(1)} %get-tuple-element.15.factor_ref, bf16[120,1008]{1,0:T(8,128)(2,1)S(1)} %get-tuple-element.13.after_ref.upper_ref, ...), custom_call_target="tpu_custom_call" | custom-call | flops 2000000000 | bytes 1000000 | tf_op jit(solution)/shard_map/main/pallas_call | solution.py:501
  16.8 0.0 collective-permute-done.3.from_core_ref
  16.8 0.0 collective-permute-done.4.from_cross_ref
  16.8 1.9 %rim.1 = (f32[32,384]{1,0:T(8,128)}, f32[32,384]{1,0:T(8,128)}) custom-call(f32[21,128]{1,0:T(8,128)S(1)} %get-tuple-element.14.taps_ref, f32[60,56,128]{2,1,0:T(8,128)S(1)} %get-tuple-element.15.factor_ref, bf16[120,1008]{1,0:T(8,128)(2,1)S(1)} %get-tuple-element.13.after_ref.upper_ref, bf16[160,1008]{1,0:T(8,128)(2,1)S(1)} %get-tuple-element.16.lower_ref, ...), custom_call_target="tpu_custom_call" | custom-call | tf_op jit(solution)/shard_map/rim/pallas_call | solution.py:515
Async XLA Ops:
  0.6 11.9 %collective-permute-start = (bf16[4,32,384]{2,1,0:T(8,128)(2,1)}, bf16[4,32,384]{2,1,0:T(8,128)(2,1)S(1)}, u32[]{:S(2)}, u32[]{:S(2)}) collective-permute-start(bf16[4,32,384]{2,1,0:T(8,128)(2,1)} %refs_3_.1), channel_id=1, source_target_pairs={{0,3},{1,2},{2,1},{3,0},{4,7},{5,6},{6,5},{7,4},{8,11},{9,10},{10,... | collective-permute-start | bytes 294920 | tf_op jit(solution)/shard_map/ppermute | solution.py:467
  5.7 6.8 %collective-permute-start.2 = (bf16[4,32,384]{2,1,0:T(8,128)(2,1)}, bf16[4,32,384]{2,1,0:T(8,128)(2,1)S(1)}, u32[]{:S(2)}, u32[]{:S(2)}) collective-permute-start(bf16[4,32,384]{2,1,0:T(8,128)(2,1)} %refs_3_.1), channel_id=1, source_target_pairs={{0,1},{1,0},{2,3},{3,2},{4,5},{5,4},{6,7},{7,6},{8,9},{9,8},{10,11... | collective-permute-start | bytes 294920 | tf_op jit(solution)/shard_map/ppermute | solution.py:467
  6.7 5.9 %copy-start = (bf16[4,32,384]{2,1,0:T(8,128)(2,1)S(1)}, bf16[4,32,384]{2,1,0:T(8,128)(2,1)}, u32[]{:S(2)}) copy-start(bf16[4,32,384]{2,1,0:T(8,128)(2,1)} %refs_3_.1) | copy-start | bytes 294916
  6.7 5.8 %collective-permute-start.1 = (bf16[3,32,384]{2,1,0:T(8,128)(2,1)S(1)}, bf16[3,32,384]{2,1,0:T(8,128)(2,1)S(1)}, u32[]{:S(2)}, u32[]{:S(2)}) collective-permute-start(bf16[3,32,384]{2,1,0:T(8,128)(2,1)S(1)} %slice.3), channel_id=1, source_target_pairs={{0,2},{1,3},{2,0},{3,1},{4,6},{5,7},{6,4},{7,5},{8,10},{9,11},{10,... | collective-permute-start | bytes 221192 | tf_op jit(solution)/shard_map/ppermute | solution.py:467
  7.4 0.8 %copy-start.1 = (bf16[5,21,21]{2,1,0:T(8,128)(2,1)S(1)}, bf16[5,21,21]{2,1,0:T(8,128)(2,1)}, u32[]{:S(2)}) copy-start(bf16[5,21,21]{2,1,0:T(8,128)(2,1)} %basis_ref.1) | copy-start | bytes 13234
  8.1 0.7 %copy-start.2 = (f32[4,5,6]{2,0,1:T(4,128)S(1)}, f32[4,5,6]{2,0,1:T(4,128)}, u32[]{:S(2)}) copy-start(f32[4,5,6]{2,0,1:T(4,128)} %param.9) | copy-start | bytes 1444
  8.1 0.7 %copy-start.3 = (f32[4]{0:T(128)S(1)}, f32[4]{0:T(128)}, u32[]{:S(2)}) copy-start(f32[4]{0:T(128)} %weight_ref.1) | copy-start | bytes 52
  8.1 0.7 %copy-start.4 = (s32[4]{0:T(128)S(1)}, s32[4]{0:T(128)}, u32[]{:S(2)}) copy-start(s32[4]{0:T(128)} %start_ref.1) | copy-start | bytes 52
  8.1 0.7 %copy-start.5 = (s32[4]{0:T(128)S(1)}, s32[4]{0:T(128)}, u32[]{:S(2)}) copy-start(s32[4]{0:T(128)} %count_ref.1) | copy-start | bytes 52
  8.2 0.7 %copy-start.6 = (f32[21]{0:T(128)S(1)}, f32[21]{0:T(128)}, u32[]{:S(2)}) copy-start(f32[21]{0:T(128)} %taps_ref.1) | copy-start | bytes 256
  12.8 4.0 %collective-permute-start.3 = (bf16[80,128]{1,0:T(8,128)(2,1)S(1)}, bf16[80,128]{1,0:T(8,128)(2,1)S(1)}, u32[]{:S(2)}, u32[]{:S(2)}) collective-permute-start(bf16[80,128]{1,0:T(8,128)(2,1)S(1)} %get-tuple-element.22.to_core_ref), channel_id=1, source_target_pairs={{0,4},{4,0},{8,12},{12,8},{16,20},{20,16},{24,28},{28,24},{1,5},{5... | collective-permute-start | bytes 61448 | tf_op jit(solution)/shard_map/ppermute | solution.py:498
  12.9 3.9 %collective-permute-start.4 = (bf16[80,128]{1,0:T(8,128)(2,1)S(1)}, bf16[80,128]{1,0:T(8,128)(2,1)S(1)}, u32[]{:S(2)}, u32[]{:S(2)}) collective-permute-start(bf16[80,128]{1,0:T(8,128)(2,1)S(1)} %get-tuple-element.23.to_cross_ref), channel_id=1, source_target_pairs={{0,1},{4,8},{8,4},{12,16},{16,12},{20,24},{24,20},{28,29},{1,0},{5... | collective-permute-start | bytes 61448 | tf_op jit(solution)/shard_map/ppermute | solution.py:499
